TPU v7x, 32 devices: a whole 2x2x4 slice. The times are simulated.
32 devices in a mesh: section: 4 (over y, x), dp: 8 (over z, core).
Axes of the slice: x: 2, y: 2, z: 4, core: 2. Of those that a mesh axis runs over, the one named last changes fastest.
Arguments:
- tokens: bfloat16 [6400, 768], P(('dp', 'section')), may hold values from -6 to 6
- cotangent: bfloat16 [6400, 768], P(('dp', 'section')), may hold values from -6 to 6
- image_kind: int32 [16], P('dp'), may hold values from 0 to 2, as said below
- norm_one_gain: float32 [4, 768], P('section'), may hold values from 0.5 to 1.5
- norm_one_bias: float32 [4, 768], P('section'), may hold values from -1.8 to 1.8
- qkv_weight: bfloat16 [4, 768, 2304], P('section'), may hold values from -0.21875 to 0.21875
- qkv_bias: float32 [4, 2304], P('section'), may hold values from -1.8 to 1.8
- rotary_freq: float32 [4, 768], P('section'), may hold values from -1 to 1
- proj_weight: bfloat16 [4, 768, 768], P('section'), may hold values from -0.625 to 0.625
- proj_bias: float32 [4, 768], P('section'), may hold values from -1.8 to 1.8
- norm_two_gain: float32 [4, 768], P('section'), may hold values from 0.5 to 1.5
- norm_two_bias: float32 [4, 768], P('section'), may hold values from -1.8 to 1.8
- up_weight: bfloat16 [4, 768, 3072], P('section'), may hold values from -0.21875 to 0.21875
- up_bias: float32 [4, 3072], P('section'), may hold values from -1.8 to 1.8
- down_weight: bfloat16 [4, 3072, 768], P('section'), may hold values from -0.109375 to 0.109375
- down_bias: float32 [4, 768], P('section'), may hold values from -1.8 to 1.8
Outputs:
- block_out: bfloat16 [6400, 768], P(('dp', 'section'))
- grad_tokens: float32 [6400, 768], P(('dp', 'section'))
- grad_norm_one_gain: float32 [4, 768], P('section')
- grad_norm_one_bias: float32 [4, 768], P('section')
- grad_qkv_weight: float32 [4, 768, 2304], P('section')
- grad_qkv_bias: float32 [4, 2304], P('section')
- grad_rotary_freq: float32 [4, 768], P('section')
- grad_proj_weight: float32 [4, 768, 768], P('section')
- grad_proj_bias: float32 [4, 768], P('section')
- grad_norm_two_gain: float32 [4, 768], P('section')
- grad_norm_two_bias: float32 [4, 768], P('section')
- grad_up_weight: float32 [4, 768, 3072], P('section')
- grad_up_bias: float32 [4, 3072], P('section')
- grad_down_weight: float32 [4, 3072, 768], P('section')
- grad_down_bias: float32 [4, 768], P('section')
Inputs may be any that keep to these rules, and one draw needn't show every extreme that they name: `image_kind`: 0: one image of 20 x 20 patches; 1: one image of 16 x 16; 2: two images of 14 x 14. Values 0 and 2 occur in every draw.
All inputs are finite; a program needn't handle non-finite values.
Results may differ from a plain program's by a relative error of at most 0.039.
Values may be sent and summed in bfloat16 or wider, within the bound.
No kernel may reach another device: no remote copies, remote signals or barrier semaphores. Data moves between devices by JAX's collectives and lax.ppermute only.
A program may use at most 448 MiB of HBM per device.

v0:
```python
from functools import partial

import jax
import jax.numpy as jnp
from jax import lax
from jax.sharding import PartitionSpec as P

HEADS = 12
SIDE_LARGE = 20
SIDE_MID = 16
SIDE_SMALL = 14
MICRO = 2
BUFS = 1
ROWS = 400


EPSILON = 1e-06
MASKED = -1e30


def passed_along(value, axis, steps):
    count = lax.axis_size(axis)
    initial, last = (max(0, -steps), min(count, count - steps))
    return lax.ppermute(value, axis, [(source, source + steps) for source in range(initial, last)])


def as_sent(shard):

    def short(part):
        return part.astype(jnp.bfloat16) if part.dtype == jnp.float32 else part

    return jax.tree.map(short, shard)


def geometry(kind_list):
    row_index = jnp.arange(ROWS, dtype=jnp.int32)[None, :]
    kind_col = kind_list[:, None]
    side_cells = jnp.where(
        kind_col == 0, SIDE_LARGE, jnp.where(kind_col == 1, SIDE_MID, SIDE_SMALL)
    ).astype(jnp.int32)
    image_count = jnp.where(kind_col == 2, 2, 1).astype(jnp.int32)
    image_area = side_cells * side_cells
    image_index = row_index // image_area
    live_rows = image_index < image_count
    local_index = row_index - image_index * image_area
    patch_row = local_index // side_cells
    patch_col = local_index - patch_row * side_cells
    segment = jnp.where(live_rows, image_index, 3)
    patch_row = jnp.where(live_rows, patch_row, 0).astype(jnp.float32).reshape(-1)
    patch_col = jnp.where(live_rows, patch_col, 0).astype(jnp.float32).reshape(-1)
    return (patch_row, patch_col, segment, live_rows.astype(jnp.float32).reshape(-1))


def normalize(values):
    center = values - jnp.mean(values, axis=-1, keepdims=True)
    inverse = lax.rsqrt(jnp.mean(center * center, axis=-1, keepdims=True) + EPSILON)
    return (center * inverse, inverse)


def norm_back(grad_hat, normed, inverse):
    return inverse * (
        grad_hat
        - jnp.mean(grad_hat, axis=-1, keepdims=True)
        - normed * jnp.mean(grad_hat * normed, axis=-1, keepdims=True)
    )


def rotate(values, cosine, sine_part):
    half_dim = values.shape[-1] // 2
    first_half = values[..., :half_dim]
    second_half = values[..., half_dim:]
    return jnp.concatenate(
        [
            first_half * cosine - second_half * sine_part,
            first_half * sine_part + second_half * cosine,
        ],
        axis=-1,
    )


def unrotate(grads_in, cosine, sine_part):
    half_dim = grads_in.shape[-1] // 2
    first_half = grads_in[..., :half_dim]
    second_half = grads_in[..., half_dim:]
    return jnp.concatenate(
        [
            first_half * cosine + second_half * sine_part,
            second_half * cosine - first_half * sine_part,
        ],
        axis=-1,
    )


def turn_grad(grads_in, rotated):
    half_dim = grads_in.shape[-1] // 2
    return (
        grads_in[..., half_dim:] * rotated[..., :half_dim]
        - grads_in[..., :half_dim] * rotated[..., half_dim:]
    )


def layer_states(inputs_low, params, layout, kept_lse):
    (
        gain_one,
        bias_one,
        qkv_weight,
        qkv_bias,
        frequency,
        proj_weight,
        proj_bias,
        gain_two,
        bias_two,
        up_weight,
        up_bias,
        down_weight,
        down_bias,
    ) = params
    patch_row, patch_col, segment, live_rows = layout
    buffers = segment.shape[0]
    model_width = inputs_low.shape[-1]
    head_dim = model_width // HEADS
    hidden_in = inputs_low.astype(jnp.float32)
    normed_one, inverse_one = normalize(hidden_in)
    attn_in = (normed_one * gain_one + bias_one).astype(jnp.bfloat16)
    qkv_pre = jnp.dot(attn_in, qkv_weight, preferred_element_type=jnp.float32) + qkv_bias
    angles = (
        patch_row[:, None] * frequency[None, : model_width // 2]
        + patch_col[:, None] * frequency[None, model_width // 2 :]
    ).reshape(-1, HEADS, head_dim // 2)
    cosine = jnp.cos(angles)
    sine_part = jnp.sin(angles)
    rot_query = rotate(qkv_pre[:, :model_width].reshape(-1, HEADS, head_dim), cosine, sine_part)
    rot_key = rotate(
        qkv_pre[:, model_width : 2 * model_width].reshape(-1, HEADS, head_dim), cosine, sine_part
    )
    query_low = rot_query.astype(jnp.bfloat16).reshape(buffers, ROWS, HEADS, head_dim)
    key_low = rot_key.astype(jnp.bfloat16).reshape(buffers, ROWS, HEADS, head_dim)
    value_low = (
        qkv_pre[:, 2 * model_width :].astype(jnp.bfloat16).reshape(buffers, ROWS, HEADS, head_dim)
    )
    raw_scores = jnp.einsum(
        "bqhe,bkhe->bhqk", query_low, key_low, preferred_element_type=jnp.float32
    ) * head_dim ** (-0.5)
    same_image = segment[:, None, :, None] == segment[:, None, None, :]
    scores = jnp.where(same_image, raw_scores, MASKED)
    if kept_lse is None:
        peak = jnp.max(scores, axis=-1, keepdims=True)
        log_total = peak + jnp.log(jnp.sum(jnp.exp(scores - peak), axis=-1, keepdims=True))
    else:
        log_total = kept_lse
    attn_probs = jnp.exp(scores - log_total)
    probs_low = attn_probs.astype(jnp.bfloat16)
    attended = jnp.einsum(
        "bhqk,bkhe->bqhe", probs_low, value_low, preferred_element_type=jnp.float32
    )
    attended_low = attended.reshape(-1, model_width).astype(jnp.bfloat16)
    middle = (
        hidden_in
        + jnp.dot(attended_low, proj_weight, preferred_element_type=jnp.float32)
        + proj_bias
    )
    normed_two, inverse_two = normalize(middle)
    mlp_in = (normed_two * gain_two + bias_two).astype(jnp.bfloat16)
    up_pre = jnp.dot(mlp_in, up_weight, preferred_element_type=jnp.float32) + up_bias
    activated_low = jax.nn.gelu(up_pre, approximate=True).astype(jnp.bfloat16)
    output = (
        middle + jnp.dot(activated_low, down_weight, preferred_element_type=jnp.float32) + down_bias
    )
    return {
        "output": output,
        "log_total": log_total,
        "normed_one": normed_one,
        "inverse_one": inverse_one,
        "attn_in": attn_in,
        "cosine": cosine,
        "sine_part": sine_part,
        "rot_query": rot_query,
        "rot_key": rot_key,
        "query_low": query_low,
        "key_low": key_low,
        "value_low": value_low,
        "attn_probs": attn_probs,
        "probs_low": probs_low,
        "attended_low": attended_low,
        "normed_two": normed_two,
        "inverse_two": inverse_two,
        "mlp_in": mlp_in,
        "up_pre": up_pre,
        "activated_low": activated_low,
    }


def branch_back(states, grad_out_low, params):
    (
        gain_one,
        bias_one,
        qkv_weight,
        qkv_bias,
        frequency,
        proj_weight,
        proj_bias,
        gain_two,
        bias_two,
        up_weight,
        up_bias,
        down_weight,
        down_bias,
    ) = params
    grad_out = grad_out_low.astype(jnp.float32)
    grad_down_weight = jnp.einsum(
        "rf,rd->fd", states["activated_low"], grad_out_low, preferred_element_type=jnp.float32
    )
    grad_down_bias = jnp.sum(grad_out, axis=0)
    grad_act = jnp.einsum(
        "rd,fd->rf", grad_out_low, down_weight, preferred_element_type=jnp.float32
    )
    gelu_value, gelu_back = jax.vjp(partial(jax.nn.gelu, approximate=True), states["up_pre"])
    grad_up_low = gelu_back(grad_act)[0].astype(jnp.bfloat16)
    grad_up_weight = jnp.einsum(
        "rd,rf->df", states["mlp_in"], grad_up_low, preferred_element_type=jnp.float32
    )
    grad_up_bias = jnp.sum(grad_up_low.astype(jnp.float32), axis=0)
    grad_mlp_in = jnp.einsum(
        "rf,df->rd", grad_up_low, up_weight, preferred_element_type=jnp.float32
    )
    grad_gain_two = jnp.sum(grad_mlp_in * states["normed_two"], axis=0)
    grad_bias_two = jnp.sum(grad_mlp_in, axis=0)
    grad_middle = grad_out + norm_back(
        grad_mlp_in * gain_two, states["normed_two"], states["inverse_two"]
    )
    grad_middle_low = grad_middle.astype(jnp.bfloat16)
    grad_proj_weight = jnp.einsum(
        "rd,re->de", states["attended_low"], grad_middle_low, preferred_element_type=jnp.float32
    )
    grad_proj_bias = jnp.sum(grad_middle_low.astype(jnp.float32), axis=0)
    later_grads = (
        grad_proj_weight,
        grad_proj_bias,
        grad_gain_two,
        grad_bias_two,
        grad_up_weight,
        grad_up_bias,
        grad_down_weight,
        grad_down_bias,
    )
    return (grad_middle, grad_middle_low, later_grads)


def attention_back(states, grad_middle, grad_middle_low, params, layout):
    (
        gain_one,
        bias_one,
        qkv_weight,
        qkv_bias,
        frequency,
        proj_weight,
        proj_bias,
        gain_two,
        bias_two,
        up_weight,
        up_bias,
        down_weight,
        down_bias,
    ) = params
    patch_row, patch_col, segment, live_rows = layout
    model_width = grad_middle.shape[-1]
    head_dim = model_width // HEADS
    buffers = segment.shape[0]
    grad_att_low = jnp.einsum(
        "re,de->rd", grad_middle_low, proj_weight, preferred_element_type=jnp.float32
    )
    grad_att_low = grad_att_low.astype(jnp.bfloat16).reshape(buffers, ROWS, HEADS, head_dim)
    grad_value = jnp.einsum(
        "bhqk,bqhe->bkhe", states["probs_low"], grad_att_low, preferred_element_type=jnp.float32
    )
    grad_probs = jnp.einsum(
        "bqhe,bkhe->bhqk", grad_att_low, states["value_low"], preferred_element_type=jnp.float32
    )
    row_delta = jnp.sum(states["attn_probs"] * grad_probs, axis=-1, keepdims=True)
    grad_scores_low = (states["attn_probs"] * (grad_probs - row_delta)).astype(jnp.bfloat16)
    grad_query = jnp.einsum(
        "bhqk,bkhe->bqhe", grad_scores_low, states["key_low"], preferred_element_type=jnp.float32
    ) * head_dim ** (-0.5)
    grad_key = jnp.einsum(
        "bhqk,bqhe->bkhe", grad_scores_low, states["query_low"], preferred_element_type=jnp.float32
    ) * head_dim ** (-0.5)
    grad_query = grad_query.reshape(-1, HEADS, head_dim)
    grad_key = grad_key.reshape(-1, HEADS, head_dim)
    grad_angles = (
        turn_grad(grad_query, states["rot_query"]) + turn_grad(grad_key, states["rot_key"])
    ).reshape(-1, model_width // 2)
    grad_frequency = jnp.concatenate(
        [
            jnp.sum(patch_row[:, None] * grad_angles, axis=0),
            jnp.sum(patch_col[:, None] * grad_angles, axis=0),
        ],
        axis=0,
    )
    grad_qkv_low = jnp.concatenate(
        [
            unrotate(grad_query, states["cosine"], states["sine_part"]).reshape(-1, model_width),
            unrotate(grad_key, states["cosine"], states["sine_part"]).reshape(-1, model_width),
            grad_value.reshape(-1, model_width),
        ],
        axis=-1,
    ).astype(jnp.bfloat16)
    grad_qkv_weight = jnp.einsum(
        "rd,re->de", states["attn_in"], grad_qkv_low, preferred_element_type=jnp.float32
    )
    grad_qkv_bias = jnp.sum(grad_qkv_low.astype(jnp.float32), axis=0)
    grad_attn_in = jnp.einsum(
        "re,de->rd", grad_qkv_low, qkv_weight, preferred_element_type=jnp.float32
    )
    grad_gain_one = jnp.sum(grad_attn_in * states["normed_one"], axis=0)
    grad_bias_one = jnp.sum(grad_attn_in, axis=0)
    grad_input = grad_middle + norm_back(
        grad_attn_in * gain_one, states["normed_one"], states["inverse_one"]
    )
    early_grads = (grad_gain_one, grad_bias_one, grad_qkv_weight, grad_qkv_bias, grad_frequency)
    return (grad_input, early_grads)


def layer_back(inputs_low, grad_out_low, params, layout, kept_lse):
    states = layer_states(inputs_low, params, layout, kept_lse)
    grad_middle, grad_middle_low, later_grads = branch_back(states, grad_out_low, params)
    grad_input, early_grads = attention_back(states, grad_middle, grad_middle_low, params, layout)
    return (grad_input, early_grads + later_grads)


def per_device(
    tokens,
    cotangent,
    image_kind,
    norm_one_gain,
    norm_one_bias,
    qkv_weight,
    qkv_bias,
    rotary_freq,
    proj_weight,
    proj_bias,
    norm_two_gain,
    norm_two_bias,
    up_weight,
    up_bias,
    down_weight,
    down_bias,
):
    sections = lax.axis_size("section")
    section_index = lax.axis_index("section")
    whole_tokens, whole_cot = (
        lax.all_gather(tokens, "section", axis=0, tiled=True),
        lax.all_gather(cotangent, "section", axis=0, tiled=True),
    )
    params = tuple(
        (
            item[0]
            for item in (
                norm_one_gain,
                norm_one_bias,
                qkv_weight,
                qkv_bias,
                rotary_freq,
                proj_weight,
                proj_bias,
                norm_two_gain,
                norm_two_bias,
                up_weight,
                up_bias,
                down_weight,
                down_bias,
            )
        )
    )
    model_width = whole_tokens.shape[1]
    micro_rows = BUFS * ROWS
    total_steps = MICRO + sections - 1
    is_first = section_index == 0
    is_last = section_index == sections - 1

    def run_front(operands):
        inputs_low, layout = operands
        states = layer_states(inputs_low, params, layout, None)
        return (states["output"].astype(jnp.bfloat16), states["log_total"])

    def skip_front(operands):
        return (
            jnp.zeros((micro_rows, model_width), jnp.bfloat16),
            jnp.zeros((BUFS, HEADS, ROWS, 1), jnp.float32),
        )

    def run_back(operands):
        inputs_low, grad_out_low, lse_one, layout = operands
        return layer_back(inputs_low, grad_out_low, params, layout, lse_one)

    def skip_back(operands):
        return (
            jnp.zeros((micro_rows, model_width), jnp.float32),
            tuple((jnp.zeros(item.shape, jnp.float32) for item in params)),
        )

    kept_inputs = jnp.zeros((MICRO, micro_rows, model_width), jnp.bfloat16)
    kept_lse = jnp.zeros((MICRO, BUFS, HEADS, ROWS, 1), jnp.float32)
    final_out = jnp.zeros((MICRO, micro_rows, model_width), jnp.bfloat16)
    incoming = jnp.zeros((micro_rows, model_width), jnp.bfloat16)
    for step_index in range(total_steps):
        micro_index = step_index - section_index
        active = (micro_index >= 0) & (micro_index < MICRO)
        micro_slot = jnp.clip(micro_index, 0, MICRO - 1)
        own_rows = lax.dynamic_slice_in_dim(whole_tokens, micro_slot * micro_rows, micro_rows, 0)
        inputs_low = jnp.where(is_first, own_rows, incoming)
        layout = geometry(lax.dynamic_slice_in_dim(image_kind, micro_slot * BUFS, BUFS, 0))
        output_low, log_total = lax.cond(active, run_front, skip_front, (inputs_low, layout))
        kept_inputs = jnp.where(active, kept_inputs.at[micro_slot].set(inputs_low), kept_inputs)
        kept_lse = jnp.where(active, kept_lse.at[micro_slot].set(log_total), kept_lse)
        final_out = jnp.where(active & is_last, final_out.at[micro_slot].set(output_low), final_out)
        incoming = passed_along(output_low, "section", 1)
    grad_store = jnp.zeros((MICRO, micro_rows, model_width), jnp.float32)
    accum = tuple((jnp.zeros(item.shape, jnp.float32) for item in params))
    grad_incoming = jnp.zeros((micro_rows, model_width), jnp.bfloat16)
    for step_index in range(total_steps):
        micro_index = step_index - (sections - 1 - section_index)
        active = (micro_index >= 0) & (micro_index < MICRO)
        micro_slot = jnp.clip(micro_index, 0, MICRO - 1)
        layout = geometry(lax.dynamic_slice_in_dim(image_kind, micro_slot * BUFS, BUFS, 0))
        own_cot = lax.dynamic_slice_in_dim(whole_cot, micro_slot * micro_rows, micro_rows, 0)
        own_cot = (own_cot.astype(jnp.float32) * layout[3][:, None]).astype(jnp.bfloat16)
        grad_out_low = jnp.where(is_last, own_cot, grad_incoming)
        grad_input, weight_grads = lax.cond(
            active,
            run_back,
            skip_back,
            (kept_inputs[micro_slot], grad_out_low, kept_lse[micro_slot], layout),
        )
        accum = tuple((total + piece for total, piece in zip(accum, weight_grads)))
        grad_store = jnp.where(
            active & is_first, grad_store.at[micro_slot].set(grad_input), grad_store
        )
        grad_incoming = passed_along(grad_input.astype(jnp.bfloat16), "section", -1)
    summed = lax.psum_scatter(accum, "dp", scatter_dimension=0, tiled=True)
    whole_grads = jax.tree.map(
        lambda part, own: part.astype(own.dtype),
        lax.all_gather(as_sent(summed), "dp", axis=0, tiled=True),
        summed,
    )
    live_all = geometry(image_kind)[3][:, None]
    out_term = jnp.where(
        is_last, final_out.reshape(-1, model_width).astype(jnp.float32) * live_all, 0.0
    )
    grad_term = jnp.where(is_first, grad_store.reshape(-1, model_width), 0.0)
    out_share, grad_share = (
        lax.psum_scatter(
            out_term.astype(jnp.bfloat16), "section", scatter_dimension=0, tiled=True
        ).astype(jnp.float32),
        lax.psum_scatter(
            grad_term.astype(jnp.bfloat16), "section", scatter_dimension=0, tiled=True
        ).astype(jnp.float32),
    )
    (
        g_one,
        b_one,
        w_qkv_g,
        b_qkv_g,
        freq_g,
        w_proj_g,
        b_proj_g,
        g_two,
        b_two,
        w_up_g,
        b_up_g,
        w_down_g,
        b_down_g,
    ) = whole_grads
    return (
        out_share.astype(jnp.bfloat16),
        grad_share,
        g_one[None],
        b_one[None],
        w_qkv_g[None],
        b_qkv_g[None],
        freq_g[None],
        w_proj_g[None],
        b_proj_g[None],
        g_two[None],
        b_two[None],
        w_up_g[None],
        b_up_g[None],
        w_down_g[None],
        b_down_g[None],
    )


def solution(mesh):
    return jax.shard_map(
        per_device,
        mesh=mesh,
        in_specs=(
            P(("dp", "section"), None),
            P(("dp", "section"), None),
            P("dp"),
            P("section", None),
            P("section", None),
            P("section", None, None),
            P("section", None),
            P("section", None),
            P("section", None, None),
            P("section", None),
            P("section", None),
            P("section", None),
            P("section", None, None),
            P("section", None),
            P("section", None, None),
            P("section", None),
        ),
        out_specs=(
            P(("dp", "section"), None),
            P(("dp", "section"), None),
            P("section", None),
            P("section", None),
            P("section", None, None),
            P("section", None),
            P("section", None),
            P("section", None, None),
            P("section", None),
            P("section", None),
            P("section", None),
            P("section", None, None),
            P("section", None),
            P("section", None, None),
            P("section", None),
        ),
        check_vma=False,
    )
```

profile of v0, /device:TPU:0, one launch (start us, length us, event | category | flops | bytes accessed | tf_op | source)
XLA Modules:
  0.0 1628.5 jit_solution(13692741998462137349)
XLA Ops:
  26.2 14.8 all-gather.8.cloned.1.call-done
  43.0 45.3 %conditional.10 = (bf16[400,768]{1,0:T(8,128)(2,1)}, f32[1,1,12,400,1]{3,2,4,1,0:T(8,128)S(1)}) conditional(s32[]{:T(128)} %convert_element_type.916, () %tuple.209, (bf16[400,768]{1,0:T(8,128)(2,1)S(1)}, f32[1,768]{1,0:T(1,128)S(1)}, f32[1,768]{1,0:T(1,128)S(1)}, bf16[768,2304]{1,0:T(8,128)(2,1)}, f32[1,2304]{1,0:T(1,128)S(1)}, ...), branch_computations={%region_1.3_spmd, %region_2.10_spmd} | conditional | flops 6202294272 | bytes 84966120 | solution.py:412
  106.2 46.7 %conditional.11 = (bf16[400,768]{1,0:T(8,128)(2,1)}, bf16[1,400,768]{2,1,0:T(8,128)(2,1)}, f32[1,1,12,400,1]{3,2,4,1,0:T(8,128)S(1)}) conditional(s32[]{:T(128)} %convert_element_type.919, () %tuple.211, (bf16[400,768]{1,0:T(8,128)(2,1)S(1)}, f32[1,768]{1,0:T(1,128)S(1)}, f32[1,768]{1,0:T(1,128)S(1)}, bf16[768,2304]{1,0:T(8,128)(2,1)}, ...), branch_computations={%region_10.12_spmd, %region_11.19_spmd} | conditional | flops 6202294272 | bytes 86194928 | solution.py:412
  179.1 45.4 %collective-permute-start.2 = (bf16[400,768]{1,0:T(8,128)(2,1)}, bf16[400,768]{1,0:T(8,128)(2,1)S(1)}, u32[]{:S(2)}, u32[]{:S(2)}) collective-permute-start(bf16[400,768]{1,0:T(8,128)(2,1)} %get-tuple-element.1508), channel_id=1, source_target_pairs={{0,8},{8,16},{16,24},{1,9},{9,17},{17,25},{2,10},{10,18},{18,26},{... | collective-permute-start | bytes 1843208 | tf_op jit(solution)/shard_map/ppermute | solution.py:24
  269.7 24.0 %conditional.15 = (bf16[400,768]{1,0:T(8,128)(2,1)}, f32[768]{0:T(1024)S(1)}, f32[768]{0:T(1024)S(1)}, f32[768,2304]{1,0:T(8,128)}, f32[2304]{0:T(1024)S(1)}, /*...) conditional(s32[]{:T(128)} %convert_element_type.935, ...), branch_computations={%region_52.54_spmd, %region_53.74_spmd} | conditional | flops 16713285632 | bytes 416755712 | solution.py:428
  297.2 53.6 %collective-permute-done.4 = bf16[400,768]{1,0:T(8,128)(2,1)S(1)} collective-permute-done((bf16[400,768]{1,0:T(8,128)(2,1)}, bf16[400,768]{1,0:T(8,128)(2,1)S(1)}, u32[]{:S(2)}, u32[]{:S(2)}) %collective-permute-start.4) | collective-permute-done | bytes 614432 | tf_op jit(solution)/shard_map/ppermute | solution.py:24
  350.8 23.4 %conditional.16 = (bf16[400,768]{1,0:T(8,128)(2,1)}, f32[768]{0:T(1024)S(1)}, f32[768]{0:T(1024)S(1)}, f32[768,2304]{1,0:T(8,128)}, f32[2304]{0:T(1024)S(1)}, /*...) conditional(s32[]{:T(128)} %convert_element_type.940, ...), branch_computations={%region_74.76_spmd, %region_75.96_spmd} | conditional | flops 16713285632 | bytes 416799040 | solution.py:428
  378.2 12.1 collective-permute-done.5
  390.3 23.9 %conditional.17 = (bf16[400,768]{1,0:T(8,128)(2,1)}, f32[768]{0:T(1024)S(1)}, f32[768]{0:T(1024)S(1)}, f32[768,2304]{1,0:T(8,128)}, f32[2304]{0:T(1024)S(1)}, /*...) conditional(s32[]{:T(128)} %convert_element_type.946, ...), branch_computations={%region_96.98_spmd, %region_97.118_spmd} | conditional | flops 16713285632 | bytes 416768576 | solution.py:428
  417.6 373.0 %collective-permute-done.6 = bf16[400,768]{1,0:T(8,128)(2,1)S(1)} collective-permute-done((bf16[400,768]{1,0:T(8,128)(2,1)}, bf16[400,768]{1,0:T(8,128)(2,1)S(1)}, u32[]{:S(2)}, u32[]{:S(2)}) %collective-permute-start.6) | collective-permute-done | bytes 614432 | tf_op jit(solution)/shard_map/ppermute | solution.py:24
  790.6 132.7 %conditional.18 = (bf16[400,768]{1,0:T(8,128)(2,1)}, f32[768]{0:T(1024)S(1)}, f32[768]{0:T(1024)S(1)}, f32[768,2304]{1,0:T(8,128)}, f32[2304]{0:T(1024)S(1)}, /*...) conditional(s32[]{:T(128)} %convert_element_type.952, ...), branch_computations={%region_118.120_spmd, %region_119.140_spmd} | conditional | flops 16713285632 | bytes 416762368 | solution.py:428
  938.1 123.0 %conditional.19 = (f32[768]{0:T(1024)S(1)}, f32[768]{0:T(1024)S(1)}, f32[768,2304]{1,0:T(8,128)}, f32[2304]{0:T(1024)S(1)}, f32[768]{0:T(1024)S(1)}, /*index=5*/...) conditional(s32[]{:T(128)} %convert_element_type.958, ...), branch_computations={%region_140.142_spmd, %region_141.162_spmd} | conditional | flops 16713285632 | bytes 422492544 | solution.py:428
  1067.8 15.5 add_add_fusion.2
  1083.4 20.9 %add_add_fusion.1 = f32[768,3072]{1,0:T(8,128)} fusion(f32[768,3072]{1,0:T(8,128)} %get-tuple-element.1571, f32[768,3072]{1,0:T(8,128)} %get-tuple-element.1570, f32[768,3072]{1,0:T(8,128)} %get-tuple-element.1569, f32[768,3072]{1,0:T(8,128)} %get-tuple-element.1567, f32[768,3072]{1,0:T(8,128)} %get-tuple-element.1568), kind=kLoop, calls=%fused_computation.903 | loop fusion | flops 9437184 | bytes 56623104 | tf_op jit(solution)/shard_map/add | solution.py:434
  1104.4 20.0 %add_add_fusion = f32[3072,768]{1,0:T(8,128)} fusion(f32[3072,768]{1,0:T(8,128)} %get-tuple-element.1581, f32[3072,768]{1,0:T(8,128)} %get-tuple-element.1580, f32[3072,768]{1,0:T(8,128)} %get-tuple-element.1579, f32[3072,768]{1,0:T(8,128)} %get-tuple-element.1577, f32[3072,768]{1,0:T(8,128)} %get-tuple-element.1578), kind=kLoop, calls=%fused_computation.902 | loop fusion | flops 9437184 | bytes 56623104 | tf_op jit(solution)/shard_map/add | solution.py:434
  1138.8 45.3 %reduce-scatter.11.cloned.1.call-done = f32[96,2304]{1,0:T(8,128)} async-done(((f32[768,2304]{1,0:T(8,128)}), f32[96,2304]{1,0:T(8,128)}) %reduce-scatter.11.cloned.1.call-update) | async-done | bytes 884752 | tf_op jit(solution)/shard_map/reduce_scatter | solution.py:439
  1186.2 98.5 %reduce-scatter.15.cloned.1.call-done = f32[96,3072]{1,0:T(8,128)} async-done(((f32[768,3072]{1,0:T(8,128)}), f32[96,3072]{1,0:T(8,128)}) %reduce-scatter.15.cloned.1.call-update) | async-done | bytes 1179664 | tf_op jit(solution)/shard_map/reduce_scatter | solution.py:439
  1286.9 98.4 %reduce-scatter.17.cloned.1.call-done = f32[384,768]{1,0:T(8,128)} async-done(((f32[3072,768]{1,0:T(8,128)}), f32[384,768]{1,0:T(8,128)}) %reduce-scatter.17.cloned.1.call-update) | async-done | bytes 1179664 | tf_op jit(solution)/shard_map/reduce_scatter | solution.py:439
  1404.4 26.6 %all-reduce.19 = (bf16[768]{0:T(1024)(128)(2,1)S(1)}, bf16[768]{0:T(1024)(128)(2,1)S(1)}, bf16[2304]{0:T(1024)(128)(2,1)S(1)}, bf16[768]{0:T(1024)(128)(2,1)S(1)...) all-reduce(f32[768]{0:T(1024)S(1)} %add_add_fusion.12, ...), channel_id=4, replica_groups=mesh['section'=4,'dp'=8] {'dp'}, use_global_device_ids=true, to_apply=%region_162.164.clone | all-reduce | flops 10752 | bytes 64512
  1433.2 26.4 %all-reduce.20 = (bf16[768]{0:T(1024)(128)(2,1)S(1)}, bf16[768]{0:T(1024)(128)(2,1)S(1)}, bf16[2304]{0:T(1024)(128)(2,1)S(1)}, bf16[768]{0:T(1024)(128)(2,1)S(1)...) all-reduce(bf16[768]{0:T(1024)(128)(2,1)S(1)} %dynamic-update-slice, ...), channel_id=1, replica_groups=mesh['section'=4,'dp'=8] {'dp'}, use_global_device_ids=true, to_apply=%add | all-reduce | flops 7680 | bytes 30720
  1463.8 13.0 all-gather
  1490.2 47.3 %all-gather.16.cloned.1.call-done = bf16[768,3072]{1,0:T(8,128)(2,1)} async-done(((bf16[96,3072]{1,0:T(8,128)(2,1)}), bf16[768,3072]{1,0:T(8,128)(2,1)}) %all-gather.16.cloned.1.call-update) | async-done | bytes 4718608 | tf_op jit(solution)/shard_map/all_gather | solution.py:442
  1544.8 44.9 %all-gather.18.cloned.1.call-done = bf16[3072,768]{1,0:T(8,128)(2,1)} async-done(((bf16[384,768]{1,0:T(8,128)(2,1)}), bf16[3072,768]{1,0:T(8,128)(2,1)}) %all-gather.18.cloned.1.call-update) | async-done | bytes 4718608 | tf_op jit(solution)/shard_map/all_gather | solution.py:442
  1596.6 24.9 %reduce-scatter.19.cloned.1.call-done = bf16[200,768]{1,0:T(8,128)(2,1)} async-done(((bf16[800,768]{1,0:T(8,128)(2,1)}), bf16[200,768]{1,0:T(8,128)(2,1)}) %reduce-scatter.19.cloned.1.call-update) | async-done | bytes 307216
  (783 shorter events, 594.2 us)
Async XLA Ops:
  7.3 33.7 %all-gather.8.cloned.1.call-start = ((), (), s32[]{:S(2)}) async-start(), calls=%async_computation.6 | async-start | bytes 1536000 | tf_op jit(solution)/shard_map/all_gather | solution.py:351
  8.0 217.4 %all-gather.10.cloned.1.call-start = ((), (), s32[]{:S(2)}) async-start(), calls=%async_computation.7 | async-start | bytes 1536000 | tf_op jit(solution)/shard_map/all_gather | solution.py:352
  8.8 1128.3 %reduce-scatter.13.cloned.1.call-start = ((), (), s32[]{:S(2)}) async-start(), calls=%async_computation.10 | async-start | bytes 2654208 | tf_op jit(solution)/shard_map/reduce_scatter | solution.py:439
  88.4 14.9 collective-permute-start
  152.8 17.2 %collective-permute-start.1 = (bf16[400,768]{1,0:T(8,128)(2,1)}, bf16[400,768]{1,0:T(8,128)(2,1)S(1)}, u32[]{:S(2)}, u32[]{:S(2)}) collective-permute-start(bf16[400,768]{1,0:T(8,128)(2,1)} %get-tuple-element.1506), channel_id=1, source_target_pairs={{0,8},{8,16},{16,24},{1,9},{9,17},{17,25},{2,10},{10,18},{18,26},{... | collective-permute-start | bytes 1843208 | tf_op jit(solution)/shard_map/ppermute | solution.py:24
  179.1 57.2 %collective-permute-start.2 = (bf16[400,768]{1,0:T(8,128)(2,1)}, bf16[400,768]{1,0:T(8,128)(2,1)S(1)}, u32[]{:S(2)}, u32[]{:S(2)}) collective-permute-start(bf16[400,768]{1,0:T(8,128)(2,1)} %get-tuple-element.1508), channel_id=1, source_target_pairs={{0,8},{8,16},{16,24},{1,9},{9,17},{17,25},{2,10},{10,18},{18,26},{... | collective-permute-start | bytes 1843208 | tf_op jit(solution)/shard_map/ppermute | solution.py:24
  243.4 16.3 collective-permute-start.3
  293.7 57.0 %collective-permute-start.4 = (bf16[400,768]{1,0:T(8,128)(2,1)}, bf16[400,768]{1,0:T(8,128)(2,1)S(1)}, u32[]{:S(2)}, u32[]{:S(2)}) collective-permute-start(bf16[400,768]{1,0:T(8,128)(2,1)} %get-tuple-element.1517), channel_id=1, source_target_pairs={{8,0},{16,8},{24,16},{9,1},{17,9},{25,17},{10,2},{18,10},{26,18},{... | collective-permute-start | bytes 1843208 | tf_op jit(solution)/shard_map/ppermute | solution.py:24
  374.8 15.5 collective-permute-start.5
  414.2 376.4 %copy-start.267 = (f32[768]{0:T(1024)}, f32[768]{0:T(1024)S(1)}, u32[]{:S(2)}) copy-start(f32[768]{0:T(1024)S(1)} %get-tuple-element.1524) | copy-start | bytes 9220
  414.2 376.4 %copy-start.270 = (f32[768]{0:T(1024)}, f32[768]{0:T(1024)S(1)}, u32[]{:S(2)}) copy-start(f32[768]{0:T(1024)S(1)} %get-tuple-element.1529) | copy-start | bytes 9220
  414.2 376.4 %copy-start.184 = (f32[2304]{0:T(1024)}, f32[2304]{0:T(1024)S(1)}, u32[]{:S(2)}) copy-start(f32[2304]{0:T(1024)S(1)} %get-tuple-element.1539) | copy-start | bytes 27652
  414.2 376.4 %collective-permute-start.6 = (bf16[400,768]{1,0:T(8,128)(2,1)}, bf16[400,768]{1,0:T(8,128)(2,1)S(1)}, u32[]{:S(2)}, u32[]{:S(2)}) collective-permute-start(bf16[400,768]{1,0:T(8,128)(2,1)} %get-tuple-element.1519), channel_id=1, source_target_pairs={{8,0},{16,8},{24,16},{9,1},{17,9},{25,17},{10,2},{18,10},{26,18},{... | collective-permute-start | bytes 1843208 | tf_op jit(solution)/shard_map/ppermute | solution.py:24
  924.6 13.6 collective-permute-start.7
  1067.8 116.3 %reduce-scatter.11.cloned.1.call-start = ((), (), s32[]{:S(2)}) async-start(), calls=%async_computation.8 | async-start | bytes 7962624 | tf_op jit(solution)/shard_map/reduce_scatter | solution.py:439
  1083.4 201.3 %reduce-scatter.15.cloned.1.call-start = ((), (), s32[]{:S(2)}) async-start(), calls=%async_computation.12 | async-start | bytes 10616832 | tf_op jit(solution)/shard_map/reduce_scatter | solution.py:439
  1104.3 281.0 %reduce-scatter.17.cloned.1.call-start = ((), (), s32[]{:S(2)}) async-start(), calls=%async_computation.14 | async-start | bytes 10616832 | tf_op jit(solution)/shard_map/reduce_scatter | solution.py:439
  1124.4 353.6 %reduce-scatter.21.cloned.1.call-start = ((), (), s32[]{:S(2)}) async-start(), calls=%async_computation.17 | async-start | bytes 1536000
  1137.0 342.8 %all-gather.14.cloned.1.call-start = ((), (), s32[]{:S(2)}) async-start(), calls=%async_computation.11 | async-start | bytes 1327104 | tf_op jit(solution)/shard_map/all_gather | solution.py:442
  1138.7 345.9 %all-gather.12.cloned.1.call-start = ((), (), s32[]{:S(2)}) async-start(), calls=%async_computation.9 | async-start | bytes 3981312 | tf_op jit(solution)/shard_map/all_gather | solution.py:442
  1186.1 202.4 %copy-start.332 = (u32[32]{0:T(128)S(1)}, u32[32]{0:T(128)}, u32[]{:S(2)}) copy-start(u32[32]{0:T(128)} %constant.1057) | copy-start | bytes 388
  1186.1 351.4 %all-gather.16.cloned.1.call-start = ((), (), s32[]{:S(2)}) async-start(), calls=%async_computation.13 | async-start | bytes 5308416 | tf_op jit(solution)/shard_map/all_gather | solution.py:442
  1286.9 302.9 %all-gather.18.cloned.1.call-start = ((), (), s32[]{:S(2)}) async-start(), calls=%async_computation.15 | async-start | bytes 5308416 | tf_op jit(solution)/shard_map/all_gather | solution.py:442
  1387.5 234.0 %reduce-scatter.19.cloned.1.call-start = ((), (), s32[]{:S(2)}) async-start(), calls=%async_computation.16 | async-start | bytes 1536000
  (179 other events, 1801.8 us)
Sparse Core Ops, SparseCore 0:
  10.0 30.9 all-gather.7
  42.8 33.4 all-gather.9
  1067.9 36.8 reduce-scatter.12
  1107.5 76.4 reduce-scatter.10
  1186.8 97.8 reduce-scatter.14
  1287.4 97.8 reduce-scatter.16
  1388.3 27.4 reduce-scatter.20
  1418.2 22.9 all-gather.13
  1443.5 41.1 all-gather.11
  1486.8 50.5 all-gather.15
  1539.2 50.5 all-gather.17
  1593.5 27.9 reduce-scatter.18
where the time goes:
time: 1640 us; the launch traced here: 1630 us
  waiting for transfers between devices  853 us (52%)
  other arithmetic  246 us (15%)
  matrix products  184 us (11%)
  local copies, waits for them, and re-layouts  147 us (9%)
  blocking collectives  66 us (4%)
  starting transfers between devices  62.3 us (4%)
  between operations  38.6 us (2%)
  loops' own time  32.4 us (2%)
    ppermute x8, waiting for transfers between devices, passed_along(): lax.ppermute(value, axis, [(source, source + steps) for source in range(i...  475 us
    reduce_scatter x4, waiting for transfers between devices, per_device(): summed = lax.psum_scatter(accum, 'dp', scatter_dimension=0, tiled=True)  242 us
    all_gather x4, waiting for transfers between devices, per_device(): lax.all_gather(as_sent(summed), 'dp', axis=0, tiled=True)  94.2 us
    add x13, other arithmetic, per_device(): accum = tuple((total + piece for total, piece in zip(accum, weight_grads)))  63.1 us
    ppermute x8, starting transfers between devices, passed_along(): lax.ppermute(value, axis, [(source, source + steps) for source in range(i...  61.8 us
    another operation x58, local copies, waits for them, and re-layouts  60 us
    unnamed x2, blocking collectives  53.1 us
  transfers between devices with their start and end apart: 20, of which 16 were waited for; matrix products, arithmetic and copies ran while one was open for 15% of the time, Pallas kernels for 0%

commit v1 on v0

v1 whole, which is shorter than its diff:
```python
from functools import partial
import math

import jax
import jax.numpy as jnp
import numpy as np
from jax import lax
from jax.experimental import pallas as pl
from jax.experimental.pallas import tpu as pltpu
from jax.sharding import PartitionSpec as P

HEADS = 12
SIDE_LARGE = 20
SIDE_MID = 16
SIDE_SMALL = 14
MICRO = 2
ROWS = 400
KEYS = 512
WIDTH = 768
HIDDEN = 3072
PAIRS = HEADS // 2
EPSILON = 1e-06
MASKED = -1e30
LOG2E = math.log2(math.e)
LN2 = math.log(2.0)
GELU_ONE = math.sqrt(2.0 / math.pi)
GELU_TWO = GELU_ONE * 0.044715

f32 = jnp.float32
bf16 = jnp.bfloat16
NT = (((1,), (1,)), ((), ()))

VEC_SIZES = (WIDTH, WIDTH, 3 * WIDTH, WIDTH, WIDTH, WIDTH, HIDDEN, WIDTH)
VEC_AT = tuple(int(v) for v in np.cumsum((0,) + VEC_SIZES))


def vec_part(vec_ref, index):
    return vec_ref[:, VEC_AT[index] : VEC_AT[index + 1]]


def swap_halves(values):
    lane = lax.broadcasted_iota(jnp.int32, values.shape, 1) % 64
    width = values.shape[1]
    return jnp.where(lane < 32, pltpu.roll(values, width - 32, 1), pltpu.roll(values, 32, 1))


def norm_parts(values):
    center = values - jnp.mean(values, axis=-1, keepdims=True)
    inverse = lax.rsqrt(jnp.mean(center * center, axis=-1, keepdims=True) + EPSILON)
    return center * inverse, inverse


def gelu_parts(pre):
    low = pre.astype(bf16)
    square = low * low
    tanh = jnp.tanh(low * (bf16(GELU_ONE) + bf16(GELU_TWO) * square))
    half = bf16(0.5) + bf16(0.5) * tanh
    value = low * half
    slope = half + (value - value * half) * (bf16(2 * GELU_ONE) + bf16(6 * GELU_TWO) * square)
    return value, slope


class Copies:
    def __init__(self, sems):
        self.sems = sems
        self.used = 0

    def start(self, source, target):
        copy = pltpu.make_async_copy(source, target, self.sems.at[self.used])
        self.used += 1
        copy.start()
        return copy


STATE_SHAPES = (
    ("x", (ROWS, WIDTH), bf16),
    ("a", (ROWS, WIDTH), bf16),
    ("qkv", (ROWS, 3 * WIDTH), bf16),
    ("e", (HEADS, ROWS, KEYS), bf16),
    ("linv", (ROWS, WIDTH), f32),
    ("o", (ROWS, WIDTH), bf16),
    ("n2", (ROWS, WIDTH), bf16),
    ("r2", (ROWS, 128), f32),
    ("c", (ROWS, WIDTH), bf16),
    ("g", (ROWS, HIDDEN), bf16),
    ("gp", (ROWS, HIDDEN), bf16),
)
STATES = tuple(name for name, _, _ in STATE_SHAPES)


def front_kernel(first, scal, *refs):
    ins, rest = refs[:8], refs[8:]
    x_in, vec_in, geo_in, cos_in, sin_in, wqkv_in, wp_in, wu_in = ins
    wd_in = rest[0]
    rest = rest[1:]
    if not first:
        rest = rest[len(STATES) :]
    out_ref = rest[0]
    state = dict(zip(STATES, rest[1 : 1 + len(STATES)]))
    (
        x_v, vec_v, geo_v, cos_v, sin_v, wqkv_v, wp_v, wu_v, wd_v,
        a_v, qkv_v, e_v, s_v, li_v, o_v, m_v, n2_v, r2_v, c_v, g_v, gp_v, qcode_v, kcode_v, out_v, sems,
    ) = rest[1 + len(STATES) :]

    @pl.when(scal[0] == 1)
    def _():
        slot = scal[1]
        copies = Copies(sems)
        get_x = copies.start(x_in, x_v)
        get_vec = copies.start(vec_in, vec_v)
        get_qkv = copies.start(wqkv_in, wqkv_v)
        get_cos = copies.start(cos_in.at[slot], cos_v)
        get_sin = copies.start(sin_in.at[slot], sin_v)
        get_geo = copies.start(geo_in.at[slot], geo_v)
        get_wp = copies.start(wp_in, wp_v)
        get_wu = copies.start(wu_in, wu_v)
        get_wd = copies.start(wd_in, wd_v)
        puts = []

        def put(source, name):
            puts.append(copies.start(source, state[name].at[slot]))

        get_x.wait()
        get_vec.wait()
        put(x_v, "x")
        normed, _ = norm_parts(x_v[...].astype(f32))
        a_v[...] = (normed * vec_part(vec_v, 0) + vec_part(vec_v, 1)).astype(bf16)
        put(a_v, "a")
        qkv_v[ROWS:KEYS, :] = jnp.zeros((KEYS - ROWS, 3 * WIDTH), bf16)
        get_geo.wait()
        segment = geo_v[:, 2:3]
        code = (lax.broadcasted_iota(jnp.int32, (KEYS, 128), 1) % 64).astype(f32)
        qcode_v[...] = jnp.where(segment[:ROWS] == code[:ROWS], 1.0, 0.0).astype(bf16)
        kcode_v[...] = jnp.where((segment != code) & (code < 4), MASKED, 0.0).astype(bf16)
        get_qkv.wait()
        get_cos.wait()
        get_sin.wait()
        for part in range(3):
            at = part * WIDTH
            acc = jnp.dot(a_v[...], wqkv_v[:, at : at + WIDTH], preferred_element_type=f32)
            acc = acc + vec_v[:, VEC_AT[2] + at : VEC_AT[2] + at + WIDTH]
            if part < 2:
                acc = acc * cos_v[...] + swap_halves(acc) * sin_v[...]
            if part == 0:
                acc = acc * (LOG2E / 8.0)
            qkv_v[:ROWS, at : at + WIDTH] = acc.astype(bf16)
        put(qkv_v.at[pl.ds(0, ROWS)], "qkv")

        def pair_step(pair, carry):
            lanes = pl.ds(pl.multiple_of(pair * 128, 128), 128)
            klanes = pl.ds(pl.multiple_of(pair * 128 + WIDTH, 128), 128)
            vlanes = pl.ds(pl.multiple_of(pair * 128 + 2 * WIDTH, 128), 128)
            q_two = qkv_v[:ROWS, lanes]
            k_two = qkv_v[:, klanes]
            v_two = qkv_v[:, vlanes]
            lane_q = lax.broadcasted_iota(jnp.int32, (ROWS, 128), 1) // 64
            lane_k = lax.broadcasted_iota(jnp.int32, (KEYS, 128), 1) // 64
            for head in range(2):
                q_one = jnp.where(lane_q == head, q_two, qcode_v[...])
                k_one = jnp.where(lane_k == head, k_two, kcode_v[...])
                s_v[head] = lax.dot_general(q_one, k_one, NT, preferred_element_type=f32)
            sums = []
            for head in range(2):
                v_one = jnp.where(lane_k == head, v_two, bf16(1.0))
                scores = s_v[head]
                peak = jnp.max(scores, axis=1, keepdims=True)
                e_v[2 * pair + head] = jnp.exp2(scores - peak).astype(bf16)
                sums.append(jnp.dot(e_v[2 * pair + head], v_one, preferred_element_type=f32))
            total = pltpu.roll(jnp.where(lane_q == 0, sums[1], sums[0]), 64, 1)
            inverse = 1.0 / total
            li_v[:, lanes] = inverse
            o_v[:, lanes] = (jnp.where(lane_q == 0, sums[0], sums[1]) * inverse).astype(bf16)
            return carry

        lax.fori_loop(0, PAIRS, pair_step, 0)
        put(e_v, "e")
        put(li_v, "linv")
        put(o_v, "o")
        get_wp.wait()
        middle = (
            x_v[...].astype(f32)
            + jnp.dot(o_v[...], wp_v[...], preferred_element_type=f32)
            + vec_part(vec_v, 3)
        )
        m_v[...] = middle
        normed, inverse = norm_parts(middle)
        n2_v[...] = normed.astype(bf16)
        r2_v[...] = jnp.broadcast_to(inverse, (ROWS, 128))
        c_v[...] = (normed * vec_part(vec_v, 4) + vec_part(vec_v, 5)).astype(bf16)
        put(n2_v, "n2")
        put(r2_v, "r2")
        put(c_v, "c")
        get_wu.wait()
        chunk = 1024

        def up_step(step, carry):
            lanes = pl.ds(pl.multiple_of(step * chunk, chunk), chunk)
            blanes = pl.ds(pl.multiple_of(step * chunk + VEC_AT[6], 128), chunk)
            pre = jnp.dot(c_v[...], wu_v[:, lanes], preferred_element_type=f32) + vec_v[:, blanes]
            value, slope = gelu_parts(pre)
            g_v[:, lanes] = value
            gp_v[:, lanes] = slope
            return carry

        lax.fori_loop(0, HIDDEN // chunk, up_step, 0)
        put(g_v, "g")
        put(gp_v, "gp")
        get_wd.wait()
        out = m_v[...] + jnp.dot(g_v[...], wd_v[...], preferred_element_type=f32) + vec_part(vec_v, 7)
        out_v[...] = out.astype(bf16)
        put_out = copies.start(out_v, out_ref)
        for copy in puts:
            copy.wait()
        put_out.wait()


ANY = pl.BlockSpec(memory_space=pl.ANY)
VMEM_LIMIT = 60 * 2**20


def vmem(*shape, dtype=bf16):
    return pltpu.VMEM(shape, dtype)


def front_call(scal, x, common, weights, states):
    vec, geo, cosine, sine = common
    wqkv, wp, wu, wd = weights
    first = states is None
    state_out = [jax.ShapeDtypeStruct((MICRO,) + shape, dtype) for _, shape, dtype in STATE_SHAPES]
    operands = [scal, x, vec, geo, cosine, sine, wqkv, wp, wu, wd] + ([] if first else list(states))
    scratch = [
        vmem(ROWS, WIDTH), vmem(1, VEC_AT[-1], dtype=f32), vmem(KEYS, 128, dtype=f32),
        vmem(ROWS, WIDTH, dtype=f32), vmem(ROWS, WIDTH, dtype=f32),
        vmem(WIDTH, 3 * WIDTH), vmem(WIDTH, WIDTH), vmem(WIDTH, HIDDEN), vmem(HIDDEN, WIDTH),
        vmem(ROWS, WIDTH), vmem(KEYS, 3 * WIDTH), vmem(HEADS, ROWS, KEYS), vmem(2, ROWS, KEYS, dtype=f32),
        vmem(ROWS, WIDTH, dtype=f32), vmem(ROWS, WIDTH), vmem(ROWS, WIDTH, dtype=f32),
        vmem(ROWS, WIDTH), vmem(ROWS, 128, dtype=f32), vmem(ROWS, WIDTH),
        vmem(ROWS, HIDDEN), vmem(ROWS, HIDDEN), vmem(ROWS, 128), vmem(KEYS, 128), vmem(ROWS, WIDTH),
        pltpu.SemaphoreType.DMA((24,)),
    ]
    results = pl.pallas_call(
        partial(front_kernel, first),
        out_shape=[jax.ShapeDtypeStruct((ROWS, WIDTH), bf16)] + state_out,
        in_specs=[pl.BlockSpec(memory_space=pltpu.SMEM)] + [ANY] * (len(operands) - 1),
        out_specs=[ANY] * (1 + len(STATES)),
        scratch_shapes=scratch,
        input_output_aliases={} if first else {10 + i: 1 + i for i in range(len(STATES))},
        compiler_params=pltpu.CompilerParams(vmem_limit_bytes=VMEM_LIMIT),
        name="layer_front",
    )(*operands)
    return results[0], tuple(results[1:])


BACK_SHAPES = (
    ("du", (ROWS, HIDDEN), bf16),
    ("dz", (ROWS, WIDTH), bf16),
    ("dy", (ROWS, WIDTH), bf16),
    ("small_two", (8, WIDTH), f32),
)
BACKS = tuple(name for name, _, _ in BACK_SHAPES)


def branch_kernel(first, scal, dy_in, vec_in, wd_in, wu_in, wp_in, gp_in, n2_in, r2_in, linv_in, *rest):
    if not first:
        rest = rest[len(BACKS) :]
    dm_ref, dop_ref = rest[:2]
    state = dict(zip(BACKS, rest[2 : 2 + len(BACKS)]))
    (
        dy_v, vec_v, wd_v, wu_v, wp_v, gp_v, n2_v, r2_v, li_v, du_v, dz_v, dm_v, dop_v, small_v, sems,
    ) = rest[2 + len(BACKS) :]

    @pl.when(scal[0] == 1)
    def _():
        slot = scal[1]
        copies = Copies(sems)
        get_dy = copies.start(dy_in, dy_v)
        get_wd = copies.start(wd_in, wd_v)
        get_gp = copies.start(gp_in.at[slot], gp_v)
        get_wu = copies.start(wu_in, wu_v)
        get_wp = copies.start(wp_in, wp_v)
        later = [
            copies.start(vec_in, vec_v),
            copies.start(n2_in.at[slot], n2_v),
            copies.start(r2_in.at[slot], r2_v),
            copies.start(linv_in.at[slot], li_v),
        ]
        puts = []

        def put(source, name):
            puts.append(copies.start(source, state[name].at[slot]))

        get_dy.wait()
        put(dy_v, "dy")
        get_wd.wait()
        get_gp.wait()
        chunk = 1024

        def act_step(step, carry):
            part = pl.ds(pl.multiple_of(step * chunk, chunk), chunk)
            act = lax.dot_general(dy_v[...], wd_v[part, :], NT, preferred_element_type=f32)
            du_v[:, part] = act.astype(bf16) * gp_v[:, part]
            return carry

        lax.fori_loop(0, HIDDEN // chunk, act_step, 0)
        put(du_v, "du")
        get_wu.wait()
        dc = lax.dot_general(du_v[...], wu_v[...], NT, preferred_element_type=f32)
        for copy in later:
            copy.wait()
        normed = n2_v[...].astype(f32)
        small_v[0:1, :] = jnp.sum(dc * normed, axis=0, keepdims=True)
        small_v[1:2, :] = jnp.sum(dc, axis=0, keepdims=True)
        put(small_v, "small_two")
        hat = dc * vec_part(vec_v, 4)
        dm = dy_v[...].astype(f32) + r2_v[:, 0:1] * (
            hat
            - jnp.mean(hat, axis=-1, keepdims=True)
            - normed * jnp.mean(hat * normed, axis=-1, keepdims=True)
        )
        dm_v[...] = dm
        dz_v[...] = dm.astype(bf16)
        put(dz_v, "dz")
        put_dm = copies.start(dm_v, dm_ref)
        get_wp.wait()
        do = lax.dot_general(dz_v[...], wp_v[...], NT, preferred_element_type=f32)
        dop_v[...] = (do * li_v[...]).astype(bf16)
        put_do = copies.start(dop_v, dop_ref)
        for copy in puts + [put_dm, put_do]:
            copy.wait()


def branch_call(scal, dy, vec, weights, fronts, backs):
    wqkv, wp, wu, wd = weights
    first = backs is None
    back_out = [jax.ShapeDtypeStruct((MICRO,) + shape, dtype) for _, shape, dtype in BACK_SHAPES]
    operands = [scal, dy, vec, wd, wu, wp, fronts["gp"], fronts["n2"], fronts["r2"], fronts["linv"]]
    count = len(operands)
    operands += [] if first else list(backs)
    scratch = [
        vmem(ROWS, WIDTH), vmem(1, VEC_AT[-1], dtype=f32), vmem(HIDDEN, WIDTH), vmem(WIDTH, HIDDEN), vmem(WIDTH, WIDTH),
        vmem(ROWS, HIDDEN), vmem(ROWS, WIDTH), vmem(ROWS, 128, dtype=f32), vmem(ROWS, WIDTH, dtype=f32),
        vmem(ROWS, HIDDEN), vmem(ROWS, WIDTH), vmem(ROWS, WIDTH, dtype=f32), vmem(ROWS, WIDTH), vmem(8, WIDTH, dtype=f32),
        pltpu.SemaphoreType.DMA((16,)),
    ]
    results = pl.pallas_call(
        partial(branch_kernel, first),
        out_shape=[jax.ShapeDtypeStruct((ROWS, WIDTH), f32), jax.ShapeDtypeStruct((ROWS, WIDTH), bf16)] + back_out,
        in_specs=[pl.BlockSpec(memory_space=pltpu.SMEM)] + [ANY] * (len(operands) - 1),
        out_specs=[ANY] * (2 + len(BACKS)),
        scratch_shapes=scratch,
        input_output_aliases={} if first else {count + i: 2 + i for i in range(len(BACKS))},
        compiler_params=pltpu.CompilerParams(vmem_limit_bytes=VMEM_LIMIT),
        name="branch_back",
    )(*operands)
    return results[0], results[1], tuple(results[2:])


LAST_SHAPES = (
    ("dqkv", (ROWS, 3 * WIDTH), bf16),
    ("small_one", (8, WIDTH), f32),
)
LASTS = tuple(name for name, _, _ in LAST_SHAPES)


def attention_kernel(
    first, scal, dm_in, dop_in, vec_in, geo_in, cos_in, sin_in, wqkv_in, qkv_in, e_in, o_in, x_in, *rest
):
    if not first:
        rest = rest[len(LASTS) :]
    dx_ref = rest[0]
    state = dict(zip(LASTS, rest[1 : 1 + len(LASTS)]))
    (
        dm_v, dop_v, vec_v, geo_v, cos_v, sin_v, wqkv_v, qkv_v, e_v, o_v, x_v,
        qt_v, dot_v, dq_v, dkt_v, dvt_v, dqkv_v, small_v, dx_v, sems,
    ) = rest[1 + len(LASTS) :]

    @pl.when(scal[0] == 1)
    def _():
        slot = scal[1]
        copies = Copies(sems)
        get_dop = copies.start(dop_in, dop_v)
        get_qkv = copies.start(qkv_in.at[slot], qkv_v.at[pl.ds(0, ROWS)])
        get_o = copies.start(o_in.at[slot], o_v)
        get_e = copies.start(e_in.at[slot], e_v)
        get_x = copies.start(x_in.at[slot], x_v)
        later = [
            copies.start(cos_in.at[slot], cos_v),
            copies.start(sin_in.at[slot], sin_v),
            copies.start(geo_in.at[slot], geo_v),
            copies.start(vec_in, vec_v),
            copies.start(dm_in, dm_v),
        ]
        get_w = copies.start(wqkv_in, wqkv_v)
        puts = []

        def put(source, name):
            puts.append(copies.start(source, state[name].at[slot]))

        qkv_v[ROWS:KEYS, :] = jnp.zeros((KEYS - ROWS, 3 * WIDTH), bf16)
        get_dop.wait()
        dot_v[...] = dop_v[...].T
        get_qkv.wait()
        qt_v[...] = qkv_v[:ROWS, :WIDTH].T
        get_o.wait()
        get_e.wait()

        def pair_step(pair, carry):
            lanes = pl.ds(pl.multiple_of(pair * 128, 128), 128)
            klanes = pl.ds(pl.multiple_of(pair * 128 + WIDTH, 128), 128)
            vlanes = pl.ds(pl.multiple_of(pair * 128 + 2 * WIDTH, 128), 128)
            do_two = dop_v[:, lanes]
            k_two = qkv_v[:, klanes]
            v_two = qkv_v[:, vlanes]
            prod = do_two.astype(f32) * o_v[:, lanes].astype(f32)
            lane = lax.broadcasted_iota(jnp.int32, (ROWS, 128), 1) // 64
            dqs = []
            for head in range(2):
                rows = pl.ds(pl.multiple_of(pair * 128 + head * 64, 64), 64)
                do_one = jnp.where(lane == head, do_two, bf16(0.0))
                dp = lax.dot_general(do_one, v_two, NT, preferred_element_type=f32)
                delta = jnp.sum(jnp.where(lane == head, prod, 0.0), axis=1, keepdims=True)
                probs = e_v[2 * pair + head]
                ds = probs * (dp - delta).astype(bf16)
                dqs.append(jnp.dot(ds, k_two, preferred_element_type=f32))
                dkt_v[rows, :] = jnp.dot(qt_v[rows, :], ds, preferred_element_type=f32)
                dvt_v[rows, :] = jnp.dot(dot_v[rows, :], probs, preferred_element_type=f32).astype(bf16)
            dq_v[:, lanes] = jnp.where(lane == 0, dqs[0], dqs[1])
            return carry

        lax.fori_loop(0, PAIRS, pair_step, 0)
        for copy in later:
            copy.wait()
        dqkv_v[:, 2 * WIDTH :] = dvt_v[...].T[:ROWS]
        dk = dkt_v[...].T[:ROWS]
        dq = dq_v[...]
        turn = dq * swap_halves(qkv_v[:ROWS, :WIDTH].astype(f32)) + dk * swap_halves(
            qkv_v[:ROWS, WIDTH : 2 * WIDTH].astype(f32)
        )
        small_v[2:3, :] = LN2 * jnp.sum(turn * geo_v[:ROWS, 0:1], axis=0, keepdims=True)
        small_v[3:4, :] = LN2 * jnp.sum(turn * geo_v[:ROWS, 1:2], axis=0, keepdims=True)
        dqkv_v[:, :WIDTH] = (0.125 * (dq * cos_v[...] - swap_halves(dq) * sin_v[...])).astype(bf16)
        dqkv_v[:, WIDTH : 2 * WIDTH] = (LN2 * (dk * cos_v[...] - swap_halves(dk) * sin_v[...])).astype(bf16)
        put(dqkv_v, "dqkv")
        get_x.wait()
        normed, inverse = norm_parts(x_v[...].astype(f32))
        get_w.wait()
        da = lax.dot_general(dqkv_v[...], wqkv_v[...], NT, preferred_element_type=f32)
        small_v[0:1, :] = jnp.sum(da * normed, axis=0, keepdims=True)
        small_v[1:2, :] = jnp.sum(da, axis=0, keepdims=True)
        put(small_v, "small_one")
        hat = da * vec_part(vec_v, 0)
        dx = dm_v[...] + inverse * (
            hat
            - jnp.mean(hat, axis=-1, keepdims=True)
            - normed * jnp.mean(hat * normed, axis=-1, keepdims=True)
        )
        dx_v[...] = dx.astype(bf16)
        put_dx = copies.start(dx_v, dx_ref)
        for copy in puts + [put_dx]:
            copy.wait()


def attention_call(scal, dm, dop, common, weights, fronts, lasts):
    vec, geo, cosine, sine = common
    first = lasts is None
    last_out = [jax.ShapeDtypeStruct((MICRO,) + shape, dtype) for _, shape, dtype in LAST_SHAPES]
    operands = [
        scal, dm, dop, vec, geo, cosine, sine, weights[0],
        fronts["qkv"], fronts["e"], fronts["o"], fronts["x"],
    ]
    count = len(operands)
    operands += [] if first else list(lasts)
    scratch = [
        vmem(ROWS, WIDTH, dtype=f32), vmem(ROWS, WIDTH), vmem(1, VEC_AT[-1], dtype=f32), vmem(KEYS, 128, dtype=f32),
        vmem(ROWS, WIDTH, dtype=f32), vmem(ROWS, WIDTH, dtype=f32), vmem(WIDTH, 3 * WIDTH),
        vmem(KEYS, 3 * WIDTH), vmem(HEADS, ROWS, KEYS), vmem(ROWS, WIDTH), vmem(ROWS, WIDTH),
        vmem(WIDTH, ROWS), vmem(WIDTH, ROWS), vmem(ROWS, WIDTH, dtype=f32),
        vmem(WIDTH, KEYS, dtype=f32), vmem(WIDTH, KEYS), vmem(ROWS, 3 * WIDTH), vmem(8, WIDTH, dtype=f32), vmem(ROWS, WIDTH),
        pltpu.SemaphoreType.DMA((16,)),
    ]
    results = pl.pallas_call(
        partial(attention_kernel, first),
        out_shape=[jax.ShapeDtypeStruct((ROWS, WIDTH), bf16)] + last_out,
        in_specs=[pl.BlockSpec(memory_space=pltpu.SMEM)] + [ANY] * (len(operands) - 1),
        out_specs=[ANY] * (1 + len(LASTS)),
        scratch_shapes=scratch,
        input_output_aliases={} if first else {count + i: 1 + i for i in range(len(LASTS))},
        compiler_params=pltpu.CompilerParams(vmem_limit_bytes=VMEM_LIMIT),
        name="attention_back",
    )(*operands)
    return results[0], tuple(results[1:])


def geometry(kind_list):
    row_index = jnp.arange(KEYS, dtype=jnp.int32)[None, :]
    kind_col = kind_list[:, None]
    side_cells = jnp.where(
        kind_col == 0, SIDE_LARGE, jnp.where(kind_col == 1, SIDE_MID, SIDE_SMALL)
    ).astype(jnp.int32)
    image_count = jnp.where(kind_col == 2, 2, 1).astype(jnp.int32)
    image_area = side_cells * side_cells
    image_index = row_index // image_area
    live_rows = (image_index < image_count) & (row_index < ROWS)
    local_index = row_index - image_index * image_area
    patch_row = local_index // side_cells
    patch_col = local_index - patch_row * side_cells
    segment = jnp.where(live_rows, image_index, jnp.where(row_index < ROWS, 3, 2)).astype(f32)
    patch_row = jnp.where(live_rows, patch_row, 0).astype(f32)
    patch_col = jnp.where(live_rows, patch_col, 0).astype(f32)
    return patch_row, patch_col, segment, live_rows.astype(f32)


def tables(kinds, frequency):
    patch_row, patch_col, segment, live = geometry(kinds)
    lane = jnp.arange(128)[None, None, :]
    geo = jnp.where(
        lane == 0, patch_row[..., None], jnp.where(lane == 1, patch_col[..., None], segment[..., None])
    )
    half = WIDTH // 2
    spread = lambda row: jnp.broadcast_to(row.reshape(HEADS, 1, 32), (HEADS, 2, 32)).reshape(1, 1, WIDTH)
    angles = patch_row[:, :ROWS, None] * spread(frequency[:half]) + patch_col[:, :ROWS, None] * spread(frequency[half:])
    sign = jnp.where((jnp.arange(WIDTH) % 64) < 32, -1.0, 1.0)[None, None, :]
    return geo, jnp.cos(angles), jnp.sin(angles) * sign, live[:, :ROWS]


def send(value, source, target):
    return lax.ppermute(value, "section", [(source, target)])


def gathered(part, target, sections):
    section = lax.axis_index("section")
    pieces = []
    for source in range(sections):
        pieces.append(part if source == target else send(part, source, target))
    return jnp.concatenate(pieces, axis=0)


def handed_out(whole, source, sections):
    section = lax.axis_index("section")
    share = whole.shape[0] // sections
    result = whole[source * share : (source + 1) * share]
    for target in range(sections):
        if target != source:
            piece = send(whole[target * share : (target + 1) * share], source, target)
            result = jnp.where(section == target, piece, result)
    return result


def rows_product(left, right):
    left = left.reshape(-1, left.shape[-1])
    right = right.reshape(-1, right.shape[-1])
    return jnp.einsum("rd,re->de", left, right, preferred_element_type=f32).astype(bf16)


def column_sum(values):
    return jnp.sum(values.reshape(-1, values.shape[-1]).astype(f32), axis=0)


def summed_over_images(part):
    own = lax.psum_scatter(part, "dp", scatter_dimension=0, tiled=True)
    return lax.all_gather(own, "dp", axis=0, tiled=True)


SMALL_ROWS = 128


def per_device(
    tokens,
    cotangent,
    image_kind,
    norm_one_gain,
    norm_one_bias,
    qkv_weight,
    qkv_bias,
    rotary_freq,
    proj_weight,
    proj_bias,
    norm_two_gain,
    norm_two_bias,
    up_weight,
    up_bias,
    down_weight,
    down_bias,
):
    sections = lax.axis_size("section")
    section = lax.axis_index("section")
    last = sections - 1
    geo, cosine, sine, live = tables(image_kind, rotary_freq[0])
    vec = jnp.concatenate(
        [
            norm_one_gain[0], norm_one_bias[0], qkv_bias[0], proj_bias[0],
            norm_two_gain[0], norm_two_bias[0], up_bias[0], down_bias[0],
        ]
    )[None]
    common = (vec, geo, cosine, sine)
    weights = (qkv_weight[0], proj_weight[0], up_weight[0], down_weight[0])
    first_in = gathered(tokens, 0, sections)
    last_in = gathered(cotangent, last, sections)
    live_rows = live.reshape(-1, 1)
    last_in = jnp.where(live_rows > 0, last_in, bf16(0.0))

    def scalars(layer, micro):
        return jnp.stack([(section == layer).astype(jnp.int32), jnp.int32(micro)])

    states = None
    values = [first_in[m * ROWS : (m + 1) * ROWS] for m in range(MICRO)]
    for layer in range(sections):
        for micro in range(MICRO):
            out, states = front_call(scalars(layer, micro), values[micro], common, weights, states)
            values[micro] = send(out, layer, layer + 1) if layer < last else out
    final = jnp.where(live_rows > 0, jnp.concatenate(values, axis=0), bf16(0.0))
    block_out = handed_out(final, last, sections)
    fronts = dict(zip(STATES, states))
    backs = lasts = None
    grads = [last_in[m * ROWS : (m + 1) * ROWS] for m in range(MICRO)]
    for layer in reversed(range(sections)):
        for micro in range(MICRO):
            scal = scalars(layer, micro)
            dm, dop, backs = branch_call(scal, grads[micro], vec, weights, fronts, backs)
            dx, lasts = attention_call(scal, dm, dop, common, weights, fronts, lasts)
            grads[micro] = send(dx, layer, layer - 1) if layer > 0 else dx
    grad_tokens = handed_out(jnp.concatenate(grads, axis=0), 0, sections)
    backs = dict(zip(BACKS, backs))
    lasts = dict(zip(LASTS, lasts))
    grad_down = rows_product(fronts["g"], backs["dy"])
    grad_up = rows_product(fronts["c"], backs["du"])
    grad_proj = rows_product(fronts["o"], backs["dz"])
    grad_qkv = rows_product(fronts["a"], lasts["dqkv"])
    one = jnp.sum(lasts["small_one"], axis=0)
    two = jnp.sum(backs["small_two"], axis=0)
    turns = one[2:4].reshape(2, HEADS, 2, 32)
    small = jnp.concatenate(
        [
            one[0], one[1], column_sum(lasts["dqkv"]), (turns[:, :, 1] - turns[:, :, 0]).reshape(-1),
            column_sum(backs["dz"]), two[0], two[1], column_sum(backs["du"]), column_sum(backs["dy"]),
        ]
    )
    small = jnp.pad(small.astype(bf16).reshape(-1, WIDTH), ((0, SMALL_ROWS - small.shape[0] // WIDTH), (0, 0)))
    grad_down = summed_over_images(grad_down).astype(f32)
    grad_up = summed_over_images(grad_up).astype(f32)
    grad_proj = summed_over_images(jnp.concatenate([grad_proj, small], axis=0)).astype(f32)
    grad_qkv = summed_over_images(grad_qkv).astype(f32)
    small = grad_proj[WIDTH:].reshape(-1)
    sizes = (WIDTH, WIDTH, 3 * WIDTH, WIDTH, WIDTH, WIDTH, WIDTH, HIDDEN, WIDTH)
    ends = np.cumsum((0,) + sizes)
    g_one, b_one, b_qkv, freq, b_proj, g_two, b_two, b_up, b_down = (
        small[int(ends[i]) : int(ends[i + 1])][None] for i in range(len(sizes))
    )
    return (
        block_out, grad_tokens.astype(f32), g_one, b_one, grad_qkv[None], b_qkv, freq,
        grad_proj[:WIDTH][None], b_proj, g_two, b_two, grad_up[None], b_up, grad_down[None], b_down,
    )


def solution(mesh):
    row = P(("dp", "section"), None)
    vector = P("section", None)
    matrix = P("section", None, None)
    params = (
        vector, vector, matrix, vector, vector, matrix, vector, vector, vector, matrix, vector, matrix, vector,
    )
    return jax.shard_map(
        per_device,
        mesh=mesh,
        in_specs=(row, row, P("dp")) + params,
        out_specs=(row, row) + params,
        check_vma=False,
    )
```

time: 1640 us -> 779 us (0.47)
  waiting for transfers between devices: 853 us -> 468 us
  other arithmetic: 246 us -> 62.8 us
  matrix products: 184 us -> 28.3 us
  Pallas kernels: 0 us -> 144 us
  local copies, waits for them, and re-layouts: 147 us -> 21.3 us
  blocking collectives: 66 us -> 0 us
  loops' own time: 32.4 us -> 0 us
  starting transfers between devices: 62.3 us -> 30 us
  between operations: 38.6 us -> 15.5 us
    ppermute x8 -> x24, waiting for transfers between devices: 475 us -> 178 us  [send(): return lax.ppermute(value, 'section', [(source, target)])]
    dot_general x44 -> x4, matrix products: 184 us -> 28.3 us  [rows_product(): jnp.einsum('rd,re->de', left, right, preferred_element_type=f32)]
    pallas_call x0 -> x24, Pallas kernels: none -> 144 us  [the longest x8 53.8 us: front_call(): pl.pallas_call(partial(front_kernel, first), out_shape=[jax.ShapeDtypeStr...]
    reduce_scatter x4, waiting for transfers between devices: 242 us -> 159 us  [summed_over_images(): own = lax.psum_scatter(part, 'dp', scatter_dimension=0, tiled=True)]
    add x18 -> x0, other arithmetic: 72.6 us -> none  [the longest x13 63.1 us: per_device(): accum = tuple((total + piece for total, piece in zip(accum, weight_grads)))]
    another operation x58 -> x0, local copies, waits for them, and re-layouts: 60 us -> none
    unnamed x2 -> x0, blocking collectives: 53.1 us -> none
    slice x24 -> x9, local copies, waits for them, and re-layouts: 45.1 us -> 3.54 us  [the longest x1 1.5 us: per_device(): small[int(ends[i]):int(ends[i + 1])][None]]
  transfers between devices with their start and end apart: 20 -> 32, of which waited for: 16 -> 14; matrix products, arithmetic and copies ran while one was open for 15% -> 10% of each run, Pallas kernels for 0% -> 15%
where the time goes in v1:
time: 779 us; the launch traced here: 770 us
  waiting for transfers between devices  468 us (60%)
  Pallas kernels  144 us (18%)
  other arithmetic  62.8 us (8%)
  starting transfers between devices  30 us (4%)
  matrix products  28.3 us (4%)
  local copies, waits for them, and re-layouts  21.3 us (3%)
  between operations  15.5 us (2%)
    ppermute x24, waiting for transfers between devices, send(): return lax.ppermute(value, 'section', [(source, target)])  178 us
    reduce_scatter x4, waiting for transfers between devices, summed_over_images(): own = lax.psum_scatter(part, 'dp', scatter_dimension=0, tiled=True)  159 us
    all_gather x4, waiting for transfers between devices, summed_over_images(): return lax.all_gather(own, 'dp', axis=0, tiled=True)  131 us
    pallas_call x8, Pallas kernels, front_call(): pl.pallas_call(partial(front_kernel, first), out_shape=[jax.ShapeDtypeStr...  53.8 us
    pallas_call x8, Pallas kernels, branch_call(): pl.pallas_call(partial(branch_kernel, first), out_shape=[jax.ShapeDtypeSt...  51.4 us
    pallas_call x8, Pallas kernels, attention_call(): pl.pallas_call(partial(attention_kernel, first), out_shape=[jax.ShapeDtyp...  38.6 us
    ppermute x24, starting transfers between devices, send(): return lax.ppermute(value, 'section', [(source, target)])  29.4 us
    dot_general x4, matrix products, rows_product(): jnp.einsum('rd,re->de', left, right, preferred_element_type=f32)  28.3 us
  transfers between devices with their start and end apart: 32, of which 14 were waited for; matrix products, arithmetic and copies ran while one was open for 10% of the time, Pallas kernels for 15%

profile of v1, /device:TPU:0, one launch (start us, length us, event | category | flops | bytes accessed | tf_op | source)
XLA Modules:
  0.0 770.2 jit_solution(1840101159100090006)
XLA Ops:
  20.9 10.5 %sine_multiply_fusion = (f32[2,400,768]{2,1,0:T(8,128)}, f32[2,400,768]{2,1,0:T(8,128)}) fusion(f32[768]{0:T(1024)S(1)} %fusion.12, f32[768]{0:T(1024)S(1)} %mul.73, f32[2,400]{1,0:T(2,128)S(1)} %bitcast.111, f32[768]{0:T(1024)S(1)} %mul.69, f32[2,400]{1,0:T(2,128)S(1)} %bitcast.110), kind=kLoop, calls=%fused_computation.8 | loop fusion | flops 2457600 | bytes 4930816 | tf_op jit(solution)/shard_map/mul | solution.py:523
  34.2 18.9 %layer_front.8 = (bf16[400,768]{1,0:T(8,128)(2,1)}, bf16[2,400,768]{2,1,0:T(8,128)(2,1)}, bf16[2,400,768]{2,1,0:T(8,128)(2,1)}, bf16[2,400,2304]{2,1,0:T(8,128)(...) custom-call(s32[2]{0:T(128)} %pad_add_fusion.scal, ...), custom_call_target="tpu_custom_call" | custom-call | tf_op jit(solution)/shard_map/layer_front/pallas_call | solution.py:241
  55.3 19.2 %layer_front.9 = (bf16[400,768]{1,0:T(8,128)(2,1)}, bf16[2,400,768]{2,1,0:T(8,128)(2,1)}, bf16[2,400,768]{2,1,0:T(8,128)(2,1)}, bf16[2,400,2304]{2,1,0:T(8,128)(...) custom-call(s32[2]{0:T(128)} %pad_add_fusion.7.scal, ...), custom_call_target="tpu_custom_call", output_to_operand_aliasing={{1}: (10, {}), {2}: (11, {}), {3}: (12, {}), {4}: (13, {}),... | custom-call | tf_op jit(solution)/shard_map/layer_front/pallas_call | solution.py:241
  79.7 10.4 %collective-permute-done.5.refs_0_ = bf16[400,768]{1,0:T(8,128)(2,1)S(1)} collective-permute-done((bf16[400,768]{1,0:T(8,128)(2,1)}, bf16[400,768]{1,0:T(8,128)(2,1)S(1)}, u32[]{:S(2)}, u32[]{:S(2)}) %collective-permute-start.5) | collective-permute-done | bytes 614432 | tf_op jit(solution)/shard_map/ppermute | solution.py:527
  110.2 5.9 layer_front.15
  125.2 5.8 branch_back.9
  163.0 159.1 %collective-permute-done.20.dy_in = bf16[400,768]{1,0:T(8,128)(2,1)S(1)} collective-permute-done((bf16[400,768]{1,0:T(8,128)(2,1)}, bf16[400,768]{1,0:T(8,128)(2,1)S(1)}, u32[]{:S(2)}, u32[]{:S(2)}) %collective-permute-start.20) | collective-permute-done | bytes 614432 | tf_op jit(solution)/shard_map/ppermute | solution.py:527
  322.9 12.4 %branch_back.14 = (f32[400,768]{1,0:T(8,128)}, bf16[400,768]{1,0:T(8,128)(2,1)}, bf16[2,400,3072]{2,1,0:T(8,128)(2,1)}, bf16[2,400,768]{2,1,0:T(8,128)(2,1)}, bf...) custom-call(s32[2]{0:T(128)} %pad_add_fusion.scal, ...), custom_call_target="tpu_custom_call", output_to_operand_aliasing={{2}: (10, {}), {3}: (11, {}), {4}: (12, {}), {5}: (13, {})} | custom-call | tf_op jit(solution)/shard_map/branch_back/pallas_call | solution.py:345
  335.4 16.7 %attention_back.14 = (bf16[400,768]{1,0:T(8,128)(2,1)}, bf16[2,400,2304]{2,1,0:T(8,128)(2,1)}, f32[2,8,768]{2,1,0:T(8,128)}) custom-call(s32[2]{0:T(128)} %pad_add_fusion.scal, f32[400,768]{1,0:T(8,128)} %get-tuple-element.334.dm_in, bf16[400,768]{1,0:T(8,128)(2,1)} %get-tuple-element.335.dop_in, ...), custom_call_target="tpu_custom_call", output_to_operand_aliasing={{1}: (12, {}), {2}: (13, {})} | custom-call | tf_op jit(solution)/shard_map/attention_back/pallas_call | solution.py:481
  354.4 12.5 %branch_back.15 = (f32[400,768]{1,0:T(8,128)}, bf16[400,768]{1,0:T(8,128)(2,1)}, bf16[2,400,3072]{2,1,0:T(8,128)(2,1)}, bf16[2,400,768]{2,1,0:T(8,128)(2,1)}, bf...) custom-call(s32[2]{0:T(128)} %pad_add_fusion.7.scal, ...), custom_call_target="tpu_custom_call", output_to_operand_aliasing={{2}: (10, {}), {3}: (11, {}), {4}: (12, {}), {5}: (13, {})} | custom-call | tf_op jit(solution)/shard_map/branch_back/pallas_call | solution.py:345
  366.9 17.0 %attention_back.15 = (bf16[400,768]{1,0:T(8,128)(2,1)}, bf16[2,400,2304]{2,1,0:T(8,128)(2,1)}, f32[2,8,768]{2,1,0:T(8,128)}) custom-call(s32[2]{0:T(128)} %pad_add_fusion.7.scal, f32[400,768]{1,0:T(8,128)} %get-tuple-element.332.dm_in, bf16[400,768]{1,0:T(8,128)(2,1)} %get-tuple-element.333.dop_in, ...), custom_call_target="tpu_custom_call", output_to_operand_aliasing={{1}: (12, {}), {2}: (13, {})} | custom-call | tf_op jit(solution)/shard_map/attention_back/pallas_call | solution.py:481
  398.5 7.4 bitcast_convert_fusion.2
  406.0 9.3 %bitcast_convert_fusion = bf16[3072,768]{1,0:T(8,128)(2,1)} fusion(bf16[2,400,3072]{2,1,0:T(8,128)(2,1)} %get-tuple-element.350, bf16[2,400,768]{2,1,0:T(8,128)(2,1)S(1)} %copy-done.2), kind=kOutput, calls=%fused_computation | convolution fusion | flops 3777232896 | bytes 10862592 | tf_op jit(solution)/shard_map/rd,re->de/dot_general | solution.py:552
  416.6 9.1 %bitcast_convert_fusion.1 = bf16[768,3072]{1,0:T(8,128)(2,1)} fusion(bf16[2,400,768]{2,1,0:T(8,128)(2,1)S(1)} %copy-done.4, bf16[2,400,3072]{2,1,0:T(8,128)(2,1)} %get-tuple-element.346), kind=kOutput, calls=%fused_computation.1 | convolution fusion | flops 3777232896 | bytes 10862592 | tf_op jit(solution)/shard_map/rd,re->de/dot_general | solution.py:552
  428.0 44.4 %reduce-scatter.7.cloned.1.call-done = bf16[96,2304]{1,0:T(8,128)(2,1)} async-done(((bf16[768,2304]{1,0:T(8,128)(2,1)}), bf16[96,2304]{1,0:T(8,128)(2,1)}) %reduce-scatter.7.cloned.1.call-update) | async-done | bytes 442384 | tf_op jit(solution)/shard_map/reduce_scatter | solution.py:560
  472.4 56.3 %reduce-scatter.11.cloned.1.call-done = bf16[384,768]{1,0:T(8,128)(2,1)} async-done(((bf16[3072,768]{1,0:T(8,128)(2,1)}), bf16[384,768]{1,0:T(8,128)(2,1)}) %reduce-scatter.11.cloned.1.call-update) | async-done | bytes 589840 | tf_op jit(solution)/shard_map/reduce_scatter | solution.py:560
  528.8 56.0 %reduce-scatter.9.cloned.1.call-done = bf16[96,3072]{1,0:T(8,128)(2,1)} async-done(((bf16[768,3072]{1,0:T(8,128)(2,1)}), bf16[96,3072]{1,0:T(8,128)(2,1)}) %reduce-scatter.9.cloned.1.call-update) | async-done | bytes 589840 | tf_op jit(solution)/shard_map/reduce_scatter | solution.py:560
  587.7 6.8 collective-permute-start.21
  614.6 36.5 %all-gather.7.cloned.1.call-done = bf16[768,2304]{1,0:T(8,128)(2,1)} async-done(((bf16[96,2304]{1,0:T(8,128)(2,1)}), bf16[768,2304]{1,0:T(8,128)(2,1)}) %all-gather.7.cloned.1.call-update) | async-done | bytes 3538960 | tf_op jit(solution)/shard_map/all_gather | solution.py:561
  651.0 5.5 bitcast_convert_fusion.5
  656.5 46.8 %all-gather.11.cloned.1.call-done = bf16[3072,768]{1,0:T(8,128)(2,1)} async-done(((bf16[384,768]{1,0:T(8,128)(2,1)}), bf16[3072,768]{1,0:T(8,128)(2,1)}) %all-gather.11.cloned.1.call-update) | async-done | bytes 4718608 | tf_op jit(solution)/shard_map/all_gather | solution.py:561
  703.3 6.8 bitcast_convert_fusion.3
  710.1 45.4 %all-gather.9.cloned.1.call-done = bf16[768,3072]{1,0:T(8,128)(2,1)} async-done(((bf16[96,3072]{1,0:T(8,128)(2,1)}), bf16[768,3072]{1,0:T(8,128)(2,1)}) %all-gather.9.cloned.1.call-update) | async-done | bytes 4718608 | tf_op jit(solution)/shard_map/all_gather | solution.py:561
  755.5 7.4 bitcast_convert_fusion.4
  (212 shorter events, 128.5 us)
Async XLA Ops:
  7.2 420.7 %reduce-scatter.5.cloned.1.call-start = ((), (), s32[]{:S(2)}) async-start(), calls=%async_computation.4 | async-start | bytes 1548288 | tf_op jit(solution)/shard_map/reduce_scatter | solution.py:560
  7.2 26.1 %collective-permute-start = (bf16[200,768]{1,0:T(8,128)(2,1)}, bf16[200,768]{1,0:T(8,128)(2,1)S(1)}, u32[]{:S(2)}, u32[]{:S(2)}) collective-permute-start(bf16[200,768]{1,0:T(8,128)(2,1)} %param.16), channel_id=1, source_target_pairs={{8,0},{9,1},{10,2},{11,3},{12,4},{13,5},{14,6},{15,7}} | collective-permute-start | bytes 921608 | tf_op jit(solution)/shard_map/ppermute | solution.py:527
  8.5 45.9 %collective-permute-start.2 = (bf16[200,768]{1,0:T(8,128)(2,1)}, bf16[200,768]{1,0:T(8,128)(2,1)S(1)}, u32[]{:S(2)}, u32[]{:S(2)}) collective-permute-start(bf16[200,768]{1,0:T(8,128)(2,1)} %param.16), channel_id=1, source_target_pairs={{16,0},{17,1},{18,2},{19,3},{20,4},{21,5},{22,6},{23,7}} | collective-permute-start | bytes 921608 | tf_op jit(solution)/shard_map/ppermute | solution.py:527
  9.8 44.6 %collective-permute-start.3 = (bf16[200,768]{1,0:T(8,128)(2,1)}, bf16[200,768]{1,0:T(8,128)(2,1)S(1)}, u32[]{:S(2)}, u32[]{:S(2)}) collective-permute-start(bf16[200,768]{1,0:T(8,128)(2,1)} %param.16), channel_id=1, source_target_pairs={{24,0},{25,1},{26,2},{27,3},{28,4},{29,5},{30,6},{31,7}} | collective-permute-start | bytes 921608 | tf_op jit(solution)/shard_map/ppermute | solution.py:527
  53.1 23.9 %collective-permute-start.1 = (bf16[400,768]{1,0:T(8,128)(2,1)}, bf16[400,768]{1,0:T(8,128)(2,1)S(1)}, u32[]{:S(2)}, u32[]{:S(2)}) collective-permute-start(bf16[400,768]{1,0:T(8,128)(2,1)} %get-tuple-element.183), channel_id=1, source_target_pairs={{0,8},{1,9},{2,10},{3,11},{4,12},{5,13},{6,14},{7,15}} | collective-permute-start | bytes 1843208 | tf_op jit(solution)/shard_map/ppermute | solution.py:527
  74.5 15.6 %collective-permute-start.5 = (bf16[400,768]{1,0:T(8,128)(2,1)}, bf16[400,768]{1,0:T(8,128)(2,1)S(1)}, u32[]{:S(2)}, u32[]{:S(2)}) collective-permute-start(bf16[400,768]{1,0:T(8,128)(2,1)} %get-tuple-element.207), channel_id=1, source_target_pairs={{0,8},{1,9},{2,10},{3,11},{4,12},{5,13},{6,14},{7,15}} | collective-permute-start | bytes 1843208 | tf_op jit(solution)/shard_map/ppermute | solution.py:527
  79.0 15.2 %collective-permute-start.4 = (bf16[400,768]{1,0:T(8,128)(2,1)}, bf16[400,768]{1,0:T(8,128)(2,1)S(1)}, u32[]{:S(2)}, u32[]{:S(2)}) collective-permute-start(bf16[400,768]{1,0:T(8,128)(2,1)} %get-tuple-element.206), channel_id=1, source_target_pairs={{8,16},{9,17},{10,18},{11,19},{12,20},{13,21},{14,22},{15,23}} | collective-permute-start | bytes 1843208 | tf_op jit(solution)/shard_map/ppermute | solution.py:527
  97.4 10.0 %collective-permute-start.6 = (bf16[400,768]{1,0:T(8,128)(2,1)}, bf16[400,768]{1,0:T(8,128)(2,1)S(1)}, u32[]{:S(2)}, u32[]{:S(2)}) collective-permute-start(bf16[400,768]{1,0:T(8,128)(2,1)} %get-tuple-element.230), channel_id=1, source_target_pairs={{16,24},{17,25},{18,26},{19,27},{20,28},{21,29},{22,30},{23,31}} | collective-permute-start | bytes 1843208 | tf_op jit(solution)/shard_map/ppermute | solution.py:527
  103.4 12.7 %collective-permute-start.12 = (bf16[200,768]{1,0:T(8,128)(2,1)S(1)}, bf16[200,768]{1,0:T(8,128)(2,1)S(1)}, u32[]{:S(2)}, u32[]{:S(2)}) collective-permute-start(bf16[200,768]{1,0:T(8,128)(2,1)S(1)} %copy-done.23), channel_id=1, source_target_pairs={{0,24},{1,25},{2,26},{3,27},{4,28},{5,29},{6,30},{7,31}} | collective-permute-start | bytes 921608 | tf_op jit(solution)/shard_map/ppermute | solution.py:527
  104.7 11.4 %collective-permute-start.13 = (bf16[200,768]{1,0:T(8,128)(2,1)S(1)}, bf16[200,768]{1,0:T(8,128)(2,1)S(1)}, u32[]{:S(2)}, u32[]{:S(2)}) collective-permute-start(bf16[200,768]{1,0:T(8,128)(2,1)S(1)} %copy-done.23), channel_id=1, source_target_pairs={{8,24},{9,25},{10,26},{11,27},{12,28},{13,29},{14,30},{15,31}} | collective-permute-start | bytes 921608 | tf_op jit(solution)/shard_map/ppermute | solution.py:527
  105.4 10.8 %collective-permute-start.14 = (bf16[200,768]{1,0:T(8,128)(2,1)S(1)}, bf16[200,768]{1,0:T(8,128)(2,1)S(1)}, u32[]{:S(2)}, u32[]{:S(2)}) collective-permute-start(bf16[200,768]{1,0:T(8,128)(2,1)S(1)} %copy-done.23), channel_id=1, source_target_pairs={{16,24},{17,25},{18,26},{19,27},{20,28},{21,29},{22,30},{23,31}} | collective-permute-start | bytes 921608 | tf_op jit(solution)/shard_map/ppermute | solution.py:527
  154.1 168.0 %collective-permute-start.20 = (bf16[400,768]{1,0:T(8,128)(2,1)}, bf16[400,768]{1,0:T(8,128)(2,1)S(1)}, u32[]{:S(2)}, u32[]{:S(2)}) collective-permute-start(bf16[400,768]{1,0:T(8,128)(2,1)} %get-tuple-element.323), channel_id=1, source_target_pairs={{8,0},{9,1},{10,2},{11,3},{12,4},{13,5},{14,6},{15,7}} | collective-permute-start | bytes 1843208 | tf_op jit(solution)/shard_map/ppermute | solution.py:527
  161.7 191.9 %collective-permute-start.19 = (bf16[400,768]{1,0:T(8,128)(2,1)}, bf16[400,768]{1,0:T(8,128)(2,1)S(1)}, u32[]{:S(2)}, u32[]{:S(2)}) collective-permute-start(bf16[400,768]{1,0:T(8,128)(2,1)} %get-tuple-element.322), channel_id=1, source_target_pairs={{8,0},{9,1},{10,2},{11,3},{12,4},{13,5},{14,6},{15,7}} | collective-permute-start | bytes 1843208 | tf_op jit(solution)/shard_map/ppermute | solution.py:527
  398.5 73.9 %reduce-scatter.7.cloned.1.call-start = ((), (), s32[]{:S(2)}) async-start(), calls=%async_computation.6 | async-start | bytes 3981312 | tf_op jit(solution)/shard_map/reduce_scatter | solution.py:560
  406.0 122.8 %reduce-scatter.11.cloned.1.call-start = ((), (), s32[]{:S(2)}) async-start(), calls=%async_computation.10 | async-start | bytes 5308416 | tf_op jit(solution)/shard_map/reduce_scatter | solution.py:560
  415.4 169.5 %reduce-scatter.9.cloned.1.call-start = ((), (), s32[]{:S(2)}) async-start(), calls=%async_computation.8 | async-start | bytes 5308416 | tf_op jit(solution)/shard_map/reduce_scatter | solution.py:560
  425.8 182.9 %all-gather.5.cloned.1.call-start = ((), (), s32[]{:S(2)}) async-start(), calls=%async_computation.5 | async-start | bytes 1548288 | tf_op jit(solution)/shard_map/all_gather | solution.py:561
  427.9 223.1 %all-gather.7.cloned.1.call-start = ((), (), s32[]{:S(2)}) async-start(), calls=%async_computation.7 | async-start | bytes 3981312 | tf_op jit(solution)/shard_map/all_gather | solution.py:561
  472.4 230.9 %all-gather.11.cloned.1.call-start = ((), (), s32[]{:S(2)}) async-start(), calls=%async_computation.11 | async-start | bytes 5308416 | tf_op jit(solution)/shard_map/all_gather | solution.py:561
  528.8 226.7 %all-gather.9.cloned.1.call-start = ((), (), s32[]{:S(2)}) async-start(), calls=%async_computation.9 | async-start | bytes 5308416 | tf_op jit(solution)/shard_map/all_gather | solution.py:561
  584.9 10.9 %collective-permute-start.10 = (bf16[200,768]{1,0:T(8,128)(2,1)S(1)}, bf16[200,768]{1,0:T(8,128)(2,1)S(1)}, u32[]{:S(2)}, u32[]{:S(2)}) collective-permute-start(bf16[200,768]{1,0:T(8,128)(2,1)S(1)} %get-tuple-element.371), channel_id=1, source_target_pairs={{24,8},{25,9},{26,10},{27,11},{28,12},{29,13},{30,14},{31,15}} | collective-permute-start | bytes 921608 | tf_op jit(solution)/shard_map/ppermute | solution.py:527
  585.6 13.6 %collective-permute-start.11 = (bf16[200,768]{1,0:T(8,128)(2,1)S(1)}, bf16[200,768]{1,0:T(8,128)(2,1)S(1)}, u32[]{:S(2)}, u32[]{:S(2)}) collective-permute-start(bf16[200,768]{1,0:T(8,128)(2,1)S(1)} %get-tuple-element.370), channel_id=1, source_target_pairs={{24,0},{25,1},{26,2},{27,3},{28,4},{29,5},{30,6},{31,7}} | collective-permute-start | bytes 921608 | tf_op jit(solution)/shard_map/ppermute | solution.py:527
  586.9 12.3 %collective-permute-start.9 = (bf16[200,768]{1,0:T(8,128)(2,1)S(1)}, bf16[200,768]{1,0:T(8,128)(2,1)S(1)}, u32[]{:S(2)}, u32[]{:S(2)}) collective-permute-start(bf16[200,768]{1,0:T(8,128)(2,1)S(1)} %get-tuple-element.372), channel_id=1, source_target_pairs={{24,16},{25,17},{26,18},{27,19},{28,20},{29,21},{30,22},{31,23}} | collective-permute-start | bytes 921608 | tf_op jit(solution)/shard_map/ppermute | solution.py:527
  587.7 14.1 %collective-permute-start.21 = (bf16[200,768]{1,0:T(8,128)(2,1)S(1)}, bf16[200,768]{1,0:T(8,128)(2,1)S(1)}, u32[]{:S(2)}, u32[]{:S(2)}) collective-permute-start(bf16[200,768]{1,0:T(8,128)(2,1)S(1)} %get-tuple-element.374), channel_id=1, source_target_pairs={{0,24},{1,25},{2,26},{3,27},{4,28},{5,29},{6,30},{7,31}} | collective-permute-start | bytes 921608 | tf_op jit(solution)/shard_map/ppermute | solution.py:527
  (32 other events, 634.1 us)
Sparse Core Ops, SparseCore 0:
  398.6 29.2 reduce-scatter.4
  430.4 41.9 reduce-scatter.6
  475.2 53.4 reduce-scatter.10
  531.5 53.2 reduce-scatter.8
  586.3 22.3 all-gather.4
  610.2 40.7 all-gather.6
  652.7 50.5 all-gather.10
  704.9 50.5 all-gather.8

commit v2 on v1

v2 whole, which is shorter than its diff:
```python
from functools import partial
import math

import jax
import jax.numpy as jnp
import numpy as np
from jax import lax
from jax.experimental import pallas as pl
from jax.experimental.pallas import tpu as pltpu
from jax.sharding import PartitionSpec as P

HEADS = 12
SIDE_LARGE = 20
SIDE_MID = 16
SIDE_SMALL = 14
MICRO = 2
ROWS = 400
KEYS = 512
WIDTH = 768
HIDDEN = 3072
PAIRS = HEADS // 2
EPSILON = 1e-06
MASKED = -1e30
LOG2E = math.log2(math.e)
LN2 = math.log(2.0)
GELU_ONE = math.sqrt(2.0 / math.pi)
GELU_TWO = GELU_ONE * 0.044715

f32 = jnp.float32
bf16 = jnp.bfloat16
NT = (((1,), (1,)), ((), ()))
TN = (((0,), (0,)), ((), ()))

VEC_SIZES = (WIDTH, WIDTH, 3 * WIDTH, WIDTH, WIDTH, WIDTH, HIDDEN, WIDTH)
VEC_AT = tuple(int(v) for v in np.cumsum((0,) + VEC_SIZES))


def vec_part(vec_ref, index):
    return vec_ref[:, VEC_AT[index] : VEC_AT[index + 1]]


def swap_halves(values):
    lane = lax.broadcasted_iota(jnp.int32, values.shape, 1) % 64
    width = values.shape[1]
    return jnp.where(lane < 32, pltpu.roll(values, width - 32, 1), pltpu.roll(values, 32, 1))


def norm_parts(values):
    center = values - jnp.mean(values, axis=-1, keepdims=True)
    inverse = lax.rsqrt(jnp.mean(center * center, axis=-1, keepdims=True) + EPSILON)
    return center * inverse, inverse


def gelu_parts(pre):
    low = pre.astype(bf16)
    square = low * low
    tanh = jnp.tanh(low * (bf16(GELU_ONE) + bf16(GELU_TWO) * square))
    half = bf16(0.5) + bf16(0.5) * tanh
    value = low * half
    slope = half + (value - value * half) * (bf16(2 * GELU_ONE) + bf16(6 * GELU_TWO) * square)
    return value, slope


class Copies:
    def __init__(self, sems):
        self.sems = sems
        self.open = []
        self.used = 0

    def start(self, source, target):
        copy = pltpu.make_async_copy(source, target, self.sems.at[self.used])
        self.used += 1
        copy.start()
        self.open.append(copy)
        return copy

    def wait(self, *copies):
        for copy in copies:
            self.open = [other for other in self.open if other is not copy]
            copy.wait()

    def finish(self):
        self.wait(*list(self.open))


STATE_SHAPES = (
    ("x", (ROWS, WIDTH), bf16),
    ("a", (ROWS, WIDTH), bf16),
    ("qkv", (ROWS, 3 * WIDTH), bf16),
    ("e", (HEADS, ROWS, KEYS), bf16),
    ("linv", (ROWS, WIDTH), f32),
    ("o", (ROWS, WIDTH), bf16),
    ("n2", (ROWS, WIDTH), bf16),
    ("r2", (ROWS, 128), f32),
    ("c", (ROWS, WIDTH), bf16),
    ("g", (ROWS, HIDDEN), bf16),
    ("gp", (ROWS, HIDDEN), bf16),
)
STATES = tuple(name for name, _, _ in STATE_SHAPES)


def front_kernel(first, scal, layer, *refs):
    x_in, geo_in, cos_in, sin_in, wqkv_in, wp_in, wu_in, wd_in = refs[:8]
    vec_in, rest = refs[8:16], refs[16:]
    if not first:
        rest = rest[len(STATES) :]
    out_ref = rest[0]
    state = dict(zip(STATES, rest[1 : 1 + len(STATES)]))
    (
        x_v, vec_v, geo_v, cos_v, sin_v, wqkv_v, wp_v, wu_v, wd_v,
        a_v, qkv_v, e_v, s_v, li_v, o_v, m_v, n2_v, r2_v, c_v, g_v, gp_v, qcode_v, kcode_v, out_v, sems,
    ) = rest[1 + len(STATES) :]

    @pl.when(scal[0] == layer[0])
    def _():
        slot = layer[1]
        copies = Copies(sems)
        wait = copies.wait
        get_x = copies.start(x_in, x_v)
        get_vec = [
            copies.start(part, vec_v.at[:, pl.ds(at, size)]) for part, at, size in zip(vec_in, VEC_AT, VEC_SIZES)
        ]
        get_geo = copies.start(geo_in.at[slot], geo_v)
        get_qkv = [
            copies.start(wqkv_in.at[:, pl.ds(at, WIDTH)], wqkv_v.at[:, pl.ds(at, WIDTH)])
            for at in range(0, 3 * WIDTH, WIDTH)
        ]
        get_cos = copies.start(cos_in.at[slot], cos_v)
        get_sin = copies.start(sin_in.at[slot], sin_v)

        def put(source, name):
            copies.start(source, state[name].at[slot])

        qkv_v[ROWS:KEYS, :] = jnp.zeros((KEYS - ROWS, 3 * WIDTH), bf16)
        wait(get_x, get_geo, *get_vec)
        normed, _ = norm_parts(x_v[...].astype(f32))
        a_v[...] = (normed * vec_part(vec_v, 0) + vec_part(vec_v, 1)).astype(bf16)
        segment = geo_v[:, 2:3]
        code = (lax.broadcasted_iota(jnp.int32, (KEYS, 128), 1) % 64).astype(f32)
        qcode_v[...] = jnp.where(segment[:ROWS] == code[:ROWS], 1.0, 0.0).astype(bf16)
        kcode_v[...] = jnp.where((segment != code) & (code < 4), MASKED, 0.0).astype(bf16)
        for part in range(3):
            at = part * WIDTH
            wait(get_qkv[part])
            if part == 0:
                wait(get_cos, get_sin)
                get_wp = copies.start(wp_in, wp_v)
                get_wu = copies.start(wu_in, wu_v)
                get_wd = copies.start(wd_in, wd_v)
            acc = jnp.dot(a_v[...], wqkv_v[:, at : at + WIDTH], preferred_element_type=f32)
            acc = acc + vec_v[:, VEC_AT[2] + at : VEC_AT[2] + at + WIDTH]
            if part < 2:
                acc = acc * cos_v[...] + swap_halves(acc) * sin_v[...]
            if part == 0:
                acc = acc * (LOG2E / 8.0)
            qkv_v[:ROWS, at : at + WIDTH] = acc.astype(bf16)

        for pair in range(PAIRS):
            lanes = pl.ds(pair * 128, 128)
            klanes = pl.ds(pair * 128 + WIDTH, 128)
            vlanes = pl.ds(pair * 128 + 2 * WIDTH, 128)
            q_two = qkv_v[:ROWS, lanes]
            k_two = qkv_v[:, klanes]
            v_two = qkv_v[:, vlanes]
            lane_q = lax.broadcasted_iota(jnp.int32, (ROWS, 128), 1) // 64
            lane_k = lax.broadcasted_iota(jnp.int32, (KEYS, 128), 1) // 64
            for head in range(2):
                q_one = jnp.where(lane_q == head, q_two, qcode_v[...])
                k_one = jnp.where(lane_k == head, k_two, kcode_v[...])
                s_v[2 * (pair % 2) + head] = lax.dot_general(q_one, k_one, NT, preferred_element_type=f32)
            sums = []
            for head in range(2):
                v_one = jnp.where(lane_k == head, v_two, bf16(1.0))
                scores = s_v[2 * (pair % 2) + head]
                peak = jnp.max(scores, axis=1, keepdims=True)
                e_v[2 * pair + head] = jnp.exp2(scores - peak).astype(bf16)
                sums.append(jnp.dot(e_v[2 * pair + head], v_one, preferred_element_type=f32))
            total = pltpu.roll(jnp.where(lane_q == 0, sums[1], sums[0]), 64, 1)
            inverse = 1.0 / total
            li_v[:, lanes] = inverse
            o_v[:, lanes] = (jnp.where(lane_q == 0, sums[0], sums[1]) * inverse).astype(bf16)
        put(x_v, "x")
        put(a_v, "a")
        put(qkv_v.at[pl.ds(0, ROWS)], "qkv")
        put(e_v, "e")
        put(li_v, "linv")
        put(o_v, "o")
        wait(get_wp)
        middle = (
            x_v[...].astype(f32)
            + jnp.dot(o_v[...], wp_v[...], preferred_element_type=f32)
            + vec_part(vec_v, 3)
        )
        m_v[...] = middle
        normed, inverse = norm_parts(middle)
        n2_v[...] = normed.astype(bf16)
        r2_v[...] = jnp.broadcast_to(inverse, (ROWS, 128))
        c_v[...] = (normed * vec_part(vec_v, 4) + vec_part(vec_v, 5)).astype(bf16)
        put(n2_v, "n2")
        put(r2_v, "r2")
        put(c_v, "c")
        wait(get_wu)
        chunk = 1024

        def up_step(step, carry):
            lanes = pl.ds(pl.multiple_of(step * chunk, chunk), chunk)
            blanes = pl.ds(pl.multiple_of(step * chunk + VEC_AT[6], 128), chunk)
            pre = jnp.dot(c_v[...], wu_v[:, lanes], preferred_element_type=f32) + vec_v[:, blanes]
            value, slope = gelu_parts(pre)
            g_v[:, lanes] = value
            gp_v[:, lanes] = slope
            return carry

        lax.fori_loop(0, HIDDEN // chunk, up_step, 0)
        put(gp_v, "gp")
        put(g_v, "g")
        wait(get_wd)
        for at in range(0, WIDTH, 256):
            part = pl.ds(at, 256)
            out = jnp.dot(g_v[...], wd_v[:, part], preferred_element_type=f32)
            out = out + m_v[:, part] + vec_v[:, VEC_AT[7] + at : VEC_AT[7] + at + 256]
            out_v[:, part] = out.astype(bf16)
            copies.start(out_v.at[:, part], out_ref.at[:, part])
        copies.finish()


ANY = pl.BlockSpec(memory_space=pl.ANY)
VMEM_LIMIT = 60 * 2**20


def vmem(*shape, dtype=bf16):
    return pltpu.VMEM(shape, dtype)


def call_states(kernel, first, operands, smem, states, plain_out, shapes, scratch, name):
    count = len(operands)
    state_out = [jax.ShapeDtypeStruct((MICRO,) + shape, dtype) for _, shape, dtype in shapes]
    operands = list(operands) + ([] if first else list(states))
    results = pl.pallas_call(
        partial(kernel, first),
        out_shape=list(plain_out) + state_out,
        in_specs=[pl.BlockSpec(memory_space=pltpu.SMEM)] * smem + [ANY] * (len(operands) - smem),
        out_specs=[ANY] * (len(plain_out) + len(shapes)),
        scratch_shapes=scratch,
        input_output_aliases={} if first else {count + i: len(plain_out) + i for i in range(len(shapes))},
        compiler_params=pltpu.CompilerParams(vmem_limit_bytes=VMEM_LIMIT),
        name=name,
    )(*operands)
    return results[0], tuple(results[1:])


def front_call(scal, layer, x, common, weights, vecs, states):
    scratch = [
        vmem(ROWS, WIDTH), vmem(1, VEC_AT[-1], dtype=f32), vmem(KEYS, 128, dtype=f32),
        vmem(ROWS, WIDTH, dtype=f32), vmem(ROWS, WIDTH, dtype=f32),
        vmem(WIDTH, 3 * WIDTH), vmem(WIDTH, WIDTH), vmem(WIDTH, HIDDEN), vmem(HIDDEN, WIDTH),
        vmem(ROWS, WIDTH), vmem(KEYS, 3 * WIDTH), vmem(HEADS, ROWS, KEYS), vmem(4, ROWS, KEYS, dtype=f32),
        vmem(ROWS, WIDTH, dtype=f32), vmem(ROWS, WIDTH), vmem(ROWS, WIDTH, dtype=f32),
        vmem(ROWS, WIDTH), vmem(ROWS, 128, dtype=f32), vmem(ROWS, WIDTH),
        vmem(ROWS, HIDDEN), vmem(ROWS, HIDDEN), vmem(ROWS, 128), vmem(KEYS, 128), vmem(ROWS, WIDTH),
        pltpu.SemaphoreType.DMA((36,)),
    ]
    operands = [scal, layer, x, *common, *weights, *vecs]
    out = jax.ShapeDtypeStruct((ROWS, WIDTH), bf16)
    return call_states(front_kernel, states is None, operands, 2, states, [out], STATE_SHAPES, scratch, "layer_front")


BACK_SHAPES = (
    ("du", (ROWS, HIDDEN), bf16),
    ("dz", (ROWS, WIDTH), bf16),
    ("dqkv", (ROWS, 3 * WIDTH), bf16),
    ("small", (8, WIDTH), f32),
)
BACKS = tuple(name for name, _, _ in BACK_SHAPES)


def back_kernel(first, scal, layer, *refs):
    dy_in, geo_in, cos_in, sin_in, wqkv_in, wp_in, wu_in, wd_in, gain_one_in, gain_two_in = refs[:10]
    saved = dict(zip(KEPT, refs[10 : 10 + len(KEPT)]))
    rest = refs[10 + len(KEPT) :]
    if not first:
        rest = rest[len(BACKS) :]
    dx_ref = rest[0]
    state = dict(zip(BACKS, rest[1 : 1 + len(BACKS)]))
    (
        dy_v, geo_v, cos_v, sin_v, wqkv_v, wp_v, wu_v, wd_v, gains_v,
        gp_v, n2_v, r2_v, li_v, qkv_v, e_v, o_v, x_v,
        du_v, dz_v, dm_v, dop_v, qt_v, dot_v, dq_v, dkt_v, dvt_v, dqkv_v, small_v, dx_v, sems,
    ) = rest[1 + len(BACKS) :]

    @pl.when(scal[0] == layer[0])
    def _():
        slot = layer[1]
        copies = Copies(sems)
        wait = copies.wait
        chunk = 1024
        steps = HIDDEN // chunk
        get_dy = copies.start(dy_in, dy_v)
        get_wd, get_gp = [], []
        for step in range(steps):
            part = pl.ds(step * chunk, chunk)
            get_wd.append(copies.start(wd_in.at[part], wd_v.at[part]))
            get_gp.append(copies.start(saved["gp"].at[slot, :, part], gp_v.at[:, part]))
        get_wu = copies.start(wu_in, wu_v)
        get_norm = [
            copies.start(saved["n2"].at[slot], n2_v),
            copies.start(saved["r2"].at[slot], r2_v),
            copies.start(gain_one_in, gains_v.at[pl.ds(0, 1)]),
            copies.start(gain_two_in, gains_v.at[pl.ds(8, 1)]),
        ]

        def put(source, name):
            copies.start(source, state[name].at[slot])

        qkv_v[ROWS:KEYS, :] = jnp.zeros((KEYS - ROWS, 3 * WIDTH), bf16)
        wait(get_dy)
        for step in range(steps):
            part = slice(step * chunk, (step + 1) * chunk)
            wait(get_wd[step], get_gp[step])
            act = lax.dot_general(dy_v[...], wd_v[part, :], NT, preferred_element_type=f32)
            du_v[:, part] = act.astype(bf16) * gp_v[:, part]
        get_wp = copies.start(wp_in, wp_v)
        get_li = copies.start(saved["linv"].at[slot], li_v)
        get_qkv = copies.start(saved["qkv"].at[slot], qkv_v.at[pl.ds(0, ROWS)])
        get_o = copies.start(saved["o"].at[slot], o_v)
        get_e = copies.start(saved["e"].at[slot], e_v)
        get_turn = [
            copies.start(cos_in.at[slot], cos_v),
            copies.start(sin_in.at[slot], sin_v),
            copies.start(geo_in.at[slot], geo_v),
        ]
        get_x = copies.start(saved["x"].at[slot], x_v)
        get_wqkv = copies.start(wqkv_in, wqkv_v)
        put(du_v, "du")
        wait(get_wu)
        dc = lax.dot_general(du_v[...], wu_v[...], NT, preferred_element_type=f32)
        wait(*get_norm)
        normed = n2_v[...].astype(f32)
        small_v[0:1, :] = jnp.sum(dc * normed, axis=0, keepdims=True)
        small_v[1:2, :] = jnp.sum(dc, axis=0, keepdims=True)
        hat = dc * gains_v[8:9, :]
        dm = dy_v[...].astype(f32) + r2_v[:, 0:1] * (
            hat
            - jnp.mean(hat, axis=-1, keepdims=True)
            - normed * jnp.mean(hat * normed, axis=-1, keepdims=True)
        )
        dm_v[...] = dm
        dz_v[...] = dm.astype(bf16)
        put(dz_v, "dz")
        wait(get_wp, get_li)
        do = lax.dot_general(dz_v[...], wp_v[...], NT, preferred_element_type=f32)
        dop_v[...] = (do * li_v[...]).astype(bf16)
        dot_v[...] = dop_v[...].T
        wait(get_qkv)
        qt_v[...] = qkv_v[:ROWS, :WIDTH].T
        wait(get_o, get_e)

        def pair_step(step, carry):
            for pair in [step * 2 + i for i in range(2)]:
                lanes = pl.ds(pl.multiple_of(pair * 128, 128), 128)
                klanes = pl.ds(pl.multiple_of(pair * 128 + WIDTH, 128), 128)
                vlanes = pl.ds(pl.multiple_of(pair * 128 + 2 * WIDTH, 128), 128)
                do_two = dop_v[:, lanes]
                k_two = qkv_v[:, klanes]
                v_two = qkv_v[:, vlanes]
                prod = do_two.astype(f32) * o_v[:, lanes].astype(f32)
                lane = lax.broadcasted_iota(jnp.int32, (ROWS, 128), 1) // 64
                dqs = []
                for head in range(2):
                    rows = pl.ds(pl.multiple_of(pair * 128 + head * 64, 64), 64)
                    do_one = jnp.where(lane == head, do_two, bf16(0.0))
                    dp = lax.dot_general(do_one, v_two, NT, preferred_element_type=f32)
                    delta = jnp.sum(jnp.where(lane == head, prod, 0.0), axis=1, keepdims=True)
                    probs = e_v[2 * pair + head]
                    ds = probs * (dp - delta).astype(bf16)
                    dqs.append(jnp.dot(ds, k_two, preferred_element_type=f32))
                    dkt_v[rows, :] = jnp.dot(qt_v[rows, :], ds, preferred_element_type=f32)
                    dvt_v[rows, :] = jnp.dot(dot_v[rows, :], probs, preferred_element_type=f32).astype(bf16)
                dq_v[:, lanes] = jnp.where(lane == 0, dqs[0], dqs[1])
            return carry

        lax.fori_loop(0, PAIRS // 2, pair_step, 0)
        wait(*get_turn)
        dqkv_v[:, 2 * WIDTH :] = dvt_v[...].T[:ROWS]
        dk = dkt_v[...].T[:ROWS]
        dq = dq_v[...]
        turn = dq * swap_halves(qkv_v[:ROWS, :WIDTH].astype(f32)) + dk * swap_halves(
            qkv_v[:ROWS, WIDTH : 2 * WIDTH].astype(f32)
        )
        small_v[4:5, :] = LN2 * jnp.sum(turn * geo_v[:ROWS, 0:1], axis=0, keepdims=True)
        small_v[5:6, :] = LN2 * jnp.sum(turn * geo_v[:ROWS, 1:2], axis=0, keepdims=True)
        dqkv_v[:, :WIDTH] = (0.125 * (dq * cos_v[...] - swap_halves(dq) * sin_v[...])).astype(bf16)
        dqkv_v[:, WIDTH : 2 * WIDTH] = (LN2 * (dk * cos_v[...] - swap_halves(dk) * sin_v[...])).astype(bf16)
        put(dqkv_v, "dqkv")
        wait(get_x)
        normed, inverse = norm_parts(x_v[...].astype(f32))
        wait(get_wqkv)
        da = lax.dot_general(dqkv_v[...], wqkv_v[...], NT, preferred_element_type=f32)
        small_v[2:3, :] = jnp.sum(da * normed, axis=0, keepdims=True)
        small_v[3:4, :] = jnp.sum(da, axis=0, keepdims=True)
        put(small_v, "small")
        hat = da * gains_v[0:1, :]
        dx = dm_v[...] + inverse * (
            hat
            - jnp.mean(hat, axis=-1, keepdims=True)
            - normed * jnp.mean(hat * normed, axis=-1, keepdims=True)
        )
        dx_v[...] = dx.astype(bf16)
        copies.start(dx_v, dx_ref)
        copies.finish()


KEPT = ("gp", "n2", "r2", "linv", "qkv", "e", "o", "x")


def back_call(scal, layer, dy, common, weights, vecs, fronts, backs):
    scratch = [
        vmem(ROWS, WIDTH), vmem(KEYS, 128, dtype=f32), vmem(ROWS, WIDTH, dtype=f32), vmem(ROWS, WIDTH, dtype=f32),
        vmem(WIDTH, 3 * WIDTH), vmem(WIDTH, WIDTH), vmem(WIDTH, HIDDEN), vmem(HIDDEN, WIDTH), vmem(16, WIDTH, dtype=f32),
        vmem(ROWS, HIDDEN), vmem(ROWS, WIDTH), vmem(ROWS, 128, dtype=f32), vmem(ROWS, WIDTH, dtype=f32),
        vmem(KEYS, 3 * WIDTH), vmem(HEADS, ROWS, KEYS), vmem(ROWS, WIDTH), vmem(ROWS, WIDTH),
        vmem(ROWS, HIDDEN), vmem(ROWS, WIDTH), vmem(ROWS, WIDTH, dtype=f32), vmem(ROWS, WIDTH),
        vmem(WIDTH, ROWS), vmem(WIDTH, ROWS), vmem(ROWS, WIDTH, dtype=f32),
        vmem(WIDTH, KEYS, dtype=f32), vmem(WIDTH, KEYS), vmem(ROWS, 3 * WIDTH), vmem(8, WIDTH, dtype=f32), vmem(ROWS, WIDTH),
        pltpu.SemaphoreType.DMA((36,)),
    ]
    operands = [scal, layer, dy, *common, *weights, vecs[0], vecs[4], *(fronts[name] for name in KEPT)]
    out = jax.ShapeDtypeStruct((ROWS, WIDTH), bf16)
    return call_states(back_kernel, backs is None, operands, 2, backs, [out], BACK_SHAPES, scratch, "layer_back")


def side_of(kind):
    return jnp.where(kind == 0, float(SIDE_LARGE), jnp.where(kind == 1, float(SIDE_MID), float(SIDE_SMALL)))


def places(kind, rows):
    side = side_of(kind)
    area = side * side
    images = jnp.where(kind == 2, 2.0, 1.0)
    image = (rows >= area).astype(f32) + (rows >= 2 * area).astype(f32)
    live = (image < images) & (rows < ROWS)
    local = rows - image * area
    patch_row = jnp.floor((local + 0.5) / side)
    patch_col = local - patch_row * side
    zero = jnp.zeros_like(rows)
    segment = jnp.where(live, image, jnp.where(rows < ROWS, 3.0, 2.0))
    return jnp.where(live, patch_row, zero), jnp.where(live, patch_col, zero), segment, live


def split_low(values):
    high = values.astype(bf16)
    return jnp.concatenate([high, (values - high.astype(f32)).astype(bf16)], axis=0)


def tables_kernel(first, turn_ref, kind_ref, freq_in, *refs):
    if not first:
        refs = refs[4:]
    geo_ref, cos_ref, sin_ref, freq_v, geo_v, cos_v, sin_v, sems = refs

    @pl.when(turn_ref[0] == 1)
    def _():
        micro = turn_ref[1]
        copies = Copies(sems)
        copies.wait(copies.start(freq_in, freq_v))
        step = lax.broadcasted_iota(jnp.int32, (32, WIDTH // 2), 0).astype(f32)
        angles = [step * freq_v[:, at : at + WIDTH // 2] for at in (0, WIDTH // 2)]
        waves = [split_low(jnp.concatenate([jnp.cos(angle), jnp.sin(angle)], axis=1)) for angle in angles]
        sixteen = lax.broadcasted_iota(jnp.int32, (ROWS, 64), 1) % 32
        rows = lax.broadcasted_iota(jnp.int32, (KEYS, 128), 0).astype(f32)
        lane = lax.broadcasted_iota(jnp.int32, (KEYS, 128), 1)
        patch_row, patch_col, segment, _ = places(kind_ref[micro], rows)
        geo_v[...] = jnp.where(lane == 0, patch_row, jnp.where(lane == 1, patch_col, segment))
        picks = [
            jnp.where(sixteen.astype(f32) == patch[:ROWS, :64], 1.0, 0.0).astype(bf16)
            for patch in (patch_row, patch_col)
        ]
        row_wave, col_wave = (
            jnp.dot(pick, wave, preferred_element_type=f32) for pick, wave in zip(picks, waves)
        )
        half = WIDTH // 2
        row_cos, row_sin = row_wave[:, :half], row_wave[:, half:]
        col_cos, col_sin = col_wave[:, :half], col_wave[:, half:]
        cosine = row_cos * col_cos - row_sin * col_sin
        sine = row_sin * col_cos + row_cos * col_sin
        lane = lax.broadcasted_iota(jnp.int32, (ROWS, 128), 1)
        for part in range(half // 128):
            for pair in range(2):
                at = (2 * part + pair) * 128
                cos_v[:, at : at + 128] = spread(cosine[:, part * 128 : part * 128 + 128], pair, lane)
                values = spread(sine[:, part * 128 : part * 128 + 128], pair, lane)
                sin_v[:, at : at + 128] = jnp.where(lane % 64 < 32, -values, values)
        copies.start(geo_v, geo_ref.at[micro])
        copies.start(cos_v, cos_ref.at[micro])
        copies.start(sin_v, sin_ref.at[micro])
        copies.finish()


def spread(values, pair, lane):
    base = values if pair == 0 else pltpu.roll(values, 64, 1)
    by_one = pltpu.roll(base, 32, 1)
    by_two = pltpu.roll(base, 64, 1)
    return jnp.where(lane < 32, base, jnp.where(lane < 96, by_one, by_two))


def tables(turn, kinds, frequency, earlier=None, held=None):
    shapes = [(KEYS, 128), (ROWS, WIDTH), (ROWS, WIDTH)]
    first = held is None
    operands = [turn, kinds, frequency] + ([] if first else [earlier, *held])
    return pl.pallas_call(
        partial(tables_kernel, first),
        out_shape=[jax.ShapeDtypeStruct((MICRO,) + shape, f32) for shape in shapes],
        in_specs=[pl.BlockSpec(memory_space=pltpu.SMEM)] * 2 + [ANY] * (len(operands) - 2),
        out_specs=[ANY] * 3,
        scratch_shapes=[vmem(1, WIDTH, dtype=f32)]
        + [vmem(*shape, dtype=f32) for shape in shapes]
        + [pltpu.SemaphoreType.DMA((8,))],
        input_output_aliases={} if first else {4: 0, 5: 1, 6: 2},
        compiler_params=pltpu.CompilerParams(vmem_limit_bytes=VMEM_LIMIT),
        name="tables",
    )(*operands)


def live_rows_of(kinds):
    rows = jnp.broadcast_to(jnp.arange(ROWS, dtype=jnp.int32).astype(f32)[None, :], (MICRO, ROWS))
    return places(kinds[:, None], rows)[3].reshape(-1, 1)


def product_kernel(
    offset, block, core_ref, left_in, right_in, other_ref, own_ref, sums_ref,
    other_v, own_v, right_v, other_out, own_out, sums_out, sems,
):
    copies = Copies(sems)
    core = core_ref[0]
    half = left_in.shape[1] // 2
    rows = other_v.shape[1]
    get_right = copies.start(right_in, right_v)
    get_other = copies.start(left_in.at[:, pl.ds(pl.multiple_of((1 - core) * half + offset, 128), rows)], other_v)
    get_own = copies.start(left_in.at[:, pl.ds(pl.multiple_of(core * half + offset, 128), rows)], own_v)
    copies.wait(get_right)
    for get, part_v, part_out, ref in (
        (get_other, other_v, other_out, other_ref),
        (get_own, own_v, own_out, own_ref),
    ):
        copies.wait(get)

        for at in range(0, rows, block):
            lanes = pl.ds(at, block)
            part_out[lanes, :] = lax.dot_general(
                part_v[:, lanes], right_v[...], TN, preferred_element_type=f32
            ).astype(bf16)
            copies.start(part_out.at[lanes], ref.at[lanes])
    sums_out[...] = jnp.dot(jnp.ones((16, right_v.shape[0]), bf16), right_v[...], preferred_element_type=f32)[:8]
    copies.start(sums_out, sums_ref)
    copies.finish()


def product_call(core, left, right, offset, rows):
    left = left.reshape(MICRO * ROWS, left.shape[-1])
    right = right.reshape(MICRO * ROWS, right.shape[-1])
    count, width = right.shape
    block = 512 if rows % 512 == 0 else 384
    return pl.pallas_call(
        partial(product_kernel, offset, block),
        out_shape=[jax.ShapeDtypeStruct((rows, width), bf16)] * 2 + [jax.ShapeDtypeStruct((8, width), f32)],
        in_specs=[pl.BlockSpec(memory_space=pltpu.SMEM), ANY, ANY],
        out_specs=[ANY] * 3,
        scratch_shapes=[
            vmem(count, rows), vmem(count, rows), vmem(count, width), vmem(rows, width), vmem(rows, width),
            vmem(8, width, dtype=f32), pltpu.SemaphoreType.DMA((16,)),
        ],
        compiler_params=pltpu.CompilerParams(vmem_limit_bytes=VMEM_LIMIT),
        name="weight_grad",
    )(core, left, right)


def send(value, source, target):
    return lax.ppermute(value, "section", [(source, target)])


def gathered(part, target, sections):
    pieces = [part if source == target else send(part, source, target) for source in range(sections)]
    return jnp.concatenate(pieces, axis=0)


def handed_out(whole, source, sections):
    section = lax.axis_index("section")
    share = whole.shape[0] // sections
    result = whole[source * share : (source + 1) * share]
    for target in range(sections):
        if target != source:
            piece = send(whole[target * share : (target + 1) * share], source, target)
            result = jnp.where(section == target, piece, result)
    return result


def added(one, other):
    return (one.astype(f32) + other.astype(f32)).astype(bf16)


def both_cores(pairs):
    return [(2 * a + core, 2 * b + core) for a, b in pairs for core in range(2)]


def core_swap():
    return [(i, i ^ 1) for i in range(lax.axis_size("dp"))]


class Relay:
    LAG = 3

    def __init__(self):
        self.chunks, self.sums, self.totals = [], [], []
        self.flying, self.joined, self.clock = [], [], 0

    def start(self, value, pairs, then, keep):
        self.flying.append((self.clock, lax.ppermute(value, "dp", pairs), then, keep))

    def step(self, *gate, every=False):
        ready = [f for f in self.flying if every or f[0] + self.LAG <= self.clock]
        self.flying = [f for f in self.flying if not (every or f[0] + self.LAG <= self.clock)]
        even = self.clock % 2 == 0
        fresh = self.chunks.pop(0) if even and self.chunks else None
        arrays, keeps = [f[1] for f in ready], [f[3] for f in ready]
        new = [] if fresh is None else [fresh[0]]
        joined, self.joined = self.joined, []
        results = [item.result for item in joined]
        arrays, keeps, new, gate, results = lax.optimization_barrier((arrays, keeps, new, gate, results))
        for item, result in zip(joined, results):
            item.result = result
        for (_, _, then, _), array, keep in zip(ready, arrays, keeps):
            then(array, keep)
        if even:
            self.outer_step((new[0],) + fresh[1:] if fresh else None, self.totals.pop(0) if self.totals else None)
        elif self.sums:
            both, done = self.sums.pop(0)
            pairs = both_cores([(1, 2), (2, 1)])
            self.start(both, pairs, lambda array, keep: self.totals.append((added(keep, array), done)), both)
        self.clock += 1
        return gate[0] if len(gate) == 1 else gate

    def outer_step(self, chunk, total):
        inward, outward = both_cores([(0, 1), (3, 2)]), both_cores([(1, 0), (2, 3)])
        chip = lax.axis_index("dp") // 2
        outer = (chip == 0) | (chip == 3)

        def inner_sum(array, own):
            self.sums.append((added(own, array), chunk[1]))

        def result(array, own):
            total[1](jnp.where(outer, array, own))

        if chunk and total and chunk[0].shape == total[0].shape:
            def land(array, keep):
                inner_sum(array, keep[0])
                result(array, keep[1])

            value = jnp.where(outer, chunk[0], total[0])
            self.start(value, inward + outward, land, (chunk[0], total[0]))
        else:
            if total:
                self.start(total[0], outward, result, total[0])
            if chunk:
                self.start(chunk[0], inward, inner_sum, chunk[0])

    def finish(self):
        while self.chunks or self.sums or self.totals or self.flying:
            self.step()


class LineSum:
    def __init__(self, relay, axis):
        self.relay, self.axis, self.count = relay, axis, 0
        self.totals, self.result = {}, None

    def add(self, other, mine, pieces):
        half = added(mine, lax.ppermute(other, "dp", core_swap()))
        for chunk in jnp.split(half, pieces, axis=self.axis):
            self.relay.chunks.append((chunk, partial(self.landed, self.count)))
            self.count += 1

    def landed(self, index, total):
        self.totals[index] = total
        if len(self.totals) == self.count:
            mine = jnp.concatenate([self.totals[i] for i in range(self.count)], axis=self.axis)
            self.relay.start(mine, core_swap(), self.join, mine)

    def join(self, other, mine):
        core = lax.axis_index("dp") % 2
        low, high = jnp.where(core == 0, mine, other), jnp.where(core == 0, other, mine)
        self.result = jnp.concatenate([low, high], axis=0).astype(f32)
        self.relay.joined.append(self)


def summed_by_compiler(part):
    count, rows = lax.axis_size("dp"), part.shape[0]
    part = jnp.pad(part, ((0, -rows % count), (0, 0)))
    own = lax.psum_scatter(part, "dp", scatter_dimension=0, tiled=True)
    return lax.all_gather(own, "dp", axis=0, tiled=True)[:rows].astype(f32)


SMALL_ROWS = 32


def per_device(
    tokens,
    cotangent,
    image_kind,
    norm_one_gain,
    norm_one_bias,
    qkv_weight,
    qkv_bias,
    rotary_freq,
    proj_weight,
    proj_bias,
    norm_two_gain,
    norm_two_bias,
    up_weight,
    up_bias,
    down_weight,
    down_bias,
):
    sections = lax.axis_size("section")
    section = lax.axis_index("section")
    last = sections - 1
    by_line = lax.axis_size("dp") == 8
    scal = section.astype(jnp.int32).reshape(1)
    core = (lax.axis_index("dp") % 2).astype(jnp.int32).reshape(1)
    low = core[0] == 0
    micros = jnp.arange(MICRO, dtype=jnp.int32)
    whole = tables(jnp.array([1, 0], jnp.int32), image_kind, rotary_freq)
    common = tables(jnp.stack([core[0], micros[1]]), image_kind, rotary_freq, tokens, whole)
    weights = (qkv_weight[0], proj_weight[0], up_weight[0], down_weight[0])
    vecs = (
        norm_one_gain, norm_one_bias, qkv_bias, proj_bias, norm_two_gain, norm_two_bias, up_bias, down_bias,
    )
    first_in = gathered(tokens, 0, sections)
    live_rows = live_rows_of(image_kind)
    last_in = gathered(cotangent, last, sections)
    last_in = jnp.where(live_rows > 0, last_in, bf16(0.0))

    def turn(layer, micro):
        return jnp.array([layer, micro], jnp.int32)

    states = None
    values = [first_in[m * ROWS : (m + 1) * ROWS] for m in range(MICRO)]
    for layer in range(sections):
        if layer == 2:
            values[0], last_in = lax.optimization_barrier((values[0], last_in))
        for micro in range(MICRO):
            out, states = front_call(scal, turn(layer, micro), values[micro], common, weights, vecs, states)
            if layer == 0 and micro == 0:
                common = tables(jnp.stack([1 - core[0], micros[1]]), image_kind, rotary_freq, out, common)
            values[micro] = send(out, layer, layer + 1) if layer < last else out
    fronts = dict(zip(STATES, states))
    backs = None
    grads = [last_in[m * ROWS : (m + 1) * ROWS] for m in range(MICRO)]
    out_grads = list(grads)
    relay = Relay()
    sums = [LineSum(relay, axis) for axis in (1, 0, 1, 0)]
    plain = [[], [], [], []]

    def to_sum(index, other, mine, pieces):
        if by_line:
            sums[index].add(other, mine, pieces)
        else:
            plain[index].append((jnp.where(low, mine, other), jnp.where(low, other, mine)))

    for layer in reversed(range(sections)):
        if 0 < layer < last:
            out_grads = [jnp.where(section == layer, new, old) for new, old in zip(grads, out_grads)]
        if layer == 0:
            received = grads[0]
        for micro in range(MICRO):
            end = layer == 0 and micro == MICRO - 1
            if end:
                grads[0], grads[1], out_grads = lax.optimization_barrier((grads[0], grads[1], out_grads))
                out_grads = [jnp.where(section == 0, new, old) for new, old in zip((received, grads[1]), out_grads)]
                all_grads = jnp.concatenate(out_grads, axis=0)
                for offset in (0, 768):
                    other, mine, b_down = product_call(core, fronts["g"], all_grads, offset, 768)
                    to_sum(3, other, mine, 2)
                relay.step()
                relay.step()
                grads[1] = relay.step(grads[1])
            dx, backs = back_call(scal, turn(layer, micro), grads[micro], common, weights, vecs, fronts, backs)
            if end:
                dx, backs = relay.step(dx, backs, every=True)
            grads[micro] = send(dx, layer, layer - 1) if layer > 0 else dx
    relay.step()
    backs = dict(zip(BACKS, relay.step(*backs)))
    other, mine, b_up = product_call(core, fronts["c"], backs["du"], 0, WIDTH // 2)
    to_sum(2, other, mine, 4)
    relay.step()
    dqkv = relay.step(backs["dqkv"])
    other, mine, b_qkv = product_call(core, fronts["a"], dqkv, 0, WIDTH // 2)
    to_sum(0, other, mine, 3)
    relay.step()
    o_kept, dz, small = relay.step(fronts["o"], backs["dz"], backs["small"])
    other, mine, b_proj = product_call(core, o_kept, dz, 0, WIDTH // 2)
    small = jnp.sum(small, axis=0)
    turns = small[4:6].reshape(2, HEADS, 2, 32)
    freq = (turns[:, :, 1] - turns[:, :, 0]).reshape(-1)
    small = jnp.concatenate(
        [small[2], small[3], b_qkv[0], freq, b_proj[0], small[0], small[1], b_up[0], b_down[0]]
    )
    small = small.astype(bf16).reshape(-1, WIDTH)
    small = jnp.pad(small, ((0, SMALL_ROWS - small.shape[0]), (0, 0)))
    half = SMALL_ROWS // 2
    mine = jnp.concatenate([mine, jnp.where(low, small[:half], small[half:])], axis=0)
    other = jnp.concatenate([other, jnp.where(low, small[half:], small[:half])], axis=0)
    to_sum(1, other, mine, 1)
    relay.step()
    values = relay.step(*values)
    final = jnp.where(live_rows > 0, jnp.concatenate(values, axis=0), bf16(0.0))
    block_out = handed_out(final, last, sections)
    relay.step()
    relay.step()
    relay.step()
    relay.step()
    grads[0], grads[1], block_out = relay.step(*grads, block_out)
    grad_tokens = handed_out(jnp.concatenate(grads, axis=0), 0, sections)
    relay.step()
    relay.step()
    relay.step()
    grad_tokens = relay.step(grad_tokens)
    relay.finish()
    if by_line:
        grad_qkv, grad_proj, grad_up, grad_down = (item.result for item in sums)
    else:
        grad_qkv, grad_proj, grad_up, grad_down = (
            summed_by_compiler(jnp.concatenate([part[side] for side in range(2) for part in parts], axis=0))
            for parts in plain
        )
    middle = WIDTH // 2
    small = jnp.concatenate([grad_proj[middle : middle + half], grad_proj[middle + half + middle :]], axis=0).reshape(-1)
    grad_proj = jnp.concatenate([grad_proj[:middle], grad_proj[middle + half : middle + half + middle]], axis=0)
    sizes = (WIDTH, WIDTH, 3 * WIDTH, WIDTH, WIDTH, WIDTH, WIDTH, HIDDEN, WIDTH)
    ends = np.cumsum((0,) + sizes)
    g_one, b_one, b_qkv, freq, b_proj, g_two, b_two, b_up, b_down = (
        small[int(ends[i]) : int(ends[i + 1])][None] for i in range(len(sizes))
    )
    return (
        block_out, grad_tokens.astype(f32), g_one, b_one, grad_qkv[None], b_qkv, freq,
        grad_proj[None], b_proj, g_two, b_two, grad_up[None], b_up, grad_down[None], b_down,
    )


def solution(mesh):
    row = P(("dp", "section"), None)
    vector = P("section", None)
    matrix = P("section", None, None)
    params = (
        vector, vector, matrix, vector, vector, matrix, vector, vector, vector, matrix, vector, matrix, vector,
    )
    return jax.shard_map(
        per_device,
        mesh=mesh,
        in_specs=(row, row, P("dp")) + params,
        out_specs=(row, row) + params,
        check_vma=False,
    )
```

time: 779 us -> 642 us (0.82)
  waiting for transfers between devices: 468 us -> 229 us
  starting transfers between devices: 30 us -> 171 us
  matrix products: 28.3 us -> 0 us
  Pallas kernels: 144 us -> 167 us
  other arithmetic: 62.8 us -> 45.6 us
  between operations: 15.5 us -> 2.31 us
    reduce_scatter x4 -> x0, waiting for transfers between devices: 159 us -> none  [summed_over_images(): own = lax.psum_scatter(part, 'dp', scatter_dimension=0, tiled=True)]
    all_gather x4 -> x0, waiting for transfers between devices: 131 us -> none  [summed_over_images(): return lax.all_gather(own, 'dp', axis=0, tiled=True)]
    ppermute x0 -> x37, starting transfers between devices: none -> 112 us  [the longest x32 111 us: start(): lax.ppermute(value, 'dp', pairs)]
    ppermute x0 -> x37, waiting for transfers between devices: none -> 102 us  [the longest x32 102 us: start(): lax.ppermute(value, 'dp', pairs)]
    ppermute x24, waiting for transfers between devices: 178 us -> 127 us  [send(): return lax.ppermute(value, 'section', [(source, target)])]
    ppermute x24, starting transfers between devices: 29.4 us -> 58.5 us  [send(): return lax.ppermute(value, 'section', [(source, target)])]
    dot_general x4 -> x0, matrix products: 28.3 us -> none  [rows_product(): jnp.einsum('rd,re->de', left, right, preferred_element_type=f32)]
    pallas_call x24, Pallas kernels: 144 us -> 167 us  [the longest x16 123 us: call_states(): pl.pallas_call(partial(kernel, first), out_shape=list(plain_out) + state_...]
  transfers between devices with their start and end apart: 32 -> 61, of which waited for: 14 -> 16; matrix products, arithmetic and copies ran while one was open for 10% -> 8% of each run, Pallas kernels for 15% -> 23%
where the time goes in v2:
time: 642 us; the launch traced here: 636 us
  waiting for transfers between devices  229 us (36%)
  starting transfers between devices  171 us (27%)
  Pallas kernels  167 us (26%)
  other arithmetic  45.6 us (7%)
  local copies, waits for them, and re-layouts  21 us (3%)
    ppermute x24, waiting for transfers between devices, send(): return lax.ppermute(value, 'section', [(source, target)])  127 us
    pallas_call x16, Pallas kernels, call_states(): pl.pallas_call(partial(kernel, first), out_shape=list(plain_out) + state_...  123 us
    ppermute x32, starting transfers between devices, start(): lax.ppermute(value, 'dp', pairs)  111 us
    ppermute x32, waiting for transfers between devices, start(): lax.ppermute(value, 'dp', pairs)  102 us
    ppermute x24, starting transfers between devices, send(): return lax.ppermute(value, 'section', [(source, target)])  58.5 us
    pallas_call x5, Pallas kernels, product_call(): pl.pallas_call(partial(product_kernel, offset, block), out_shape=[jax.Sha...  32.8 us
    convert_element_type x4, other arithmetic, join(): self.result = jnp.concatenate([low, high], axis=0).astype(f32)  13.2 us
    unnamed x68, local copies, waits for them, and re-layouts  13 us
  transfers between devices with their start and end apart: 61, of which 16 were waited for; matrix products, arithmetic and copies ran while one was open for 8% of the time, Pallas kernels for 23%

profile of v2, /device:TPU:0, one launch (start us, length us, event | category | flops | bytes accessed | tf_op | source)
XLA Modules:
  0.0 636.2 jit_solution(13377089303028602176)
XLA Ops:
  13.8 18.9 %layer_front.8 = (bf16[400,768]{1,0:T(8,128)(2,1)}, bf16[2,400,768]{2,1,0:T(8,128)(2,1)}, bf16[2,400,768]{2,1,0:T(8,128)(2,1)}, bf16[2,400,2304]{2,1,0:T(8,128)(...) custom-call(s32[1]{0:T(128)} %bitcast.1.scal, ...), custom_call_target="tpu_custom_call" | custom-call | tf_op jit(solution)/shard_map/layer_front/pallas_call | solution.py:239
  40.6 18.8 %layer_front.9 = (bf16[400,768]{1,0:T(8,128)(2,1)}, bf16[2,400,768]{2,1,0:T(8,128)(2,1)}, bf16[2,400,768]{2,1,0:T(8,128)(2,1)}, bf16[2,400,2304]{2,1,0:T(8,128)(...) custom-call(s32[1]{0:T(128)} %bitcast.1.scal, ...), custom_call_target="tpu_custom_call", output_to_operand_aliasing={{1}: (18, {}), {2}: (19, {}), {3}: (20, {}), {4}: (21, {}),... | custom-call | tf_op jit(solution)/shard_map/layer_front/pallas_call | solution.py:239
  66.9 8.3 %collective-permute-done.3.refs_0_ = bf16[400,768]{1,0:T(8,128)(2,1)S(1)} collective-permute-done((bf16[400,768]{1,0:T(8,128)(2,1)}, bf16[400,768]{1,0:T(8,128)(2,1)S(1)}, u32[]{:S(2)}, u32[]{:S(2)}) %collective-permute-start.3) | collective-permute-done | bytes 614432 | tf_op jit(solution)/shard_map/ppermute | solution.py:577
  107.2 8.6 %layer_back.8 = (bf16[400,768]{1,0:T(8,128)(2,1)}, bf16[2,400,3072]{2,1,0:T(8,128)(2,1)}, bf16[2,400,768]{2,1,0:T(8,128)(2,1)}, bf16[2,400,2304]{2,1,0:T(8,128)(2,1)}, f32[2,8,768]{2,1,0:T(8,128)}) custom-call(s32[1]{0:T(128)} %bitcast.1.scal, s32[2]{0:T(128)} %constant.109.clone.layer, bf16[400,768]{1,0:T(8,128)(2,1)} %get-tuple-element.605.refs_0_, ...), custom_call_target="tpu_custom_call" | custom-call | tf_op jit(solution)/shard_map/layer_back/pallas_call | solution.py:239
  115.8 8.7 %collective-permute-start.12 = (bf16[400,768]{1,0:T(8,128)(2,1)}, bf16[400,768]{1,0:T(8,128)(2,1)S(1)}, u32[]{:S(2)}, u32[]{:S(2)}) collective-permute-start(bf16[400,768]{1,0:T(8,128)(2,1)} %get-tuple-element.387), channel_id=1, source_target_pairs={{24,16},{25,17},{26,18},{27,19},{28,20},{29,21},{30,22},{31,23}} | collective-permute-start | bytes 1843208 | tf_op jit(solution)/shard_map/ppermute | solution.py:577
  133.2 8.5 %collective-permute-start.13 = (bf16[400,768]{1,0:T(8,128)(2,1)}, bf16[400,768]{1,0:T(8,128)(2,1)S(1)}, u32[]{:S(2)}, u32[]{:S(2)}) collective-permute-start(bf16[400,768]{1,0:T(8,128)(2,1)} %get-tuple-element.396), channel_id=1, source_target_pairs={{16,8},{17,9},{18,10},{19,11},{20,12},{21,13},{22,14},{23,15}} | collective-permute-start | bytes 1843208 | tf_op jit(solution)/shard_map/ppermute | solution.py:577
  168.6 112.6 %collective-permute-done.15.refs_0_ = bf16[400,768]{1,0:T(8,128)(2,1)} collective-permute-done((bf16[400,768]{1,0:T(8,128)(2,1)}, bf16[400,768]{1,0:T(8,128)(2,1)}, u32[]{:S(2)}, u32[]{:S(2)}) %collective-permute-start.15) | collective-permute-done | bytes 614432 | tf_op jit(solution)/shard_map/ppermute | solution.py:577
  281.2 22.9 %layer_back.14 = (bf16[400,768]{1,0:T(8,128)(2,1)}, bf16[2,400,3072]{2,1,0:T(8,128)(2,1)}, bf16[2,400,768]{2,1,0:T(8,128)(2,1)}, bf16[2,400,2304]{2,1,0:T(8,128)(2,1)}, f32[2,8,768]{2,1,0:T(8,128)}) custom-call(s32[1]{0:T(128)} %bitcast.1.scal, s32[2]{0:T(128)} %call_exported.0.layer, ...), custom_call_target="tpu_custom_call", output_to_operand_aliasing={{1}: (20, {}), {2}: (21, {}), {3}: (22, {}), {4}: (23, {})} | custom-call | tf_op jit(solution)/shard_map/layer_back/pallas_call | solution.py:239
  326.2 22.7 %layer_back.15 = (bf16[400,768]{1,0:T(8,128)(2,1)}, bf16[2,400,3072]{2,1,0:T(8,128)(2,1)}, bf16[2,400,768]{2,1,0:T(8,128)(2,1)}, bf16[2,400,2304]{2,1,0:T(8,128)(2,1)}, f32[2,8,768]{2,1,0:T(8,128)}) custom-call(s32[1]{0:T(128)} %bitcast.1.scal, s32[2]{0:T(128)} %call_exported.1.layer, ...), custom_call_target="tpu_custom_call", output_to_operand_aliasing={{1}: (20, {}), {2}: (21, {}), {3}: (22, {}), {4}: (23, {})} | custom-call | tf_op jit(solution)/shard_map/layer_back/pallas_call | solution.py:239
  355.1 9.4 %weight_grad.7 = (bf16[384,3072]{1,0:T(8,128)(2,1)}, bf16[384,3072]{1,0:T(8,128)(2,1)}, f32[8,3072]{1,0:T(8,128)}) custom-call(s32[1]{0:T(128)} %bitcast.core_ref, bf16[800,768]{1,0:T(8,128)(2,1)} %bitcast.97, bf16[800,3072]{1,0:T(8,128)(2,1)} %bitcast.77), custom_call_target="tpu_custom_call" | custom-call | tf_op jit(solution)/shard_map/weight_grad/pallas_call | solution.py:562
  373.1 10.3 %collective-permute-done.19 = bf16[384,768]{1,0:T(8,128)(2,1)S(1)} collective-permute-done((bf16[384,768]{1,0:T(8,128)(2,1)S(1)}, bf16[384,768]{1,0:T(8,128)(2,1)S(1)}, u32[]{:S(2)}, u32[]{:S(2)}) %collective-permute-start.19) | collective-permute-done | bytes 589856 | tf_op jit(solution)/shard_map/ppermute | solution.py:616
  386.5 7.9 %weight_grad.8 = (bf16[384,2304]{1,0:T(8,128)(2,1)}, bf16[384,2304]{1,0:T(8,128)(2,1)}, f32[8,2304]{1,0:T(8,128)}) custom-call(s32[1]{0:T(128)} %bitcast.core_ref, bf16[800,768]{1,0:T(8,128)(2,1)} %bitcast.96, bf16[800,2304]{1,0:T(8,128)(2,1)} %bitcast.95), custom_call_target="tpu_custom_call" | custom-call | tf_op jit(solution)/shard_map/weight_grad/pallas_call | solution.py:562
  409.7 20.4 %collective-permute-start.43 = (bf16[384,768]{1,0:T(8,128)(2,1)S(1)}, bf16[384,768]{1,0:T(8,128)(2,1)S(1)}, u32[]{:S(2)}, u32[]{:S(2)}) collective-permute-start(bf16[384,768]{1,0:T(8,128)(2,1)S(1)} %get-tuple-element.561), channel_id=1, source_target_pairs={{0,2},{1,3},{6,4},{7,5},{2,0},{3,1},{4,6},{5,7},{8,10},{9,11},{14,... | collective-permute-start | bytes 1769480 | tf_op jit(solution)/shard_map/ppermute | solution.py:616
  444.3 12.6 %collective-permute-done.29 = bf16[384,768]{1,0:T(8,128)(2,1)S(1)} collective-permute-done((bf16[384,768]{1,0:T(8,128)(2,1)S(1)}, bf16[384,768]{1,0:T(8,128)(2,1)S(1)}, u32[]{:S(2)}, u32[]{:S(2)}) %collective-permute-start.29) | collective-permute-done | bytes 589856 | tf_op jit(solution)/shard_map/ppermute | solution.py:616
  457.0 11.6 %collective-permute-done.25 = bf16[384,768]{1,0:T(8,128)(2,1)S(1)} collective-permute-done((bf16[384,768]{1,0:T(8,128)(2,1)S(1)}, bf16[384,768]{1,0:T(8,128)(2,1)S(1)}, u32[]{:S(2)}, u32[]{:S(2)}) %collective-permute-start.25) | collective-permute-done | bytes 589856 | tf_op jit(solution)/shard_map/ppermute | solution.py:616
  474.6 17.6 %collective-permute-start.34 = (bf16[384,768]{1,0:T(8,128)(2,1)S(1)}, bf16[384,768]{1,0:T(8,128)(2,1)S(1)}, u32[]{:S(2)}, u32[]{:S(2)}) collective-permute-start(bf16[384,768]{1,0:T(8,128)(2,1)S(1)} %get-tuple-element.567), channel_id=1, source_target_pairs={{0,2},{1,3},{6,4},{7,5},{2,0},{3,1},{4,6},{5,7},{8,10},{9,11},{14,... | collective-permute-start | bytes 1769480 | tf_op jit(solution)/shard_map/ppermute | solution.py:616
  497.3 7.7 %collective-permute-done.34 = bf16[384,768]{1,0:T(8,128)(2,1)S(1)} collective-permute-done((bf16[384,768]{1,0:T(8,128)(2,1)S(1)}, bf16[384,768]{1,0:T(8,128)(2,1)S(1)}, u32[]{:S(2)}, u32[]{:S(2)}) %collective-permute-start.34) | collective-permute-done | bytes 589856 | tf_op jit(solution)/shard_map/ppermute | solution.py:616
  506.9 10.8 %collective-permute-start.39 = (bf16[384,768]{1,0:T(8,128)(2,1)S(1)}, bf16[384,768]{1,0:T(8,128)(2,1)S(1)}, u32[]{:S(2)}, u32[]{:S(2)}) collective-permute-start(bf16[384,768]{1,0:T(8,128)(2,1)S(1)} %get-tuple-element.565), channel_id=1, source_target_pairs={{0,2},{1,3},{6,4},{7,5},{2,0},{3,1},{4,6},{5,7},{8,10},{9,11},{14,... | collective-permute-start | bytes 1769480 | tf_op jit(solution)/shard_map/ppermute | solution.py:616
  518.1 9.8 %collective-permute-start.56 = (bf16[384,768]{1,0:T(8,128)(2,1)S(1)}, bf16[384,768]{1,0:T(8,128)(2,1)S(1)}, u32[]{:S(2)}, u32[]{:S(2)}) collective-permute-start(bf16[384,768]{1,0:T(8,128)(2,1)S(1)} %get-tuple-element.559), channel_id=1, source_target_pairs={{0,2},{1,3},{6,4},{7,5},{2,0},{3,1},{4,6},{5,7},{8,10},{9,11},{14,... | collective-permute-start | bytes 1769480 | tf_op jit(solution)/shard_map/ppermute | solution.py:616
  533.9 12.6 %collective-permute-start.53 = (bf16[384,768]{1,0:T(8,128)(2,1)S(1)}, bf16[384,768]{1,0:T(8,128)(2,1)S(1)}, u32[]{:S(2)}, u32[]{:S(2)}) collective-permute-start(bf16[384,768]{1,0:T(8,128)(2,1)S(1)} %get-tuple-element.557), channel_id=1, source_target_pairs={{0,2},{1,3},{6,4},{7,5},{2,0},{3,1},{4,6},{5,7},{8,10},{9,11},{14,... | collective-permute-start | bytes 1769480 | tf_op jit(solution)/shard_map/ppermute | solution.py:616
  548.1 13.0 %collective-permute-start.49 = (bf16[400,768]{1,0:T(8,128)(2,1)S(1)}, bf16[400,768]{1,0:T(8,128)(2,1)S(1)}, u32[]{:S(2)}, u32[]{:S(2)}) collective-permute-start(bf16[400,768]{1,0:T(8,128)(2,1)S(1)} %add_convert_fusion.6), channel_id=1, source_target_pairs={{0,2},{1,3},{6,4},{7,5},{8,10},{9,11},{14,12},{15,13},{16,18},{17,... | collective-permute-start | bytes 1843208 | tf_op jit(solution)/shard_map/ppermute | solution.py:616
  561.5 8.5 %collective-permute-done.48 = bf16[384,768]{1,0:T(8,128)(2,1)S(1)} collective-permute-done((bf16[384,768]{1,0:T(8,128)(2,1)S(1)}, bf16[384,768]{1,0:T(8,128)(2,1)S(1)}, u32[]{:S(2)}, u32[]{:S(2)}) %collective-permute-start.48) | collective-permute-done | bytes 589856 | tf_op jit(solution)/shard_map/ppermute | solution.py:616
  576.7 30.0 %collective-permute-done.51 = bf16[400,768]{1,0:T(8,128)(2,1)S(1)} collective-permute-done((bf16[400,768]{1,0:T(8,128)(2,1)S(1)}, bf16[400,768]{1,0:T(8,128)(2,1)S(1)}, u32[]{:S(2)}, u32[]{:S(2)}) %collective-permute-start.51) | collective-permute-done | bytes 614432 | tf_op jit(solution)/shard_map/ppermute | solution.py:616
  617.1 10.1 %collective-permute-done.59 = bf16[384,768]{1,0:T(8,128)(2,1)S(1)} collective-permute-done((bf16[384,768]{1,0:T(8,128)(2,1)S(1)}, bf16[384,768]{1,0:T(8,128)(2,1)S(1)}, u32[]{:S(2)}, u32[]{:S(2)}) %collective-permute-start.59) | collective-permute-done | bytes 589856 | tf_op jit(solution)/shard_map/ppermute | solution.py:616
  (293 shorter events, 211.5 us)
Async XLA Ops:
  1.9 37.3 %collective-permute-start = (bf16[200,768]{1,0:T(8,128)(2,1)}, bf16[200,768]{1,0:T(8,128)(2,1)S(1)}, u32[]{:S(2)}, u32[]{:S(2)}) collective-permute-start(bf16[200,768]{1,0:T(8,128)(2,1)} %refs_0_.1), channel_id=1, source_target_pairs={{16,0},{17,1},{18,2},{19,3},{20,4},{21,5},{22,6},{23,7}} | collective-permute-start | bytes 921608 | tf_op jit(solution)/shard_map/ppermute | solution.py:577
  3.2 36.0 %collective-permute-start.1 = (bf16[200,768]{1,0:T(8,128)(2,1)}, bf16[200,768]{1,0:T(8,128)(2,1)S(1)}, u32[]{:S(2)}, u32[]{:S(2)}) collective-permute-start(bf16[200,768]{1,0:T(8,128)(2,1)} %refs_0_.1), channel_id=1, source_target_pairs={{24,0},{25,1},{26,2},{27,3},{28,4},{29,5},{30,6},{31,7}} | collective-permute-start | bytes 921608 | tf_op jit(solution)/shard_map/ppermute | solution.py:577
  32.7 31.4 %collective-permute-start.4 = (bf16[400,768]{1,0:T(8,128)(2,1)}, bf16[400,768]{1,0:T(8,128)(2,1)S(1)}, u32[]{:S(2)}, u32[]{:S(2)}) collective-permute-start(bf16[400,768]{1,0:T(8,128)(2,1)} %get-tuple-element.290.refs_0_), channel_id=1, source_target_pairs={{0,8},{1,9},{2,10},{3,11},{4,12},{5,13},{6,14},{7,15}} | collective-permute-start | bytes 1843208 | tf_op jit(solution)/shard_map/ppermute | solution.py:577
  152.2 129.0 %collective-permute-start.15 = (bf16[400,768]{1,0:T(8,128)(2,1)}, bf16[400,768]{1,0:T(8,128)(2,1)}, u32[]{:S(2)}, u32[]{:S(2)}) collective-permute-start(bf16[400,768]{1,0:T(8,128)(2,1)} %get-tuple-element.406), channel_id=1, source_target_pairs={{8,0},{9,1},{10,2},{11,3},{12,4},{13,5},{14,6},{15,7}} | collective-permute-start | bytes 1843208 | tf_op jit(solution)/shard_map/ppermute | solution.py:577
  161.6 145.2 %collective-permute-start.17 = (bf16[400,768]{1,0:T(8,128)(2,1)}, bf16[400,768]{1,0:T(8,128)(2,1)S(1)}, u32[]{:S(2)}, u32[]{:S(2)}) collective-permute-start(bf16[400,768]{1,0:T(8,128)(2,1)} %get-tuple-element.417), channel_id=1, source_target_pairs={{8,0},{9,1},{10,2},{11,3},{12,4},{13,5},{14,6},{15,7}} | collective-permute-start | bytes 1843208 | tf_op jit(solution)/shard_map/ppermute | solution.py:577
  320.6 31.9 %collective-permute-start.18 = (bf16[768,768]{1,0:T(8,128)(2,1)}, bf16[768,768]{1,0:T(8,128)(2,1)S(1)}, u32[]{:S(2)}, u32[]{:S(2)}) collective-permute-start(bf16[768,768]{1,0:T(8,128)(2,1)} %get-tuple-element.422), channel_id=1, source_target_pairs={{0,1},{1,0},{2,3},{3,2},{4,5},{5,4},{6,7},{7,6},{8,9},{9,8},{10,11... | collective-permute-start | bytes 3538952 | tf_op jit(solution)/shard_map/ppermute | solution.py:676
  322.7 26.2 %collective-permute-start.22 = (bf16[384,768]{1,0:T(8,128)(2,1)S(1)}, bf16[384,768]{1,0:T(8,128)(2,1)S(1)}, u32[]{:S(2)}, u32[]{:S(2)}) collective-permute-start(bf16[384,768]{1,0:T(8,128)(2,1)S(1)} %get-tuple-element.458), channel_id=1, source_target_pairs={{0,2},{1,3},{6,4},{7,5},{8,10},{9,11},{14,12},{15,13},{16,18},{17,... | collective-permute-start | bytes 1769480 | tf_op jit(solution)/shard_map/ppermute | solution.py:616
  324.1 25.7 %collective-permute-start.21 = (bf16[384,768]{1,0:T(8,128)(2,1)S(1)}, bf16[384,768]{1,0:T(8,128)(2,1)}, u32[]{:S(2)}, u32[]{:S(2)}) collective-permute-start(bf16[384,768]{1,0:T(8,128)(2,1)S(1)} %get-tuple-element.481), channel_id=1, source_target_pairs={{0,2},{1,3},{6,4},{7,5},{8,10},{9,11},{14,12},{15,13},{16,18},{17,... | collective-permute-start | bytes 1769480 | tf_op jit(solution)/shard_map/ppermute | solution.py:616
  364.5 41.4 %collective-permute-start.24 = (bf16[384,3072]{1,0:T(8,128)(2,1)}, bf16[384,3072]{1,0:T(8,128)(2,1)}, u32[]{:S(2)}, u32[]{:S(2)}) collective-permute-start(bf16[384,3072]{1,0:T(8,128)(2,1)} %get-tuple-element.446), channel_id=1, source_target_pairs={{0,1},{1,0},{2,3},{3,2},{4,5},{5,4},{6,7},{7,6},{8,9},{9,8},{10,11... | collective-permute-start | bytes 7077896 | tf_op jit(solution)/shard_map/ppermute | solution.py:676
  383.4 46.8 %collective-permute-start.28 = (bf16[384,768]{1,0:T(8,128)(2,1)S(1)}, bf16[384,768]{1,0:T(8,128)(2,1)}, u32[]{:S(2)}, u32[]{:S(2)}) collective-permute-start(bf16[384,768]{1,0:T(8,128)(2,1)S(1)} %add_convert_fusion.25), channel_id=1, source_target_pairs={{2,4},{3,5},{4,2},{5,3},{10,12},{11,13},{12,10},{13,11},{18,20},{1... | collective-permute-start | bytes 1769480 | tf_op jit(solution)/shard_map/ppermute | solution.py:616
  385.0 46.6 %collective-permute-start.23 = (bf16[384,768]{1,0:T(8,128)(2,1)S(1)}, bf16[384,768]{1,0:T(8,128)(2,1)}, u32[]{:S(2)}, u32[]{:S(2)}) collective-permute-start(bf16[384,768]{1,0:T(8,128)(2,1)S(1)} %add_convert_fusion.28), channel_id=1, source_target_pairs={{2,4},{3,5},{4,2},{5,3},{10,12},{11,13},{12,10},{13,11},{18,20},{1... | collective-permute-start | bytes 1769480 | tf_op jit(solution)/shard_map/ppermute | solution.py:616
  394.4 40.6 %collective-permute-start.27 = (bf16[384,2304]{1,0:T(8,128)(2,1)}, bf16[384,2304]{1,0:T(8,128)(2,1)}, u32[]{:S(2)}, u32[]{:S(2)}) collective-permute-start(bf16[384,2304]{1,0:T(8,128)(2,1)} %get-tuple-element.455), channel_id=1, source_target_pairs={{0,1},{1,0},{2,3},{3,2},{4,5},{5,4},{6,7},{7,6},{8,9},{9,8},{10,11... | collective-permute-start | bytes 5308424 | tf_op jit(solution)/shard_map/ppermute | solution.py:676
  405.1 32.0 %collective-permute-start.47 = (bf16[400,768]{1,0:T(8,128)(2,1)S(1)}, bf16[400,768]{1,0:T(8,128)(2,1)S(1)}, u32[]{:S(2)}, u32[]{:S(2)}) collective-permute-start(bf16[400,768]{1,0:T(8,128)(2,1)S(1)} %pad_maximum_fusion.6), channel_id=1, source_target_pairs={{0,1},{1,0},{2,3},{3,2},{4,5},{5,4},{6,7},{7,6},{8,9},{9,8},{10,11... | collective-permute-start | bytes 1843208 | tf_op jit(solution)/shard_map/ppermute | solution.py:676
  409.7 34.6 %collective-permute-start.43 = (bf16[384,768]{1,0:T(8,128)(2,1)S(1)}, bf16[384,768]{1,0:T(8,128)(2,1)S(1)}, u32[]{:S(2)}, u32[]{:S(2)}) collective-permute-start(bf16[384,768]{1,0:T(8,128)(2,1)S(1)} %get-tuple-element.561), channel_id=1, source_target_pairs={{0,2},{1,3},{6,4},{7,5},{2,0},{3,1},{4,6},{5,7},{8,10},{9,11},{14,... | collective-permute-start | bytes 1769480 | tf_op jit(solution)/shard_map/ppermute | solution.py:616
  433.0 35.5 %collective-permute-start.25 = (bf16[384,768]{1,0:T(8,128)(2,1)S(1)}, bf16[384,768]{1,0:T(8,128)(2,1)S(1)}, u32[]{:S(2)}, u32[]{:S(2)}) collective-permute-start(bf16[384,768]{1,0:T(8,128)(2,1)S(1)} %get-tuple-element.571), channel_id=1, source_target_pairs={{0,2},{1,3},{6,4},{7,5},{2,0},{3,1},{4,6},{5,7},{8,10},{9,11},{14,... | collective-permute-start | bytes 1769480 | tf_op jit(solution)/shard_map/ppermute | solution.py:616
  469.0 59.0 %collective-permute-start.44 = (bf16[1536,768]{1,0:T(8,128)(2,1)S(1)}, bf16[1536,768]{1,0:T(8,128)(2,1)S(1)}, u32[]{:S(2)}, u32[]{:S(2)}) collective-permute-start(bf16[1536,768]{1,0:T(8,128)(2,1)S(1)} %pad_maximum_fusion), channel_id=1, source_target_pairs={{0,1},{1,0},{2,3},{3,2},{4,5},{5,4},{6,7},{7,6},{8,9},{9,8},{10,11... | collective-permute-start | bytes 7077896 | tf_op jit(solution)/shard_map/ppermute | solution.py:616
  474.6 30.4 %collective-permute-start.34 = (bf16[384,768]{1,0:T(8,128)(2,1)S(1)}, bf16[384,768]{1,0:T(8,128)(2,1)S(1)}, u32[]{:S(2)}, u32[]{:S(2)}) collective-permute-start(bf16[384,768]{1,0:T(8,128)(2,1)S(1)} %get-tuple-element.567), channel_id=1, source_target_pairs={{0,2},{1,3},{6,4},{7,5},{2,0},{3,1},{4,6},{5,7},{8,10},{9,11},{14,... | collective-permute-start | bytes 1769480 | tf_op jit(solution)/shard_map/ppermute | solution.py:616
  506.9 25.9 %collective-permute-start.39 = (bf16[384,768]{1,0:T(8,128)(2,1)S(1)}, bf16[384,768]{1,0:T(8,128)(2,1)S(1)}, u32[]{:S(2)}, u32[]{:S(2)}) collective-permute-start(bf16[384,768]{1,0:T(8,128)(2,1)S(1)} %get-tuple-element.565), channel_id=1, source_target_pairs={{0,2},{1,3},{6,4},{7,5},{2,0},{3,1},{4,6},{5,7},{8,10},{9,11},{14,... | collective-permute-start | bytes 1769480 | tf_op jit(solution)/shard_map/ppermute | solution.py:616
  518.1 28.4 %collective-permute-start.56 = (bf16[384,768]{1,0:T(8,128)(2,1)S(1)}, bf16[384,768]{1,0:T(8,128)(2,1)S(1)}, u32[]{:S(2)}, u32[]{:S(2)}) collective-permute-start(bf16[384,768]{1,0:T(8,128)(2,1)S(1)} %get-tuple-element.559), channel_id=1, source_target_pairs={{0,2},{1,3},{6,4},{7,5},{2,0},{3,1},{4,6},{5,7},{8,10},{9,11},{14,... | collective-permute-start | bytes 1769480 | tf_op jit(solution)/shard_map/ppermute | solution.py:616
  533.9 27.2 %collective-permute-start.53 = (bf16[384,768]{1,0:T(8,128)(2,1)S(1)}, bf16[384,768]{1,0:T(8,128)(2,1)S(1)}, u32[]{:S(2)}, u32[]{:S(2)}) collective-permute-start(bf16[384,768]{1,0:T(8,128)(2,1)S(1)} %get-tuple-element.557), channel_id=1, source_target_pairs={{0,2},{1,3},{6,4},{7,5},{2,0},{3,1},{4,6},{5,7},{8,10},{9,11},{14,... | collective-permute-start | bytes 1769480 | tf_op jit(solution)/shard_map/ppermute | solution.py:616
  561.4 45.5 %collective-permute-start.57 = (bf16[384,3072]{1,0:T(8,128)(2,1)S(1)}, bf16[384,3072]{1,0:T(8,128)(2,1)S(1)}, u32[]{:S(2)}, u32[]{:S(2)}) collective-permute-start(bf16[384,3072]{1,0:T(8,128)(2,1)S(1)} %pad_maximum_fusion.1), channel_id=1, source_target_pairs={{0,1},{1,0},{2,3},{3,2},{4,5},{5,4},{6,7},{7,6},{8,9},{9,8},{10,11... | collective-permute-start | bytes 7077896 | tf_op jit(solution)/shard_map/ppermute | solution.py:616
  573.0 33.8 %collective-permute-start.51 = (bf16[400,768]{1,0:T(8,128)(2,1)S(1)}, bf16[400,768]{1,0:T(8,128)(2,1)S(1)}, u32[]{:S(2)}, u32[]{:S(2)}) collective-permute-start(bf16[400,768]{1,0:T(8,128)(2,1)S(1)} %add_convert_fusion.4), channel_id=1, source_target_pairs={{2,0},{3,1},{4,6},{5,7},{10,8},{11,9},{12,14},{13,15},{18,16},{19,... | collective-permute-start | bytes 1843208 | tf_op jit(solution)/shard_map/ppermute | solution.py:616
  574.4 32.5 %collective-permute-start.58 = (bf16[384,768]{1,0:T(8,128)(2,1)S(1)}, bf16[384,768]{1,0:T(8,128)(2,1)S(1)}, u32[]{:S(2)}, u32[]{:S(2)}) collective-permute-start(bf16[384,768]{1,0:T(8,128)(2,1)S(1)} %add_convert_fusion.8), channel_id=1, source_target_pairs={{2,4},{3,5},{4,2},{5,3},{10,12},{11,13},{12,10},{13,11},{18,20},{1... | collective-permute-start | bytes 1769480 | tf_op jit(solution)/shard_map/ppermute | solution.py:616
  575.3 41.7 %collective-permute-start.55 = (bf16[384,768]{1,0:T(8,128)(2,1)S(1)}, bf16[384,768]{1,0:T(8,128)(2,1)S(1)}, u32[]{:S(2)}, u32[]{:S(2)}) collective-permute-start(bf16[384,768]{1,0:T(8,128)(2,1)S(1)} %add_convert_fusion.10), channel_id=1, source_target_pairs={{2,0},{3,1},{4,6},{5,7},{10,8},{11,9},{12,14},{13,15},{18,16},{19,... | collective-permute-start | bytes 1769480 | tf_op jit(solution)/shard_map/ppermute | solution.py:616
  (66 other events, 670.6 us)

commit v3 on v2

--- a/solution.py
+++ b/solution.py
@@ -101,7 +101,7 @@
 
 def front_kernel(first, scal, layer, *refs):
     x_in, geo_in, cos_in, sin_in, wqkv_in, wp_in, wu_in, wd_in = refs[:8]
-    vec_in, rest = refs[8:16], refs[16:]
+    vec_in, rest = refs[8:16], refs[17:]
     if not first:
         rest = rest[len(STATES) :]
     out_ref = rest[0]
@@ -249,7 +249,7 @@
     return results[0], tuple(results[1:])
 
 
-def front_call(scal, layer, x, common, weights, vecs, states):
+def front_call(scal, layer, x, common, weights, vecs, states, earlier):
     scratch = [
         vmem(ROWS, WIDTH), vmem(1, VEC_AT[-1], dtype=f32), vmem(KEYS, 128, dtype=f32),
         vmem(ROWS, WIDTH, dtype=f32), vmem(ROWS, WIDTH, dtype=f32),
@@ -260,7 +260,7 @@
         vmem(ROWS, HIDDEN), vmem(ROWS, HIDDEN), vmem(ROWS, 128), vmem(KEYS, 128), vmem(ROWS, WIDTH),
         pltpu.SemaphoreType.DMA((36,)),
     ]
-    operands = [scal, layer, x, *common, *weights, *vecs]
+    operands = [scal, layer, x, *common, *weights, *vecs, earlier]
     out = jax.ShapeDtypeStruct((ROWS, WIDTH), bf16)
     return call_states(front_kernel, states is None, operands, 2, states, [out], STATE_SHAPES, scratch, "layer_front")
 
@@ -452,24 +452,18 @@
     return jnp.concatenate([high, (values - high.astype(f32)).astype(bf16)], axis=0)
 
 
-def tables_kernel(first, turn_ref, kind_ref, freq_in, *refs):
-    if not first:
-        refs = refs[4:]
-    geo_ref, cos_ref, sin_ref, freq_v, geo_v, cos_v, sin_v, sems = refs
-
-    @pl.when(turn_ref[0] == 1)
-    def _():
-        micro = turn_ref[1]
-        copies = Copies(sems)
-        copies.wait(copies.start(freq_in, freq_v))
-        step = lax.broadcasted_iota(jnp.int32, (32, WIDTH // 2), 0).astype(f32)
-        angles = [step * freq_v[:, at : at + WIDTH // 2] for at in (0, WIDTH // 2)]
-        waves = [split_low(jnp.concatenate([jnp.cos(angle), jnp.sin(angle)], axis=1)) for angle in angles]
-        sixteen = lax.broadcasted_iota(jnp.int32, (ROWS, 64), 1) % 32
+def tables_kernel(kind_ref, freq_in, geo_ref, cos_ref, sin_ref, freq_v, geo_v, cos_v, sin_v, sems):
+    copies = Copies(sems)
+    copies.wait(copies.start(freq_in, freq_v))
+    step = lax.broadcasted_iota(jnp.int32, (32, WIDTH // 2), 0).astype(f32)
+    angles = [step * freq_v[:, at : at + WIDTH // 2] for at in (0, WIDTH // 2)]
+    waves = [split_low(jnp.concatenate([jnp.cos(angle), jnp.sin(angle)], axis=1)) for angle in angles]
+    sixteen = lax.broadcasted_iota(jnp.int32, (ROWS, 64), 1) % 32
+    for micro in range(MICRO):
         rows = lax.broadcasted_iota(jnp.int32, (KEYS, 128), 0).astype(f32)
         lane = lax.broadcasted_iota(jnp.int32, (KEYS, 128), 1)
         patch_row, patch_col, segment, _ = places(kind_ref[micro], rows)
-        geo_v[...] = jnp.where(lane == 0, patch_row, jnp.where(lane == 1, patch_col, segment))
+        geo_v[micro] = jnp.where(lane == 0, patch_row, jnp.where(lane == 1, patch_col, segment))
         picks = [
             jnp.where(sixteen.astype(f32) == patch[:ROWS, :64], 1.0, 0.0).astype(bf16)
             for patch in (patch_row, patch_col)
@@ -486,13 +480,13 @@
         for part in range(half // 128):
             for pair in range(2):
                 at = (2 * part + pair) * 128
-                cos_v[:, at : at + 128] = spread(cosine[:, part * 128 : part * 128 + 128], pair, lane)
+                cos_v[micro, :, at : at + 128] = spread(cosine[:, part * 128 : part * 128 + 128], pair, lane)
                 values = spread(sine[:, part * 128 : part * 128 + 128], pair, lane)
-                sin_v[:, at : at + 128] = jnp.where(lane % 64 < 32, -values, values)
-        copies.start(geo_v, geo_ref.at[micro])
-        copies.start(cos_v, cos_ref.at[micro])
-        copies.start(sin_v, sin_ref.at[micro])
-        copies.finish()
+                sin_v[micro, :, at : at + 128] = jnp.where(lane % 64 < 32, -values, values)
+        copies.start(geo_v.at[micro], geo_ref.at[micro])
+        copies.start(cos_v.at[micro], cos_ref.at[micro])
+        copies.start(sin_v.at[micro], sin_ref.at[micro])
+    copies.finish()
 
 
 def spread(values, pair, lane):
@@ -502,22 +496,19 @@
     return jnp.where(lane < 32, base, jnp.where(lane < 96, by_one, by_two))
 
 
-def tables(turn, kinds, frequency, earlier=None, held=None):
-    shapes = [(KEYS, 128), (ROWS, WIDTH), (ROWS, WIDTH)]
-    first = held is None
-    operands = [turn, kinds, frequency] + ([] if first else [earlier, *held])
+def tables(kinds, frequency):
+    shapes = [(MICRO, KEYS, 128), (MICRO, ROWS, WIDTH), (MICRO, ROWS, WIDTH)]
     return pl.pallas_call(
-        partial(tables_kernel, first),
-        out_shape=[jax.ShapeDtypeStruct((MICRO,) + shape, f32) for shape in shapes],
-        in_specs=[pl.BlockSpec(memory_space=pltpu.SMEM)] * 2 + [ANY] * (len(operands) - 2),
+        tables_kernel,
+        out_shape=[jax.ShapeDtypeStruct(shape, f32) for shape in shapes],
+        in_specs=[pl.BlockSpec(memory_space=pltpu.SMEM), ANY],
         out_specs=[ANY] * 3,
         scratch_shapes=[vmem(1, WIDTH, dtype=f32)]
         + [vmem(*shape, dtype=f32) for shape in shapes]
         + [pltpu.SemaphoreType.DMA((8,))],
-        input_output_aliases={} if first else {4: 0, 5: 1, 6: 2},
         compiler_params=pltpu.CompilerParams(vmem_limit_bytes=VMEM_LIMIT),
         name="tables",
-    )(*operands)
+    )(kinds, frequency)
 
 
 def live_rows_of(kinds):
@@ -573,6 +564,49 @@
     )(core, left, right)
 
 
+SMALL_AT = (WIDTH, WIDTH, 3 * WIDTH, WIDTH, WIDTH, WIDTH, WIDTH, WIDTH, HIDDEN, WIDTH)
+SMALL_ROWS = 32
+
+
+def small_kernel(small_in, qkv_in, proj_in, up_in, down_in, low_ref, high_ref, *scratch):
+    small_v, qkv_v, proj_v, up_v, down_v, rows_v, low_v, high_v, sems = scratch
+    copies = Copies(sems)
+    for source, target in ((small_in, small_v), (qkv_in, qkv_v), (proj_in, proj_v), (up_in, up_v), (down_in, down_v)):
+        copies.start(source, target)
+    copies.finish()
+    rows_v[...] = jnp.zeros_like(rows_v)
+    small = small_v[0] + small_v[1]
+    parts = [small[2:3], small[3:4]]
+    parts += [qkv_v[0:1, at : at + WIDTH] for at in range(0, 3 * WIDTH, WIDTH)]
+    parts += [small[4:5], small[5:6], proj_v[0:1, :], small[0:1], small[1:2]]
+    parts += [up_v[0:1, at : at + WIDTH] for at in range(0, HIDDEN, WIDTH)]
+    parts += [down_v[0:1, :]]
+    for index, part in enumerate(parts):
+        rows_v[index : index + 1, :] = part
+    half = SMALL_ROWS // 2
+    low_v[...] = rows_v[:half, :].astype(bf16)
+    high_v[...] = rows_v[half:, :].astype(bf16)
+    copies.start(low_v, low_ref)
+    copies.start(high_v, high_ref)
+    copies.finish()
+
+
+def small_call(small, qkv, proj, up, down):
+    half = (SMALL_ROWS // 2, WIDTH)
+    return pl.pallas_call(
+        small_kernel,
+        out_shape=[jax.ShapeDtypeStruct(half, bf16)] * 2,
+        in_specs=[ANY] * 5,
+        out_specs=[ANY] * 2,
+        scratch_shapes=[
+            vmem(MICRO, 8, WIDTH, dtype=f32), vmem(8, 3 * WIDTH, dtype=f32), vmem(8, WIDTH, dtype=f32),
+            vmem(8, HIDDEN, dtype=f32), vmem(8, WIDTH, dtype=f32), vmem(SMALL_ROWS, WIDTH, dtype=f32),
+            vmem(*half), vmem(*half), pltpu.SemaphoreType.DMA((8,)),
+        ],
+        name="small_grads",
+    )(small, qkv, proj, up, down)
+
+
 def send(value, source, target):
     return lax.ppermute(value, "section", [(source, target)])
 
@@ -606,8 +640,6 @@
 
 
 class Relay:
-    LAG = 3
-
     def __init__(self):
         self.chunks, self.sums, self.totals = [], [], []
         self.flying, self.joined, self.clock = [], [], 0
@@ -615,13 +647,12 @@
     def start(self, value, pairs, then, keep):
         self.flying.append((self.clock, lax.ppermute(value, "dp", pairs), then, keep))
 
-    def step(self, *gate, every=False):
-        ready = [f for f in self.flying if every or f[0] + self.LAG <= self.clock]
-        self.flying = [f for f in self.flying if not (every or f[0] + self.LAG <= self.clock)]
-        even = self.clock % 2 == 0
-        fresh = self.chunks.pop(0) if even and self.chunks else None
+    def step(self, *gate, outer=0, inner=0, age=3):
+        ready = [f for f in self.flying if f[0] + age <= self.clock]
+        self.flying = [f for f in self.flying if f[0] + age > self.clock]
+        fresh, self.chunks = self.chunks[:outer], self.chunks[outer:]
         arrays, keeps = [f[1] for f in ready], [f[3] for f in ready]
-        new = [] if fresh is None else [fresh[0]]
+        new = [value for value, _ in fresh]
         joined, self.joined = self.joined, []
         results = [item.result for item in joined]
         arrays, keeps, new, gate, results = lax.optimization_barrier((arrays, keeps, new, gate, results))
@@ -629,16 +660,19 @@
             item.result = result
         for (_, _, then, _), array, keep in zip(ready, arrays, keeps):
             then(array, keep)
-        if even:
-            self.outer_step((new[0],) + fresh[1:] if fresh else None, self.totals.pop(0) if self.totals else None)
-        elif self.sums:
-            both, done = self.sums.pop(0)
-            pairs = both_cores([(1, 2), (2, 1)])
-            self.start(both, pairs, lambda array, keep: self.totals.append((added(keep, array), done)), both)
+        fresh = [(value, done) for value, (_, done) in zip(new, fresh)]
+        for _ in range(outer):
+            self.outer_start(fresh.pop(0) if fresh else None, self.totals.pop(0) if self.totals else None)
+        for _ in range(min(inner, len(self.sums))):
+            self.inner_start(*self.sums.pop(0))
         self.clock += 1
         return gate[0] if len(gate) == 1 else gate
 
-    def outer_step(self, chunk, total):
+    def inner_start(self, both, done):
+        pairs = both_cores([(1, 2), (2, 1)])
+        self.start(both, pairs, lambda array, keep: self.totals.append((added(keep, array), done)), both)
+
+    def outer_start(self, chunk, total):
         inward, outward = both_cores([(0, 1), (3, 2)]), both_cores([(1, 0), (2, 3)])
         chip = lax.axis_index("dp") // 2
         outer = (chip == 0) | (chip == 3)
@@ -664,7 +698,11 @@
 
     def finish(self):
         while self.chunks or self.sums or self.totals or self.flying:
-            self.step()
+            self.pulse()
+
+    def pulse(self, *gate):
+        most = 1 if self.chunks else 4
+        return self.step(*gate, inner=most * (self.clock % 2), outer=most * (1 - self.clock % 2))
 
 
 class LineSum:
@@ -672,9 +710,9 @@
         self.relay, self.axis, self.count = relay, axis, 0
         self.totals, self.result = {}, None
 
-    def add(self, other, mine, pieces):
+    def add(self, other, mine, ends):
         half = added(mine, lax.ppermute(other, "dp", core_swap()))
-        for chunk in jnp.split(half, pieces, axis=self.axis):
+        for chunk in jnp.split(half, ends, axis=self.axis):
             self.relay.chunks.append((chunk, partial(self.landed, self.count)))
             self.count += 1
 
@@ -696,9 +734,6 @@
     part = jnp.pad(part, ((0, -rows % count), (0, 0)))
     own = lax.psum_scatter(part, "dp", scatter_dimension=0, tiled=True)
     return lax.all_gather(own, "dp", axis=0, tiled=True)[:rows].astype(f32)
-
-
-SMALL_ROWS = 32
 
 
 def per_device(
@@ -726,9 +761,7 @@
     scal = section.astype(jnp.int32).reshape(1)
     core = (lax.axis_index("dp") % 2).astype(jnp.int32).reshape(1)
     low = core[0] == 0
-    micros = jnp.arange(MICRO, dtype=jnp.int32)
-    whole = tables(jnp.array([1, 0], jnp.int32), image_kind, rotary_freq)
-    common = tables(jnp.stack([core[0], micros[1]]), image_kind, rotary_freq, tokens, whole)
+    common = tables(image_kind, rotary_freq)
     weights = (qkv_weight[0], proj_weight[0], up_weight[0], down_weight[0])
     vecs = (
         norm_one_gain, norm_one_bias, qkv_bias, proj_bias, norm_two_gain, norm_two_bias, up_bias, down_bias,
@@ -743,25 +776,28 @@
 
     states = None
     values = [first_in[m * ROWS : (m + 1) * ROWS] for m in range(MICRO)]
+    backs, out_grads = None, None
     for layer in range(sections):
-        if layer == 2:
+        for micro in range(MICRO):
+            earlier = tokens
+            if layer == last and micro == 1:
+                fronts = dict(zip(STATES, states))
+                turned, backs = back_call(scal, turn(last, 0), grads[0], common, weights, vecs, fronts, None)
+                earlier = turned
+            out, states = front_call(scal, turn(layer, micro), values[micro], common, weights, vecs, states, earlier)
+            values[micro] = send(out, layer, layer + 1) if layer < last else out
+        if layer == 1:
             values[0], last_in = lax.optimization_barrier((values[0], last_in))
-        for micro in range(MICRO):
-            out, states = front_call(scal, turn(layer, micro), values[micro], common, weights, vecs, states)
-            if layer == 0 and micro == 0:
-                common = tables(jnp.stack([1 - core[0], micros[1]]), image_kind, rotary_freq, out, common)
-            values[micro] = send(out, layer, layer + 1) if layer < last else out
+            grads = [last_in[m * ROWS : (m + 1) * ROWS] for m in range(MICRO)]
+            out_grads = list(grads)
     fronts = dict(zip(STATES, states))
-    backs = None
-    grads = [last_in[m * ROWS : (m + 1) * ROWS] for m in range(MICRO)]
-    out_grads = list(grads)
     relay = Relay()
     sums = [LineSum(relay, axis) for axis in (1, 0, 1, 0)]
     plain = [[], [], [], []]
 
-    def to_sum(index, other, mine, pieces):
+    def to_sum(index, other, mine, ends):
         if by_line:
-            sums[index].add(other, mine, pieces)
+            sums[index].add(other, mine, ends)
         else:
             plain[index].append((jnp.where(low, mine, other), jnp.where(low, other, mine)))
 
@@ -778,51 +814,34 @@
                 all_grads = jnp.concatenate(out_grads, axis=0)
                 for offset in (0, 768):
                     other, mine, b_down = product_call(core, fronts["g"], all_grads, offset, 768)
-                    to_sum(3, other, mine, 2)
-                relay.step()
-                relay.step()
-                grads[1] = relay.step(grads[1])
-            dx, backs = back_call(scal, turn(layer, micro), grads[micro], common, weights, vecs, fronts, backs)
+                    to_sum(3, other, mine, [384])
+                grads[1] = relay.step(grads[1], outer=2)
+            if layer == last and micro == 0:
+                dx = turned
+            else:
+                dx, backs = back_call(scal, turn(layer, micro), grads[micro], common, weights, vecs, fronts, backs)
             if end:
-                dx, backs = relay.step(dx, backs, every=True)
+                values[0], values[1], dx, backs = relay.step(*values, dx, backs, outer=1, inner=1, age=1)
             grads[micro] = send(dx, layer, layer - 1) if layer > 0 else dx
-    relay.step()
-    backs = dict(zip(BACKS, relay.step(*backs)))
+    backs = dict(zip(BACKS, backs))
     other, mine, b_up = product_call(core, fronts["c"], backs["du"], 0, WIDTH // 2)
-    to_sum(2, other, mine, 4)
-    relay.step()
-    dqkv = relay.step(backs["dqkv"])
-    other, mine, b_qkv = product_call(core, fronts["a"], dqkv, 0, WIDTH // 2)
-    to_sum(0, other, mine, 3)
-    relay.step()
-    o_kept, dz, small = relay.step(fronts["o"], backs["dz"], backs["small"])
-    other, mine, b_proj = product_call(core, o_kept, dz, 0, WIDTH // 2)
-    small = jnp.sum(small, axis=0)
-    turns = small[4:6].reshape(2, HEADS, 2, 32)
-    freq = (turns[:, :, 1] - turns[:, :, 0]).reshape(-1)
-    small = jnp.concatenate(
-        [small[2], small[3], b_qkv[0], freq, b_proj[0], small[0], small[1], b_up[0], b_down[0]]
-    )
-    small = small.astype(bf16).reshape(-1, WIDTH)
-    small = jnp.pad(small, ((0, SMALL_ROWS - small.shape[0]), (0, 0)))
-    half = SMALL_ROWS // 2
-    mine = jnp.concatenate([mine, jnp.where(low, small[:half], small[half:])], axis=0)
-    other = jnp.concatenate([other, jnp.where(low, small[half:], small[:half])], axis=0)
-    to_sum(1, other, mine, 1)
-    relay.step()
-    values = relay.step(*values)
+    to_sum(2, other, mine, [768, 1536, 2304])
     final = jnp.where(live_rows > 0, jnp.concatenate(values, axis=0), bf16(0.0))
     block_out = handed_out(final, last, sections)
-    relay.step()
-    relay.step()
-    relay.step()
-    relay.step()
-    grads[0], grads[1], block_out = relay.step(*grads, block_out)
     grad_tokens = handed_out(jnp.concatenate(grads, axis=0), 0, sections)
-    relay.step()
-    relay.step()
-    relay.step()
-    grad_tokens = relay.step(grad_tokens)
+    b_up, block_out, grad_tokens, dqkv = relay.step(
+        b_up, block_out, grad_tokens, backs["dqkv"], outer=1, inner=1, age=1
+    )
+    other, mine, b_qkv = product_call(core, fronts["a"], dqkv, 0, WIDTH // 2)
+    to_sum(0, other, mine, [768, 1536])
+    b_qkv, dz, small = relay.step(b_qkv, backs["dz"], backs["small"], outer=1, inner=1, age=1)
+    other, mine, b_proj = product_call(core, fronts["o"], dz, 0, WIDTH // 2)
+    lows, highs = small_call(small, b_qkv, b_proj, b_up, b_down)
+    mine = jnp.concatenate([mine, jnp.where(low, lows, highs)], axis=0)
+    other = jnp.concatenate([other, jnp.where(low, highs, lows)], axis=0)
+    mine, other = relay.step(mine, other, outer=1, inner=1, age=1)
+    to_sum(1, other, mine, [])
+    relay.clock += relay.clock % 2
     relay.finish()
     if by_line:
         grad_qkv, grad_proj, grad_up, grad_down = (item.result for item in sums)
@@ -831,14 +850,13 @@
             summed_by_compiler(jnp.concatenate([part[side] for side in range(2) for part in parts], axis=0))
             for parts in plain
         )
-    middle = WIDTH // 2
-    small = jnp.concatenate([grad_proj[middle : middle + half], grad_proj[middle + half + middle :]], axis=0).reshape(-1)
+    middle, half = WIDTH // 2, SMALL_ROWS // 2
+    small = jnp.concatenate([grad_proj[middle : middle + half], grad_proj[middle + half + middle :]], axis=0)
     grad_proj = jnp.concatenate([grad_proj[:middle], grad_proj[middle + half : middle + half + middle]], axis=0)
-    sizes = (WIDTH, WIDTH, 3 * WIDTH, WIDTH, WIDTH, WIDTH, WIDTH, HIDDEN, WIDTH)
-    ends = np.cumsum((0,) + sizes)
-    g_one, b_one, b_qkv, freq, b_proj, g_two, b_two, b_up, b_down = (
-        small[int(ends[i]) : int(ends[i + 1])][None] for i in range(len(sizes))
-    )
+    turns = small[5:7].reshape(2, HEADS, 2, 32)
+    freq = (turns[:, :, 1] - turns[:, :, 0]).reshape(1, WIDTH)
+    g_one, b_one, b_proj, g_two, b_two, b_down = (small[i : i + 1] for i in (0, 1, 7, 8, 9, 14))
+    b_qkv, b_up = small[2:5].reshape(1, -1), small[10:14].reshape(1, -1)
     return (
         block_out, grad_tokens.astype(f32), g_one, b_one, grad_qkv[None], b_qkv, freq,
         grad_proj[None], b_proj, g_two, b_two, grad_up[None], b_up, grad_down[None], b_down,

time: 642 us -> 612 us (0.953)
  starting transfers between devices: 171 us -> 130 us
  waiting for transfers between devices: 229 us -> 245 us
  other arithmetic: 45.6 us -> 54.3 us
  Pallas kernels: 167 us -> 160 us
    ppermute x32 -> x33, starting transfers between devices: 111 us -> 59.1 us  [start(): lax.ppermute(value, 'dp', pairs)]
    ppermute x32 -> x33, waiting for transfers between devices: 102 us -> 125 us  [start(): lax.ppermute(value, 'dp', pairs)]
    ppermute x24, starting transfers between devices: 58.5 us -> 70.1 us  [send(): return lax.ppermute(value, 'section', [(source, target)])]
    ppermute x24, waiting for transfers between devices: 127 us -> 120 us  [send(): return lax.ppermute(value, 'section', [(source, target)])]
    unnamed x68 -> x60, local copies, waits for them, and re-layouts: 13 us -> 10 us
    convert_element_type x21 -> x22, other arithmetic: 11.2 us -> 13.9 us  [added(): return (one.astype(f32) + other.astype(f32)).astype(bf16)]
  transfers between devices with their start and end apart: 61 -> 62, of which waited for: 16 -> 19; matrix products, arithmetic and copies ran while one was open for 8% -> 9% of each run, Pallas kernels for 23% -> 26%
where the time goes in v3:
time: 612 us; the launch traced here: 607 us
  waiting for transfers between devices  245 us (40%)
  Pallas kernels  160 us (26%)
  starting transfers between devices  130 us (21%)
  other arithmetic  54.3 us (9%)
  local copies, waits for them, and re-layouts  15 us (2%)
    ppermute x33, waiting for transfers between devices, start(): lax.ppermute(value, 'dp', pairs)  125 us
    ppermute x24, waiting for transfers between devices, send(): return lax.ppermute(value, 'section', [(source, target)])  120 us
    pallas_call x16, Pallas kernels, call_states(): pl.pallas_call(partial(kernel, first), out_shape=list(plain_out) + state_...  119 us
    ppermute x24, starting transfers between devices, send(): return lax.ppermute(value, 'section', [(source, target)])  70.1 us
    ppermute x33, starting transfers between devices, start(): lax.ppermute(value, 'dp', pairs)  59.1 us
    pallas_call x5, Pallas kernels, product_call(): pl.pallas_call(partial(product_kernel, offset, block), out_shape=[jax.Sha...  33 us
    convert_element_type x22, other arithmetic, added(): return (one.astype(f32) + other.astype(f32)).astype(bf16)  13.9 us
    convert_element_type x4, other arithmetic, join(): self.result = jnp.concatenate([low, high], axis=0).astype(f32)  13.2 us
  transfers between devices with their start and end apart: 62, of which 19 were waited for; matrix products, arithmetic and copies ran while one was open for 9% of the time, Pallas kernels for 26%

profile of v3, /device:TPU:0, one launch (start us, length us, event | category | flops | bytes accessed | tf_op | source)
XLA Modules:
  0.0 606.6 jit_solution(4934060703521458224)
XLA Ops:
  14.7 18.6 %layer_front.8 = (bf16[400,768]{1,0:T(8,128)(2,1)}, bf16[2,400,768]{2,1,0:T(8,128)(2,1)}, bf16[2,400,768]{2,1,0:T(8,128)(2,1)}, bf16[2,400,2304]{2,1,0:T(8,128)(...) custom-call(s32[1]{0:T(128)} %bitcast.1.scal, ...), custom_call_target="tpu_custom_call" | custom-call | tf_op jit(solution)/shard_map/layer_front/pallas_call | solution.py:239
  36.1 18.8 %layer_front.9 = (bf16[400,768]{1,0:T(8,128)(2,1)}, bf16[2,400,768]{2,1,0:T(8,128)(2,1)}, bf16[2,400,768]{2,1,0:T(8,128)(2,1)}, bf16[2,400,2304]{2,1,0:T(8,128)(...) custom-call(s32[1]{0:T(128)} %bitcast.1.scal, ...), custom_call_target="tpu_custom_call", output_to_operand_aliasing={{1}: (19, {}), {2}: (20, {}), {3}: (21, {}), {4}: (22, {}),... | custom-call | tf_op jit(solution)/shard_map/layer_front/pallas_call | solution.py:239
  62.7 8.2 %collective-permute-done.3.refs_0_ = bf16[400,768]{1,0:T(8,128)(2,1)S(1)} collective-permute-done((bf16[400,768]{1,0:T(8,128)(2,1)}, bf16[400,768]{1,0:T(8,128)(2,1)S(1)}, u32[]{:S(2)}, u32[]{:S(2)}) %collective-permute-start.3) | collective-permute-done | bytes 614432 | tf_op jit(solution)/shard_map/ppermute | solution.py:611
  95.2 8.5 %layer_back.8 = (bf16[400,768]{1,0:T(8,128)(2,1)}, bf16[2,400,3072]{2,1,0:T(8,128)(2,1)}, bf16[2,400,768]{2,1,0:T(8,128)(2,1)}, bf16[2,400,2304]{2,1,0:T(8,128)(2,1)}, f32[2,8,768]{2,1,0:T(8,128)}) custom-call(s32[1]{0:T(128)} %bitcast.1.scal, s32[2]{0:T(128)} %constant.106.clone.layer, bf16[400,768]{1,0:T(8,128)(2,1)} %get-tuple-element.586.refs_0_, ...), custom_call_target="tpu_custom_call" | custom-call | tf_op jit(solution)/shard_map/layer_back/pallas_call | solution.py:239
  103.8 7.3 %collective-permute-start.12 = (bf16[400,768]{1,0:T(8,128)(2,1)}, bf16[400,768]{1,0:T(8,128)(2,1)S(1)}, u32[]{:S(2)}, u32[]{:S(2)}) collective-permute-start(bf16[400,768]{1,0:T(8,128)(2,1)} %get-tuple-element.363.refs_16_), channel_id=1, source_target_pairs={{24,16},{25,17},{26,18},{27,19},{28,20},{29,21},{30,22},{31,23}} | collective-permute-start | bytes 1843208 | tf_op jit(solution)/shard_map/ppermute | solution.py:611
  119.9 8.5 %collective-permute-start.14 = (bf16[400,768]{1,0:T(8,128)(2,1)}, bf16[400,768]{1,0:T(8,128)(2,1)S(1)}, u32[]{:S(2)}, u32[]{:S(2)}) collective-permute-start(bf16[400,768]{1,0:T(8,128)(2,1)} %get-tuple-element.385), channel_id=1, source_target_pairs={{24,16},{25,17},{26,18},{27,19},{28,20},{29,21},{30,22},{31,23}} | collective-permute-start | bytes 1843208 | tf_op jit(solution)/shard_map/ppermute | solution.py:611
  147.8 7.3 %collective-permute-start.15 = (bf16[400,768]{1,0:T(8,128)(2,1)}, bf16[400,768]{1,0:T(8,128)(2,1)}, u32[]{:S(2)}, u32[]{:S(2)}) collective-permute-start(bf16[400,768]{1,0:T(8,128)(2,1)} %get-tuple-element.394), channel_id=1, source_target_pairs={{8,0},{9,1},{10,2},{11,3},{12,4},{13,5},{14,6},{15,7}} | collective-permute-start | bytes 1843208 | tf_op jit(solution)/shard_map/ppermute | solution.py:611
  156.9 7.0 %collective-permute-start.17 = (bf16[400,768]{1,0:T(8,128)(2,1)}, bf16[400,768]{1,0:T(8,128)(2,1)S(1)}, u32[]{:S(2)}, u32[]{:S(2)}) collective-permute-start(bf16[400,768]{1,0:T(8,128)(2,1)} %get-tuple-element.405), channel_id=1, source_target_pairs={{8,0},{9,1},{10,2},{11,3},{12,4},{13,5},{14,6},{15,7}} | collective-permute-start | bytes 1843208 | tf_op jit(solution)/shard_map/ppermute | solution.py:611
  164.2 84.7 %collective-permute-done.15.refs_0_ = bf16[400,768]{1,0:T(8,128)(2,1)} collective-permute-done((bf16[400,768]{1,0:T(8,128)(2,1)}, bf16[400,768]{1,0:T(8,128)(2,1)}, u32[]{:S(2)}, u32[]{:S(2)}) %collective-permute-start.15) | collective-permute-done | bytes 614432 | tf_op jit(solution)/shard_map/ppermute | solution.py:611
  248.9 22.7 %layer_back.14 = (bf16[400,768]{1,0:T(8,128)(2,1)}, bf16[2,400,3072]{2,1,0:T(8,128)(2,1)}, bf16[2,400,768]{2,1,0:T(8,128)(2,1)}, bf16[2,400,2304]{2,1,0:T(8,128)(2,1)}, f32[2,8,768]{2,1,0:T(8,128)}) custom-call(s32[1]{0:T(128)} %bitcast.1.scal, s32[2]{0:T(128)} %call_exported.0.layer, ...), custom_call_target="tpu_custom_call", output_to_operand_aliasing={{1}: (20, {}), {2}: (21, {}), {3}: (22, {}), {4}: (23, {})} | custom-call | tf_op jit(solution)/shard_map/layer_back/pallas_call | solution.py:239
  271.6 21.4 %collective-permute-done.17.refs_0_ = bf16[400,768]{1,0:T(8,128)(2,1)S(1)} collective-permute-done((bf16[400,768]{1,0:T(8,128)(2,1)}, bf16[400,768]{1,0:T(8,128)(2,1)S(1)}, u32[]{:S(2)}, u32[]{:S(2)}) %collective-permute-start.17) | collective-permute-done | bytes 614432 | tf_op jit(solution)/shard_map/ppermute | solution.py:611
  317.8 23.0 %layer_back.15 = (bf16[400,768]{1,0:T(8,128)(2,1)}, bf16[2,400,3072]{2,1,0:T(8,128)(2,1)}, bf16[2,400,768]{2,1,0:T(8,128)(2,1)}, bf16[2,400,2304]{2,1,0:T(8,128)(2,1)}, f32[2,8,768]{2,1,0:T(8,128)}) custom-call(s32[1]{0:T(128)} %bitcast.1.scal, s32[2]{0:T(128)} %call_exported.1.layer, ...), custom_call_target="tpu_custom_call", output_to_operand_aliasing={{1}: (20, {}), {2}: (21, {}), {3}: (22, {}), {4}: (23, {})} | custom-call | tf_op jit(solution)/shard_map/layer_back/pallas_call | solution.py:239
  343.3 9.5 %weight_grad.7 = (bf16[384,3072]{1,0:T(8,128)(2,1)}, bf16[384,3072]{1,0:T(8,128)(2,1)}, f32[8,3072]{1,0:T(8,128)}) custom-call(s32[1]{0:T(128)} %bitcast.core_ref, bf16[800,768]{1,0:T(8,128)(2,1)} %bitcast.97, bf16[800,3072]{1,0:T(8,128)(2,1)} %bitcast.76), custom_call_target="tpu_custom_call" | custom-call | tf_op jit(solution)/shard_map/weight_grad/pallas_call | solution.py:553
  372.6 8.6 %collective-permute-done.22 = bf16[384,768]{1,0:T(8,128)(2,1)S(1)} collective-permute-done((bf16[384,768]{1,0:T(8,128)(2,1)S(1)}, bf16[384,768]{1,0:T(8,128)(2,1)S(1)}, u32[]{:S(2)}, u32[]{:S(2)}) %collective-permute-start.22) | collective-permute-done | bytes 589856 | tf_op jit(solution)/shard_map/ppermute | solution.py:648
  386.7 8.1 %weight_grad.8 = (bf16[384,2304]{1,0:T(8,128)(2,1)}, bf16[384,2304]{1,0:T(8,128)(2,1)}, f32[8,2304]{1,0:T(8,128)}) custom-call(s32[1]{0:T(128)} %bitcast.core_ref, bf16[800,768]{1,0:T(8,128)(2,1)} %bitcast.96, bf16[800,2304]{1,0:T(8,128)(2,1)} %bitcast.94), custom_call_target="tpu_custom_call" | custom-call | tf_op jit(solution)/shard_map/weight_grad/pallas_call | solution.py:553
  424.7 16.1 %collective-permute-done.38 = bf16[384,768]{1,0:T(8,128)(2,1)S(1)} collective-permute-done((bf16[384,768]{1,0:T(8,128)(2,1)S(1)}, bf16[384,768]{1,0:T(8,128)(2,1)S(1)}, u32[]{:S(2)}, u32[]{:S(2)}) %collective-permute-start.38) | collective-permute-done | bytes 589856 | tf_op jit(solution)/shard_map/ppermute | solution.py:648
  446.9 10.9 %collective-permute-done.42 = bf16[384,768]{1,0:T(8,128)(2,1)S(1)} collective-permute-done((bf16[384,768]{1,0:T(8,128)(2,1)S(1)}, bf16[384,768]{1,0:T(8,128)(2,1)S(1)}, u32[]{:S(2)}, u32[]{:S(2)}) %collective-permute-start.42) | collective-permute-done | bytes 589856 | tf_op jit(solution)/shard_map/ppermute | solution.py:648
  469.0 12.4 %collective-permute-start.50 = (bf16[400,768]{1,0:T(8,128)(2,1)S(1)}, bf16[400,768]{1,0:T(8,128)(2,1)S(1)}, u32[]{:S(2)}, u32[]{:S(2)}) collective-permute-start(bf16[400,768]{1,0:T(8,128)(2,1)S(1)} %add_convert_fusion.6), channel_id=1, source_target_pairs={{0,2},{1,3},{6,4},{7,5},{8,10},{9,11},{14,12},{15,13},{16,18},{17,... | collective-permute-start | bytes 1843208 | tf_op jit(solution)/shard_map/ppermute | solution.py:648
  482.8 11.4 %collective-permute-done.49 = bf16[384,768]{1,0:T(8,128)(2,1)S(1)} collective-permute-done((bf16[384,768]{1,0:T(8,128)(2,1)S(1)}, bf16[384,768]{1,0:T(8,128)(2,1)S(1)}, u32[]{:S(2)}, u32[]{:S(2)}) %collective-permute-start.49) | collective-permute-done | bytes 589856 | tf_op jit(solution)/shard_map/ppermute | solution.py:648
  508.4 10.9 %collective-permute-done.46 = bf16[384,768]{1,0:T(8,128)(2,1)S(1)} collective-permute-done((bf16[384,768]{1,0:T(8,128)(2,1)S(1)}, bf16[384,768]{1,0:T(8,128)(2,1)S(1)}, u32[]{:S(2)}, u32[]{:S(2)}) %collective-permute-start.46) | collective-permute-done | bytes 589856 | tf_op jit(solution)/shard_map/ppermute | solution.py:648
  522.9 14.7 %collective-permute-done.56 = bf16[384,768]{1,0:T(8,128)(2,1)S(1)} collective-permute-done((bf16[384,768]{1,0:T(8,128)(2,1)S(1)}, bf16[384,768]{1,0:T(8,128)(2,1)S(1)}, u32[]{:S(2)}, u32[]{:S(2)}) %collective-permute-start.56) | collective-permute-done | bytes 589856 | tf_op jit(solution)/shard_map/ppermute | solution.py:648
  548.5 21.8 %collective-permute-done.60 = bf16[384,768]{1,0:T(8,128)(2,1)S(1)} collective-permute-done((bf16[384,768]{1,0:T(8,128)(2,1)S(1)}, bf16[384,768]{1,0:T(8,128)(2,1)S(1)}, u32[]{:S(2)}, u32[]{:S(2)}) %collective-permute-start.60) | collective-permute-done | bytes 589856 | tf_op jit(solution)/shard_map/ppermute | solution.py:648
  570.3 12.6 %collective-permute-done.59 = bf16[384,768]{1,0:T(8,128)(2,1)S(1)} collective-permute-done((bf16[384,768]{1,0:T(8,128)(2,1)S(1)}, bf16[384,768]{1,0:T(8,128)(2,1)S(1)}, u32[]{:S(2)}, u32[]{:S(2)}) %collective-permute-start.59) | collective-permute-done | bytes 589856 | tf_op jit(solution)/shard_map/ppermute | solution.py:648
  583.1 11.2 %collective-permute-done.53 = bf16[400,768]{1,0:T(8,128)(2,1)S(1)} collective-permute-done((bf16[400,768]{1,0:T(8,128)(2,1)S(1)}, bf16[400,768]{1,0:T(8,128)(2,1)S(1)}, u32[]{:S(2)}, u32[]{:S(2)}) %collective-permute-start.53) | collective-permute-done | bytes 614432 | tf_op jit(solution)/shard_map/ppermute | solution.py:648
  (273 shorter events, 220.0 us)
Async XLA Ops:
  1.9 32.8 %collective-permute-start = (bf16[200,768]{1,0:T(8,128)(2,1)}, bf16[200,768]{1,0:T(8,128)(2,1)S(1)}, u32[]{:S(2)}, u32[]{:S(2)}) collective-permute-start(bf16[200,768]{1,0:T(8,128)(2,1)} %refs_16_.13), channel_id=1, source_target_pairs={{16,0},{17,1},{18,2},{19,3},{20,4},{21,5},{22,6},{23,7}} | collective-permute-start | bytes 921608 | tf_op jit(solution)/shard_map/ppermute | solution.py:611
  3.2 31.5 %collective-permute-start.1 = (bf16[200,768]{1,0:T(8,128)(2,1)}, bf16[200,768]{1,0:T(8,128)(2,1)S(1)}, u32[]{:S(2)}, u32[]{:S(2)}) collective-permute-start(bf16[200,768]{1,0:T(8,128)(2,1)} %refs_16_.13), channel_id=1, source_target_pairs={{24,0},{25,1},{26,2},{27,3},{28,4},{29,5},{30,6},{31,7}} | collective-permute-start | bytes 921608 | tf_op jit(solution)/shard_map/ppermute | solution.py:611
  33.4 26.4 %collective-permute-start.4 = (bf16[400,768]{1,0:T(8,128)(2,1)}, bf16[400,768]{1,0:T(8,128)(2,1)S(1)}, u32[]{:S(2)}, u32[]{:S(2)}) collective-permute-start(bf16[400,768]{1,0:T(8,128)(2,1)} %get-tuple-element.293), channel_id=1, source_target_pairs={{0,8},{1,9},{2,10},{3,11},{4,12},{5,13},{6,14},{7,15}} | collective-permute-start | bytes 1843208 | tf_op jit(solution)/shard_map/ppermute | solution.py:611
  147.8 101.1 %collective-permute-start.15 = (bf16[400,768]{1,0:T(8,128)(2,1)}, bf16[400,768]{1,0:T(8,128)(2,1)}, u32[]{:S(2)}, u32[]{:S(2)}) collective-permute-start(bf16[400,768]{1,0:T(8,128)(2,1)} %get-tuple-element.394), channel_id=1, source_target_pairs={{8,0},{9,1},{10,2},{11,3},{12,4},{13,5},{14,6},{15,7}} | collective-permute-start | bytes 1843208 | tf_op jit(solution)/shard_map/ppermute | solution.py:611
  156.9 136.1 %collective-permute-start.17 = (bf16[400,768]{1,0:T(8,128)(2,1)}, bf16[400,768]{1,0:T(8,128)(2,1)S(1)}, u32[]{:S(2)}, u32[]{:S(2)}) collective-permute-start(bf16[400,768]{1,0:T(8,128)(2,1)} %get-tuple-element.405), channel_id=1, source_target_pairs={{8,0},{9,1},{10,2},{11,3},{12,4},{13,5},{14,6},{15,7}} | collective-permute-start | bytes 1843208 | tf_op jit(solution)/shard_map/ppermute | solution.py:611
  306.9 34.0 %collective-permute-start.21 = (bf16[768,768]{1,0:T(8,128)(2,1)}, bf16[768,768]{1,0:T(8,128)(2,1)}, u32[]{:S(2)}, u32[]{:S(2)}) collective-permute-start(bf16[768,768]{1,0:T(8,128)(2,1)} %get-tuple-element.414), channel_id=1, source_target_pairs={{0,1},{1,0},{2,3},{3,2},{4,5},{5,4},{6,7},{7,6},{8,9},{9,8},{10,11... | collective-permute-start | bytes 3538952 | tf_op jit(solution)/shard_map/ppermute | solution.py:714
  307.7 34.7 %collective-permute-start.19 = (bf16[384,768]{1,0:T(8,128)(2,1)S(1)}, bf16[384,768]{1,0:T(8,128)(2,1)}, u32[]{:S(2)}, u32[]{:S(2)}) collective-permute-start(bf16[384,768]{1,0:T(8,128)(2,1)S(1)} %get-tuple-element.428), channel_id=1, source_target_pairs={{0,2},{1,3},{6,4},{7,5},{8,10},{9,11},{14,12},{15,13},{16,18},{17,... | collective-permute-start | bytes 1769480 | tf_op jit(solution)/shard_map/ppermute | solution.py:648
  312.0 30.5 %collective-permute-start.20 = (bf16[384,768]{1,0:T(8,128)(2,1)S(1)}, bf16[384,768]{1,0:T(8,128)(2,1)S(1)}, u32[]{:S(2)}, u32[]{:S(2)}) collective-permute-start(bf16[384,768]{1,0:T(8,128)(2,1)S(1)} %get-tuple-element.443), channel_id=1, source_target_pairs={{0,2},{1,3},{6,4},{7,5},{8,10},{9,11},{14,12},{15,13},{16,18},{17,... | collective-permute-start | bytes 1769480 | tf_op jit(solution)/shard_map/ppermute | solution.py:648
  314.1 43.3 %collective-permute-start.29 = (bf16[200,768]{1,0:T(8,128)(2,1)}, bf16[200,768]{1,0:T(8,128)(2,1)}, u32[]{:S(2)}, u32[]{:S(2)}) collective-permute-start(bf16[200,768]{1,0:T(8,128)(2,1)} %slice.91), channel_id=1, source_target_pairs={{0,8},{1,9},{2,10},{3,11},{4,12},{5,13},{6,14},{7,15}} | collective-permute-start | bytes 921608 | tf_op jit(solution)/shard_map/ppermute | solution.py:611
  352.8 42.0 %collective-permute-start.32 = (bf16[384,3072]{1,0:T(8,128)(2,1)}, bf16[384,3072]{1,0:T(8,128)(2,1)}, u32[]{:S(2)}, u32[]{:S(2)}) collective-permute-start(bf16[384,3072]{1,0:T(8,128)(2,1)} %get-tuple-element.446), channel_id=1, source_target_pairs={{0,1},{1,0},{2,3},{3,2},{4,5},{5,4},{6,7},{7,6},{8,9},{9,8},{10,11... | collective-permute-start | bytes 7077896 | tf_op jit(solution)/shard_map/ppermute | solution.py:714
  370.3 27.2 %collective-permute-start.31 = (bf16[384,768]{1,0:T(8,128)(2,1)}, bf16[384,768]{1,0:T(8,128)(2,1)}, u32[]{:S(2)}, u32[]{:S(2)}) collective-permute-start(bf16[384,768]{1,0:T(8,128)(2,1)} %add_convert_fusion.26), channel_id=1, source_target_pairs={{2,4},{3,5},{4,2},{5,3},{10,12},{11,13},{12,10},{13,11},{18,20},{1... | collective-permute-start | bytes 1769480 | tf_op jit(solution)/shard_map/ppermute | solution.py:648
  385.2 35.7 %collective-permute-start.34 = (bf16[384,768]{1,0:T(8,128)(2,1)S(1)}, bf16[384,768]{1,0:T(8,128)(2,1)}, u32[]{:S(2)}, u32[]{:S(2)}) collective-permute-start(bf16[384,768]{1,0:T(8,128)(2,1)S(1)} %add_convert_fusion.24), channel_id=1, source_target_pairs={{2,4},{3,5},{4,2},{5,3},{10,12},{11,13},{12,10},{13,11},{18,20},{1... | collective-permute-start | bytes 1769480 | tf_op jit(solution)/shard_map/ppermute | solution.py:648
  404.7 41.3 %collective-permute-start.44 = (bf16[384,768]{1,0:T(8,128)(2,1)S(1)}, bf16[384,768]{1,0:T(8,128)(2,1)}, u32[]{:S(2)}, u32[]{:S(2)}) collective-permute-start(bf16[384,768]{1,0:T(8,128)(2,1)S(1)} %get-tuple-element.493), channel_id=1, source_target_pairs={{0,2},{1,3},{6,4},{7,5},{8,10},{9,11},{14,12},{15,13},{16,18},{17,... | collective-permute-start | bytes 1769480 | tf_op jit(solution)/shard_map/ppermute | solution.py:648
  422.5 38.6 %collective-permute-start.48 = (bf16[400,768]{1,0:T(8,128)(2,1)S(1)}, bf16[400,768]{1,0:T(8,128)(2,1)S(1)}, u32[]{:S(2)}, u32[]{:S(2)}) collective-permute-start(bf16[400,768]{1,0:T(8,128)(2,1)S(1)} %pad_maximum_fusion.7), channel_id=1, source_target_pairs={{0,1},{1,0},{2,3},{3,2},{4,5},{5,4},{6,7},{7,6},{8,9},{9,8},{10,11... | collective-permute-start | bytes 1843208 | tf_op jit(solution)/shard_map/ppermute | solution.py:714
  423.8 36.3 %collective-permute-start.35 = (bf16[384,768]{1,0:T(8,128)(2,1)S(1)}, bf16[384,768]{1,0:T(8,128)(2,1)S(1)}, u32[]{:S(2)}, u32[]{:S(2)}) collective-permute-start(bf16[384,768]{1,0:T(8,128)(2,1)S(1)} %add_convert_fusion.23), channel_id=1, source_target_pairs={{2,4},{3,5},{4,2},{5,3},{10,12},{11,13},{12,10},{13,11},{18,20},{1... | collective-permute-start | bytes 1769480 | tf_op jit(solution)/shard_map/ppermute | solution.py:648
  458.0 37.8 %collective-permute-start.43 = (bf16[1536,768]{1,0:T(8,128)(2,1)S(1)}, bf16[1536,768]{1,0:T(8,128)(2,1)S(1)}, u32[]{:S(2)}, u32[]{:S(2)}) collective-permute-start(bf16[1536,768]{1,0:T(8,128)(2,1)S(1)} %pad_maximum_fusion), channel_id=1, source_target_pairs={{0,1},{1,0},{2,3},{3,2},{4,5},{5,4},{6,7},{7,6},{8,9},{9,8},{10,11... | collective-permute-start | bytes 7077896 | tf_op jit(solution)/shard_map/ppermute | solution.py:648
  460.1 35.6 %collective-permute-start.45 = (bf16[384,768]{1,0:T(8,128)(2,1)S(1)}, bf16[384,768]{1,0:T(8,128)(2,1)S(1)}, u32[]{:S(2)}, u32[]{:S(2)}) collective-permute-start(bf16[384,768]{1,0:T(8,128)(2,1)S(1)} %add_convert_fusion.16), channel_id=1, source_target_pairs={{2,4},{3,5},{4,2},{5,3},{10,12},{11,13},{12,10},{13,11},{18,20},{1... | collective-permute-start | bytes 1769480 | tf_op jit(solution)/shard_map/ppermute | solution.py:648
  467.7 26.4 %collective-permute-start.49 = (bf16[384,768]{1,0:T(8,128)(2,1)S(1)}, bf16[384,768]{1,0:T(8,128)(2,1)S(1)}, u32[]{:S(2)}, u32[]{:S(2)}) collective-permute-start(bf16[384,768]{1,0:T(8,128)(2,1)S(1)} %add_convert_fusion.13), channel_id=1, source_target_pairs={{2,0},{3,1},{4,6},{5,7},{10,8},{11,9},{12,14},{13,15},{18,16},{19,... | collective-permute-start | bytes 1769480 | tf_op jit(solution)/shard_map/ppermute | solution.py:648
  469.0 26.6 %collective-permute-start.50 = (bf16[400,768]{1,0:T(8,128)(2,1)S(1)}, bf16[400,768]{1,0:T(8,128)(2,1)S(1)}, u32[]{:S(2)}, u32[]{:S(2)}) collective-permute-start(bf16[400,768]{1,0:T(8,128)(2,1)S(1)} %add_convert_fusion.6), channel_id=1, source_target_pairs={{0,2},{1,3},{6,4},{7,5},{8,10},{9,11},{14,12},{15,13},{16,18},{17,... | collective-permute-start | bytes 1843208 | tf_op jit(solution)/shard_map/ppermute | solution.py:648
  481.7 26.6 %collective-permute-start.41 = (bf16[384,768]{1,0:T(8,128)(2,1)S(1)}, bf16[384,768]{1,0:T(8,128)(2,1)S(1)}, u32[]{:S(2)}, u32[]{:S(2)}) collective-permute-start(bf16[384,768]{1,0:T(8,128)(2,1)S(1)} %get-tuple-element.543), channel_id=1, source_target_pairs={{0,2},{1,3},{6,4},{7,5},{2,0},{3,1},{4,6},{5,7},{8,10},{9,11},{14,... | collective-permute-start | bytes 1769480 | tf_op jit(solution)/shard_map/ppermute | solution.py:648
  494.2 25.5 %collective-permute-start.55 = (bf16[384,768]{1,0:T(8,128)(2,1)S(1)}, bf16[384,768]{1,0:T(8,128)(2,1)S(1)}, u32[]{:S(2)}, u32[]{:S(2)}) collective-permute-start(bf16[384,768]{1,0:T(8,128)(2,1)S(1)} %add_convert_fusion.12), channel_id=1, source_target_pairs={{2,4},{3,5},{4,2},{5,3},{10,12},{11,13},{12,10},{13,11},{18,20},{1... | collective-permute-start | bytes 1769480 | tf_op jit(solution)/shard_map/ppermute | solution.py:648
  538.7 31.6 %collective-permute-start.60 = (bf16[384,768]{1,0:T(8,128)(2,1)S(1)}, bf16[384,768]{1,0:T(8,128)(2,1)S(1)}, u32[]{:S(2)}, u32[]{:S(2)}) collective-permute-start(bf16[384,768]{1,0:T(8,128)(2,1)S(1)} %add_convert_fusion.7), channel_id=1, source_target_pairs={{2,0},{3,1},{4,6},{5,7},{10,8},{11,9},{12,14},{13,15},{18,16},{19,... | collective-permute-start | bytes 1769480 | tf_op jit(solution)/shard_map/ppermute | solution.py:648
  540.2 42.8 %collective-permute-start.59 = (bf16[384,768]{1,0:T(8,128)(2,1)S(1)}, bf16[384,768]{1,0:T(8,128)(2,1)S(1)}, u32[]{:S(2)}, u32[]{:S(2)}) collective-permute-start(bf16[384,768]{1,0:T(8,128)(2,1)S(1)} %add_convert_fusion.8), channel_id=1, source_target_pairs={{2,0},{3,1},{4,6},{5,7},{10,8},{11,9},{12,14},{13,15},{18,16},{19,... | collective-permute-start | bytes 1769480 | tf_op jit(solution)/shard_map/ppermute | solution.py:648
  541.7 52.7 %collective-permute-start.53 = (bf16[400,768]{1,0:T(8,128)(2,1)S(1)}, bf16[400,768]{1,0:T(8,128)(2,1)S(1)}, u32[]{:S(2)}, u32[]{:S(2)}) collective-permute-start(bf16[400,768]{1,0:T(8,128)(2,1)S(1)} %add_convert_fusion.4), channel_id=1, source_target_pairs={{2,0},{3,1},{4,6},{5,7},{10,8},{11,9},{12,14},{13,15},{18,16},{19,... | collective-permute-start | bytes 1843208 | tf_op jit(solution)/shard_map/ppermute | solution.py:648
  (67 other events, 763.3 us)

commit v4 on v3

--- a/solution.py
+++ b/solution.py
@@ -121,20 +121,20 @@
             copies.start(part, vec_v.at[:, pl.ds(at, size)]) for part, at, size in zip(vec_in, VEC_AT, VEC_SIZES)
         ]
         get_geo = copies.start(geo_in.at[slot], geo_v)
-        get_qkv = [
-            copies.start(wqkv_in.at[:, pl.ds(at, WIDTH)], wqkv_v.at[:, pl.ds(at, WIDTH)])
-            for at in range(0, 3 * WIDTH, WIDTH)
-        ]
+        get_qkv = [copies.start(wqkv_in.at[:, pl.ds(0, WIDTH)], wqkv_v.at[:, pl.ds(0, WIDTH)])]
+
+        def put(source, name):
+            copies.start(source, state[name].at[slot])
+
+        qkv_v[ROWS:KEYS, :] = jnp.zeros((KEYS - ROWS, 3 * WIDTH), bf16)
+        wait(get_x, *get_vec)
         get_cos = copies.start(cos_in.at[slot], cos_v)
         get_sin = copies.start(sin_in.at[slot], sin_v)
-
-        def put(source, name):
-            copies.start(source, state[name].at[slot])
-
-        qkv_v[ROWS:KEYS, :] = jnp.zeros((KEYS - ROWS, 3 * WIDTH), bf16)
-        wait(get_x, get_geo, *get_vec)
+        for at in (WIDTH, 2 * WIDTH):
+            get_qkv.append(copies.start(wqkv_in.at[:, pl.ds(at, WIDTH)], wqkv_v.at[:, pl.ds(at, WIDTH)]))
         normed, _ = norm_parts(x_v[...].astype(f32))
         a_v[...] = (normed * vec_part(vec_v, 0) + vec_part(vec_v, 1)).astype(bf16)
+        wait(get_geo)
         segment = geo_v[:, 2:3]
         code = (lax.broadcasted_iota(jnp.int32, (KEYS, 128), 1) % 64).astype(f32)
         qcode_v[...] = jnp.where(segment[:ROWS] == code[:ROWS], 1.0, 0.0).astype(bf16)
@@ -155,30 +155,32 @@
                 acc = acc * (LOG2E / 8.0)
             qkv_v[:ROWS, at : at + WIDTH] = acc.astype(bf16)
 
-        for pair in range(PAIRS):
-            lanes = pl.ds(pair * 128, 128)
-            klanes = pl.ds(pair * 128 + WIDTH, 128)
-            vlanes = pl.ds(pair * 128 + 2 * WIDTH, 128)
-            q_two = qkv_v[:ROWS, lanes]
-            k_two = qkv_v[:, klanes]
-            v_two = qkv_v[:, vlanes]
-            lane_q = lax.broadcasted_iota(jnp.int32, (ROWS, 128), 1) // 64
-            lane_k = lax.broadcasted_iota(jnp.int32, (KEYS, 128), 1) // 64
-            for head in range(2):
-                q_one = jnp.where(lane_q == head, q_two, qcode_v[...])
-                k_one = jnp.where(lane_k == head, k_two, kcode_v[...])
-                s_v[2 * (pair % 2) + head] = lax.dot_general(q_one, k_one, NT, preferred_element_type=f32)
-            sums = []
-            for head in range(2):
-                v_one = jnp.where(lane_k == head, v_two, bf16(1.0))
-                scores = s_v[2 * (pair % 2) + head]
-                peak = jnp.max(scores, axis=1, keepdims=True)
-                e_v[2 * pair + head] = jnp.exp2(scores - peak).astype(bf16)
-                sums.append(jnp.dot(e_v[2 * pair + head], v_one, preferred_element_type=f32))
-            total = pltpu.roll(jnp.where(lane_q == 0, sums[1], sums[0]), 64, 1)
-            inverse = 1.0 / total
-            li_v[:, lanes] = inverse
-            o_v[:, lanes] = (jnp.where(lane_q == 0, sums[0], sums[1]) * inverse).astype(bf16)
+        lane_q = lax.broadcasted_iota(jnp.int32, (ROWS, 128), 1) // 64
+        lane_k = lax.broadcasted_iota(jnp.int32, (KEYS, 128), 1) // 64
+
+        def scores(index):
+            pair, head = divmod(index, 2)
+            q_one = jnp.where(lane_q == head, qkv_v[:ROWS, pair * 128 : pair * 128 + 128], qcode_v[...])
+            k_at = WIDTH + pair * 128
+            k_one = jnp.where(lane_k == head, qkv_v[:, k_at : k_at + 128], kcode_v[...])
+            s_v[index % 4] = lax.dot_general(q_one, k_one, NT, preferred_element_type=f32)
+
+        scores(0)
+        sums = []
+        for index in range(HEADS):
+            pair, head = divmod(index, 2)
+            if index + 1 < HEADS:
+                scores(index + 1)
+            v_at = 2 * WIDTH + pair * 128
+            v_one = jnp.where(lane_k == head, qkv_v[:, v_at : v_at + 128], bf16(1.0))
+            peak = jnp.max(s_v[index % 4], axis=1, keepdims=True)
+            e_v[index] = jnp.exp2(s_v[index % 4] - peak).astype(bf16)
+            sums.append(jnp.dot(e_v[index], v_one, preferred_element_type=f32))
+            if head == 1:
+                lanes = pl.ds(pair * 128, 128)
+                inverse = 1.0 / pltpu.roll(jnp.where(lane_q == 0, sums[index], sums[index - 1]), 64, 1)
+                li_v[:, lanes] = inverse
+                o_v[:, lanes] = (jnp.where(lane_q == 0, sums[index - 1], sums[index]) * inverse).astype(bf16)
         put(x_v, "x")
         put(a_v, "a")
         put(qkv_v.at[pl.ds(0, ROWS)], "qkv")
@@ -616,15 +618,21 @@
     return jnp.concatenate(pieces, axis=0)
 
 
-def handed_out(whole, source, sections):
-    section = lax.axis_index("section")
-    share = whole.shape[0] // sections
-    result = whole[source * share : (source + 1) * share]
-    for target in range(sections):
-        if target != source:
-            piece = send(whole[target * share : (target + 1) * share], source, target)
-            result = jnp.where(section == target, piece, result)
-    return result
+def handed_out(output, grads, sections):
+    section, last = lax.axis_index("section"), sections - 1
+    share = output.shape[0] // sections
+
+    def rows(whole, target):
+        return whole[target * share : (target + 1) * share]
+
+    output_share, grad_share = rows(output, last), rows(grads, 0)
+    for target in range(last):
+        mirror = last - target
+        piece = jnp.where(section == last, rows(output, target), rows(grads, mirror))
+        piece = lax.ppermute(piece, "section", [(last, target), (0, mirror)])
+        output_share = jnp.where(section == target, piece, output_share)
+        grad_share = jnp.where(section == mirror, piece, grad_share)
+    return output_share, grad_share
 
 
 def added(one, other):
@@ -644,12 +652,12 @@
         self.chunks, self.sums, self.totals = [], [], []
         self.flying, self.joined, self.clock = [], [], 0
 
-    def start(self, value, pairs, then, keep):
-        self.flying.append((self.clock, lax.ppermute(value, "dp", pairs), then, keep))
-
-    def step(self, *gate, outer=0, inner=0, age=3):
-        ready = [f for f in self.flying if f[0] + age <= self.clock]
-        self.flying = [f for f in self.flying if f[0] + age > self.clock]
+    def start(self, value, pairs, then, keep, age, chunk=False):
+        self.flying.append((self.clock + age, lax.ppermute(value, "dp", pairs), then, keep, chunk))
+
+    def step(self, *gate, outer=0, inner=0, ahead=0):
+        ready = [f for f in self.flying if f[0] <= self.clock + ahead]
+        self.flying = [f for f in self.flying if f[0] > self.clock + ahead]
         fresh, self.chunks = self.chunks[:outer], self.chunks[outer:]
         arrays, keeps = [f[1] for f in ready], [f[3] for f in ready]
         new = [value for value, _ in fresh]
@@ -658,7 +666,7 @@
         arrays, keeps, new, gate, results = lax.optimization_barrier((arrays, keeps, new, gate, results))
         for item, result in zip(joined, results):
             item.result = result
-        for (_, _, then, _), array, keep in zip(ready, arrays, keeps):
+        for (_, _, then, _, _), array, keep in zip(ready, arrays, keeps):
             then(array, keep)
         fresh = [(value, done) for value, (_, done) in zip(new, fresh)]
         for _ in range(outer):
@@ -670,7 +678,7 @@
 
     def inner_start(self, both, done):
         pairs = both_cores([(1, 2), (2, 1)])
-        self.start(both, pairs, lambda array, keep: self.totals.append((added(keep, array), done)), both)
+        self.start(both, pairs, lambda array, keep: self.totals.append((added(keep, array), done)), both, 2)
 
     def outer_start(self, chunk, total):
         inward, outward = both_cores([(0, 1), (3, 2)]), both_cores([(1, 0), (2, 3)])
@@ -689,20 +697,23 @@
                 result(array, keep[1])
 
             value = jnp.where(outer, chunk[0], total[0])
-            self.start(value, inward + outward, land, (chunk[0], total[0]))
+            self.start(value, inward + outward, land, (chunk[0], total[0]), 3, True)
         else:
             if total:
-                self.start(total[0], outward, result, total[0])
+                self.start(total[0], outward, result, total[0], 3 if self.chunks or chunk else 8)
             if chunk:
-                self.start(chunk[0], inward, inner_sum, chunk[0])
+                self.start(chunk[0], inward, inner_sum, chunk[0], 3, True)
 
     def finish(self):
-        while self.chunks or self.sums or self.totals or self.flying:
+        while self.chunks:
             self.pulse()
+        while any(flight[0] > self.clock - 1 and flight[4] for flight in self.flying):
+            self.step(outer=4, inner=4)
+        while self.sums or self.totals or self.flying:
+            self.step(outer=4, inner=4, ahead=9)
 
     def pulse(self, *gate):
-        most = 1 if self.chunks else 4
-        return self.step(*gate, inner=most * (self.clock % 2), outer=most * (1 - self.clock % 2))
+        return self.step(*gate, inner=self.clock % 2, outer=1 - self.clock % 2)
 
 
 class LineSum:
@@ -720,7 +731,7 @@
         self.totals[index] = total
         if len(self.totals) == self.count:
             mine = jnp.concatenate([self.totals[i] for i in range(self.count)], axis=self.axis)
-            self.relay.start(mine, core_swap(), self.join, mine)
+            self.relay.start(mine, core_swap(), self.join, mine, 2)
 
     def join(self, other, mine):
         core = lax.axis_index("dp") % 2
@@ -821,25 +832,23 @@
             else:
                 dx, backs = back_call(scal, turn(layer, micro), grads[micro], common, weights, vecs, fronts, backs)
             if end:
-                values[0], values[1], dx, backs = relay.step(*values, dx, backs, outer=1, inner=1, age=1)
+                values[0], values[1], dx, backs = relay.step(*values, dx, backs, outer=1, inner=1, ahead=9)
             grads[micro] = send(dx, layer, layer - 1) if layer > 0 else dx
     backs = dict(zip(BACKS, backs))
     other, mine, b_up = product_call(core, fronts["c"], backs["du"], 0, WIDTH // 2)
     to_sum(2, other, mine, [768, 1536, 2304])
     final = jnp.where(live_rows > 0, jnp.concatenate(values, axis=0), bf16(0.0))
-    block_out = handed_out(final, last, sections)
-    grad_tokens = handed_out(jnp.concatenate(grads, axis=0), 0, sections)
+    block_out, grad_tokens = handed_out(final, jnp.concatenate(grads, axis=0), sections)
     b_up, block_out, grad_tokens, dqkv = relay.step(
-        b_up, block_out, grad_tokens, backs["dqkv"], outer=1, inner=1, age=1
+        b_up, block_out, grad_tokens, backs["dqkv"], outer=1, inner=1, ahead=9
     )
     other, mine, b_qkv = product_call(core, fronts["a"], dqkv, 0, WIDTH // 2)
     to_sum(0, other, mine, [768, 1536])
-    b_qkv, dz, small = relay.step(b_qkv, backs["dz"], backs["small"], outer=1, inner=1, age=1)
-    other, mine, b_proj = product_call(core, fronts["o"], dz, 0, WIDTH // 2)
-    lows, highs = small_call(small, b_qkv, b_proj, b_up, b_down)
+    other, mine, b_proj = product_call(core, fronts["o"], backs["dz"], 0, WIDTH // 2)
+    lows, highs = small_call(backs["small"], b_qkv, b_proj, b_up, b_down)
     mine = jnp.concatenate([mine, jnp.where(low, lows, highs)], axis=0)
     other = jnp.concatenate([other, jnp.where(low, highs, lows)], axis=0)
-    mine, other = relay.step(mine, other, outer=1, inner=1, age=1)
+    other, mine = relay.step(other, mine, outer=1, inner=1, ahead=9)
     to_sum(1, other, mine, [])
     relay.clock += relay.clock % 2
     relay.finish()

time: 612 us -> 594 us (0.971)
  waiting for transfers between devices: 245 us -> 227 us
    ppermute x33, waiting for transfers between devices: 125 us -> 110 us  [start(): lax.ppermute(value, 'dp', pairs)]
    ppermute x24 -> x18, starting transfers between devices: 70.1 us -> 56.3 us  [send(): return lax.ppermute(value, 'section', [(source, target)])]
    ppermute x33, starting transfers between devices: 59.1 us -> 71.9 us  [start(): lax.ppermute(value, 'dp', pairs)]
    ppermute x0 -> x3, starting transfers between devices: none -> 6.8 us  [handed_out(): piece = lax.ppermute(piece, 'section', [(last, target), (0, mirror)])]
    ppermute x24 -> x18, waiting for transfers between devices: 120 us -> 115 us  [send(): return lax.ppermute(value, 'section', [(source, target)])]
  transfers between devices with their start and end apart: 62 -> 59, of which waited for: 19 -> 18; matrix products, arithmetic and copies ran while one was open for 9% -> 8% of each run, Pallas kernels for 26% -> 24%
where the time goes in v4:
time: 594 us; the launch traced here: 588 us
  waiting for transfers between devices  227 us (38%)
  Pallas kernels  157 us (26%)
  starting transfers between devices  136 us (23%)
  other arithmetic  52.3 us (9%)
  local copies, waits for them, and re-layouts  14.3 us (2%)
    pallas_call x16, Pallas kernels, call_states(): pl.pallas_call(partial(kernel, first), out_shape=list(plain_out) + state_...  116 us
    ppermute x18, waiting for transfers between devices, send(): return lax.ppermute(value, 'section', [(source, target)])  115 us
    ppermute x33, waiting for transfers between devices, start(): lax.ppermute(value, 'dp', pairs)  110 us
    ppermute x33, starting transfers between devices, start(): lax.ppermute(value, 'dp', pairs)  71.9 us
    ppermute x18, starting transfers between devices, send(): return lax.ppermute(value, 'section', [(source, target)])  56.3 us
    pallas_call x5, Pallas kernels, product_call(): pl.pallas_call(partial(product_kernel, offset, block), out_shape=[jax.Sha...  33 us
    convert_element_type x4, other arithmetic, join(): self.result = jnp.concatenate([low, high], axis=0).astype(f32)  13.1 us
    convert_element_type x22, other arithmetic, added(): return (one.astype(f32) + other.astype(f32)).astype(bf16)  13.1 us
  transfers between devices with their start and end apart: 59, of which 18 were waited for; matrix products, arithmetic and copies ran while one was open for 8% of the time, Pallas kernels for 24%

profile of v4, /device:TPU:0, one launch (start us, length us, event | category | flops | bytes accessed | tf_op | source)
XLA Modules:
  0.0 588.3 jit_solution(2064506950474554379)
XLA Ops:
  14.7 17.4 %layer_front.8 = (bf16[400,768]{1,0:T(8,128)(2,1)}, bf16[2,400,768]{2,1,0:T(8,128)(2,1)}, bf16[2,400,768]{2,1,0:T(8,128)(2,1)}, bf16[2,400,2304]{2,1,0:T(8,128)(...) custom-call(s32[1]{0:T(128)} %bitcast.1.scal, ...), custom_call_target="tpu_custom_call" | custom-call | tf_op jit(solution)/shard_map/layer_front/pallas_call | solution.py:241
  34.9 17.6 %layer_front.9 = (bf16[400,768]{1,0:T(8,128)(2,1)}, bf16[2,400,768]{2,1,0:T(8,128)(2,1)}, bf16[2,400,768]{2,1,0:T(8,128)(2,1)}, bf16[2,400,2304]{2,1,0:T(8,128)(...) custom-call(s32[1]{0:T(128)} %bitcast.1.scal, ...), custom_call_target="tpu_custom_call", output_to_operand_aliasing={{1}: (19, {}), {2}: (20, {}), {3}: (21, {}), {4}: (22, {}),... | custom-call | tf_op jit(solution)/shard_map/layer_front/pallas_call | solution.py:241
  60.2 8.2 %collective-permute-done.3.refs_0_ = bf16[400,768]{1,0:T(8,128)(2,1)S(1)} collective-permute-done((bf16[400,768]{1,0:T(8,128)(2,1)}, bf16[400,768]{1,0:T(8,128)(2,1)S(1)}, u32[]{:S(2)}, u32[]{:S(2)}) %collective-permute-start.3) | collective-permute-done | bytes 614432 | tf_op jit(solution)/shard_map/ppermute | solution.py:613
  91.7 8.5 %layer_back.8 = (bf16[400,768]{1,0:T(8,128)(2,1)}, bf16[2,400,3072]{2,1,0:T(8,128)(2,1)}, bf16[2,400,768]{2,1,0:T(8,128)(2,1)}, bf16[2,400,2304]{2,1,0:T(8,128)(2,1)}, f32[2,8,768]{2,1,0:T(8,128)}) custom-call(s32[1]{0:T(128)} %bitcast.1.scal, s32[2]{0:T(128)} %constant.106.clone.layer, bf16[400,768]{1,0:T(8,128)(2,1)} %get-tuple-element.576.refs_0_, ...), custom_call_target="tpu_custom_call" | custom-call | tf_op jit(solution)/shard_map/layer_back/pallas_call | solution.py:241
  100.3 7.0 %collective-permute-start.12 = (bf16[400,768]{1,0:T(8,128)(2,1)}, bf16[400,768]{1,0:T(8,128)(2,1)S(1)}, u32[]{:S(2)}, u32[]{:S(2)}) collective-permute-start(bf16[400,768]{1,0:T(8,128)(2,1)} %get-tuple-element.358.refs_16_), channel_id=1, source_target_pairs={{24,16},{25,17},{26,18},{27,19},{28,20},{29,21},{30,22},{31,23}} | collective-permute-start | bytes 1843208 | tf_op jit(solution)/shard_map/ppermute | solution.py:613
  116.1 8.5 %collective-permute-start.14 = (bf16[400,768]{1,0:T(8,128)(2,1)}, bf16[400,768]{1,0:T(8,128)(2,1)S(1)}, u32[]{:S(2)}, u32[]{:S(2)}) collective-permute-start(bf16[400,768]{1,0:T(8,128)(2,1)} %get-tuple-element.380), channel_id=1, source_target_pairs={{24,16},{25,17},{26,18},{27,19},{28,20},{29,21},{30,22},{31,23}} | collective-permute-start | bytes 1843208 | tf_op jit(solution)/shard_map/ppermute | solution.py:613
  143.9 7.3 %collective-permute-start.15 = (bf16[400,768]{1,0:T(8,128)(2,1)}, bf16[400,768]{1,0:T(8,128)(2,1)}, u32[]{:S(2)}, u32[]{:S(2)}) collective-permute-start(bf16[400,768]{1,0:T(8,128)(2,1)} %get-tuple-element.389), channel_id=1, source_target_pairs={{8,0},{9,1},{10,2},{11,3},{12,4},{13,5},{14,6},{15,7}} | collective-permute-start | bytes 1843208 | tf_op jit(solution)/shard_map/ppermute | solution.py:613
  153.1 7.0 %collective-permute-start.17 = (bf16[400,768]{1,0:T(8,128)(2,1)}, bf16[400,768]{1,0:T(8,128)(2,1)S(1)}, u32[]{:S(2)}, u32[]{:S(2)}) collective-permute-start(bf16[400,768]{1,0:T(8,128)(2,1)} %get-tuple-element.400), channel_id=1, source_target_pairs={{8,0},{9,1},{10,2},{11,3},{12,4},{13,5},{14,6},{15,7}} | collective-permute-start | bytes 1843208 | tf_op jit(solution)/shard_map/ppermute | solution.py:613
  160.3 83.7 %collective-permute-done.15.refs_0_ = bf16[400,768]{1,0:T(8,128)(2,1)} collective-permute-done((bf16[400,768]{1,0:T(8,128)(2,1)}, bf16[400,768]{1,0:T(8,128)(2,1)}, u32[]{:S(2)}, u32[]{:S(2)}) %collective-permute-start.15) | collective-permute-done | bytes 614432 | tf_op jit(solution)/shard_map/ppermute | solution.py:613
  244.0 22.7 %layer_back.14 = (bf16[400,768]{1,0:T(8,128)(2,1)}, bf16[2,400,3072]{2,1,0:T(8,128)(2,1)}, bf16[2,400,768]{2,1,0:T(8,128)(2,1)}, bf16[2,400,2304]{2,1,0:T(8,128)(2,1)}, f32[2,8,768]{2,1,0:T(8,128)}) custom-call(s32[1]{0:T(128)} %bitcast.1.scal, s32[2]{0:T(128)} %call_exported.0.layer, ...), custom_call_target="tpu_custom_call", output_to_operand_aliasing={{1}: (20, {}), {2}: (21, {}), {3}: (22, {}), {4}: (23, {})} | custom-call | tf_op jit(solution)/shard_map/layer_back/pallas_call | solution.py:241
  266.7 20.1 %collective-permute-done.17.refs_0_ = bf16[400,768]{1,0:T(8,128)(2,1)S(1)} collective-permute-done((bf16[400,768]{1,0:T(8,128)(2,1)}, bf16[400,768]{1,0:T(8,128)(2,1)S(1)}, u32[]{:S(2)}, u32[]{:S(2)}) %collective-permute-start.17) | collective-permute-done | bytes 614432 | tf_op jit(solution)/shard_map/ppermute | solution.py:613
  306.8 23.0 %layer_back.15 = (bf16[400,768]{1,0:T(8,128)(2,1)}, bf16[2,400,3072]{2,1,0:T(8,128)(2,1)}, bf16[2,400,768]{2,1,0:T(8,128)(2,1)}, bf16[2,400,2304]{2,1,0:T(8,128)(2,1)}, f32[2,8,768]{2,1,0:T(8,128)}) custom-call(s32[1]{0:T(128)} %bitcast.1.scal, s32[2]{0:T(128)} %call_exported.1.layer, ...), custom_call_target="tpu_custom_call", output_to_operand_aliasing={{1}: (20, {}), {2}: (21, {}), {3}: (22, {}), {4}: (23, {})} | custom-call | tf_op jit(solution)/shard_map/layer_back/pallas_call | solution.py:241
  331.5 9.6 %weight_grad.7 = (bf16[384,3072]{1,0:T(8,128)(2,1)}, bf16[384,3072]{1,0:T(8,128)(2,1)}, f32[8,3072]{1,0:T(8,128)}) custom-call(s32[1]{0:T(128)} %bitcast.core_ref, bf16[800,768]{1,0:T(8,128)(2,1)} %bitcast.97, bf16[800,3072]{1,0:T(8,128)(2,1)} %bitcast.76), custom_call_target="tpu_custom_call" | custom-call | tf_op jit(solution)/shard_map/weight_grad/pallas_call | solution.py:555
  349.4 7.2 %collective-permute-start.22 = (bf16[384,768]{1,0:T(8,128)(2,1)S(1)}, bf16[384,768]{1,0:T(8,128)(2,1)}, u32[]{:S(2)}, u32[]{:S(2)}) collective-permute-start(bf16[384,768]{1,0:T(8,128)(2,1)S(1)} %get-tuple-element.460), channel_id=1, source_target_pairs={{0,2},{1,3},{6,4},{7,5},{8,10},{9,11},{14,12},{15,13},{16,18},{17,... | collective-permute-start | bytes 1769480 | tf_op jit(solution)/shard_map/ppermute | solution.py:656
  377.4 7.9 %weight_grad.8 = (bf16[384,2304]{1,0:T(8,128)(2,1)}, bf16[384,2304]{1,0:T(8,128)(2,1)}, f32[8,2304]{1,0:T(8,128)}) custom-call(s32[1]{0:T(128)} %bitcast.core_ref, bf16[800,768]{1,0:T(8,128)(2,1)} %bitcast.96, bf16[800,2304]{1,0:T(8,128)(2,1)} %bitcast.94), custom_call_target="tpu_custom_call" | custom-call | tf_op jit(solution)/shard_map/weight_grad/pallas_call | solution.py:555
  403.8 8.1 %collective-permute-done.31 = bf16[384,768]{1,0:T(8,128)(2,1)S(1)} collective-permute-done((bf16[384,768]{1,0:T(8,128)(2,1)S(1)}, bf16[384,768]{1,0:T(8,128)(2,1)S(1)}, u32[]{:S(2)}, u32[]{:S(2)}) %collective-permute-start.31) | collective-permute-done | bytes 589856 | tf_op jit(solution)/shard_map/ppermute | solution.py:656
  437.2 9.7 %collective-permute-done.38 = bf16[384,768]{1,0:T(8,128)(2,1)S(1)} collective-permute-done((bf16[384,768]{1,0:T(8,128)(2,1)S(1)}, bf16[384,768]{1,0:T(8,128)(2,1)S(1)}, u32[]{:S(2)}, u32[]{:S(2)}) %collective-permute-start.38) | collective-permute-done | bytes 589856 | tf_op jit(solution)/shard_map/ppermute | solution.py:656
  456.8 13.2 %collective-permute-start.45 = (bf16[384,768]{1,0:T(8,128)(2,1)S(1)}, bf16[384,768]{1,0:T(8,128)(2,1)S(1)}, u32[]{:S(2)}, u32[]{:S(2)}) collective-permute-start(bf16[384,768]{1,0:T(8,128)(2,1)S(1)} %get-tuple-element.531), channel_id=1, source_target_pairs={{0,2},{1,3},{6,4},{7,5},{2,0},{3,1},{4,6},{5,7},{8,10},{9,11},{14,... | collective-permute-start | bytes 1769480 | tf_op jit(solution)/shard_map/ppermute | solution.py:656
  486.5 10.3 %collective-permute-done.42 = bf16[384,768]{1,0:T(8,128)(2,1)S(1)} collective-permute-done((bf16[384,768]{1,0:T(8,128)(2,1)S(1)}, bf16[384,768]{1,0:T(8,128)(2,1)S(1)}, u32[]{:S(2)}, u32[]{:S(2)}) %collective-permute-start.42) | collective-permute-done | bytes 589856 | tf_op jit(solution)/shard_map/ppermute | solution.py:656
  498.1 7.7 %collective-permute-done.49 = bf16[400,768]{1,0:T(8,128)(2,1)S(1)} collective-permute-done((bf16[400,768]{1,0:T(8,128)(2,1)S(1)}, bf16[400,768]{1,0:T(8,128)(2,1)S(1)}, u32[]{:S(2)}, u32[]{:S(2)}) %collective-permute-start.49) | collective-permute-done | bytes 614432 | tf_op jit(solution)/shard_map/ppermute | solution.py:656
  511.7 23.1 %collective-permute-done.44 = bf16[384,768]{1,0:T(8,128)(2,1)S(1)} collective-permute-done((bf16[384,768]{1,0:T(8,128)(2,1)S(1)}, bf16[384,768]{1,0:T(8,128)(2,1)S(1)}, u32[]{:S(2)}, u32[]{:S(2)}) %collective-permute-start.44) | collective-permute-done | bytes 589856 | tf_op jit(solution)/shard_map/ppermute | solution.py:656
  534.8 12.6 %collective-permute-done.54 = bf16[384,768]{1,0:T(8,128)(2,1)S(1)} collective-permute-done((bf16[384,768]{1,0:T(8,128)(2,1)S(1)}, bf16[384,768]{1,0:T(8,128)(2,1)S(1)}, u32[]{:S(2)}, u32[]{:S(2)}) %collective-permute-start.54) | collective-permute-done | bytes 589856 | tf_op jit(solution)/shard_map/ppermute | solution.py:656
  547.4 12.4 %collective-permute-done.53 = bf16[384,768]{1,0:T(8,128)(2,1)S(1)} collective-permute-done((bf16[384,768]{1,0:T(8,128)(2,1)S(1)}, bf16[384,768]{1,0:T(8,128)(2,1)S(1)}, u32[]{:S(2)}, u32[]{:S(2)}) %collective-permute-start.53) | collective-permute-done | bytes 589856 | tf_op jit(solution)/shard_map/ppermute | solution.py:656
  568.0 11.5 %collective-permute-done.57 = bf16[400,768]{1,0:T(8,128)(2,1)S(1)} collective-permute-done((bf16[400,768]{1,0:T(8,128)(2,1)S(1)}, bf16[400,768]{1,0:T(8,128)(2,1)S(1)}, u32[]{:S(2)}, u32[]{:S(2)}) %collective-permute-start.57) | collective-permute-done | bytes 614432 | tf_op jit(solution)/shard_map/ppermute | solution.py:656
  (256 shorter events, 221.5 us)
Async XLA Ops:
  1.9 31.5 %collective-permute-start = (bf16[200,768]{1,0:T(8,128)(2,1)}, bf16[200,768]{1,0:T(8,128)(2,1)S(1)}, u32[]{:S(2)}, u32[]{:S(2)}) collective-permute-start(bf16[200,768]{1,0:T(8,128)(2,1)} %refs_16_.13), channel_id=1, source_target_pairs={{16,0},{17,1},{18,2},{19,3},{20,4},{21,5},{22,6},{23,7}} | collective-permute-start | bytes 921608 | tf_op jit(solution)/shard_map/ppermute | solution.py:613
  3.2 30.2 %collective-permute-start.1 = (bf16[200,768]{1,0:T(8,128)(2,1)}, bf16[200,768]{1,0:T(8,128)(2,1)S(1)}, u32[]{:S(2)}, u32[]{:S(2)}) collective-permute-start(bf16[200,768]{1,0:T(8,128)(2,1)} %refs_16_.13), channel_id=1, source_target_pairs={{24,0},{25,1},{26,2},{27,3},{28,4},{29,5},{30,6},{31,7}} | collective-permute-start | bytes 921608 | tf_op jit(solution)/shard_map/ppermute | solution.py:613
  32.1 25.1 %collective-permute-start.4 = (bf16[400,768]{1,0:T(8,128)(2,1)}, bf16[400,768]{1,0:T(8,128)(2,1)S(1)}, u32[]{:S(2)}, u32[]{:S(2)}) collective-permute-start(bf16[400,768]{1,0:T(8,128)(2,1)} %get-tuple-element.288), channel_id=1, source_target_pairs={{0,8},{1,9},{2,10},{3,11},{4,12},{5,13},{6,14},{7,15}} | collective-permute-start | bytes 1843208 | tf_op jit(solution)/shard_map/ppermute | solution.py:613
  100.3 24.4 %collective-permute-start.12 = (bf16[400,768]{1,0:T(8,128)(2,1)}, bf16[400,768]{1,0:T(8,128)(2,1)S(1)}, u32[]{:S(2)}, u32[]{:S(2)}) collective-permute-start(bf16[400,768]{1,0:T(8,128)(2,1)} %get-tuple-element.358.refs_16_), channel_id=1, source_target_pairs={{24,16},{25,17},{26,18},{27,19},{28,20},{29,21},{30,22},{31,23}} | collective-permute-start | bytes 1843208 | tf_op jit(solution)/shard_map/ppermute | solution.py:613
  143.9 100.1 %collective-permute-start.15 = (bf16[400,768]{1,0:T(8,128)(2,1)}, bf16[400,768]{1,0:T(8,128)(2,1)}, u32[]{:S(2)}, u32[]{:S(2)}) collective-permute-start(bf16[400,768]{1,0:T(8,128)(2,1)} %get-tuple-element.389), channel_id=1, source_target_pairs={{8,0},{9,1},{10,2},{11,3},{12,4},{13,5},{14,6},{15,7}} | collective-permute-start | bytes 1843208 | tf_op jit(solution)/shard_map/ppermute | solution.py:613
  153.1 133.7 %collective-permute-start.17 = (bf16[400,768]{1,0:T(8,128)(2,1)}, bf16[400,768]{1,0:T(8,128)(2,1)S(1)}, u32[]{:S(2)}, u32[]{:S(2)}) collective-permute-start(bf16[400,768]{1,0:T(8,128)(2,1)} %get-tuple-element.400), channel_id=1, source_target_pairs={{8,0},{9,1},{10,2},{11,3},{12,4},{13,5},{14,6},{15,7}} | collective-permute-start | bytes 1843208 | tf_op jit(solution)/shard_map/ppermute | solution.py:613
  300.7 29.2 %collective-permute-start.21 = (bf16[768,768]{1,0:T(8,128)(2,1)}, bf16[768,768]{1,0:T(8,128)(2,1)}, u32[]{:S(2)}, u32[]{:S(2)}) collective-permute-start(bf16[768,768]{1,0:T(8,128)(2,1)} %get-tuple-element.409), channel_id=1, source_target_pairs={{0,1},{1,0},{2,3},{3,2},{4,5},{5,4},{6,7},{7,6},{8,9},{9,8},{10,11... | collective-permute-start | bytes 3538952 | tf_op jit(solution)/shard_map/ppermute | solution.py:725
  301.5 30.0 %collective-permute-start.19 = (bf16[384,768]{1,0:T(8,128)(2,1)S(1)}, bf16[384,768]{1,0:T(8,128)(2,1)}, u32[]{:S(2)}, u32[]{:S(2)}) collective-permute-start(bf16[384,768]{1,0:T(8,128)(2,1)S(1)} %get-tuple-element.423), channel_id=1, source_target_pairs={{0,2},{1,3},{6,4},{7,5},{8,10},{9,11},{14,12},{15,13},{16,18},{17,... | collective-permute-start | bytes 1769480 | tf_op jit(solution)/shard_map/ppermute | solution.py:656
  305.4 26.1 %collective-permute-start.20 = (bf16[384,768]{1,0:T(8,128)(2,1)S(1)}, bf16[384,768]{1,0:T(8,128)(2,1)S(1)}, u32[]{:S(2)}, u32[]{:S(2)}) collective-permute-start(bf16[384,768]{1,0:T(8,128)(2,1)S(1)} %get-tuple-element.442), channel_id=1, source_target_pairs={{0,2},{1,3},{6,4},{7,5},{8,10},{9,11},{14,12},{15,13},{16,18},{17,... | collective-permute-start | bytes 1769480 | tf_op jit(solution)/shard_map/ppermute | solution.py:656
  341.1 48.9 %collective-permute-start.30 = (bf16[384,3072]{1,0:T(8,128)(2,1)}, bf16[384,3072]{1,0:T(8,128)(2,1)}, u32[]{:S(2)}, u32[]{:S(2)}) collective-permute-start(bf16[384,3072]{1,0:T(8,128)(2,1)} %get-tuple-element.445), channel_id=1, source_target_pairs={{0,1},{1,0},{2,3},{3,2},{4,5},{5,4},{6,7},{7,6},{8,9},{9,8},{10,11... | collective-permute-start | bytes 7077896 | tf_op jit(solution)/shard_map/ppermute | solution.py:725
  347.9 24.3 %collective-permute-start.23 = (bf16[384,768]{1,0:T(8,128)(2,1)}, bf16[384,768]{1,0:T(8,128)(2,1)}, u32[]{:S(2)}, u32[]{:S(2)}) collective-permute-start(bf16[384,768]{1,0:T(8,128)(2,1)} %add_convert_fusion.28), channel_id=1, source_target_pairs={{2,4},{3,5},{4,2},{5,3},{10,12},{11,13},{12,10},{13,11},{18,20},{1... | collective-permute-start | bytes 1769480 | tf_op jit(solution)/shard_map/ppermute | solution.py:656
  367.8 25.7 %collective-permute-start.29 = (bf16[384,768]{1,0:T(8,128)(2,1)}, bf16[384,768]{1,0:T(8,128)(2,1)}, u32[]{:S(2)}, u32[]{:S(2)}) collective-permute-start(bf16[384,768]{1,0:T(8,128)(2,1)} %add_convert_fusion.26), channel_id=1, source_target_pairs={{2,4},{3,5},{4,2},{5,3},{10,12},{11,13},{12,10},{13,11},{18,20},{1... | collective-permute-start | bytes 1769480 | tf_op jit(solution)/shard_map/ppermute | solution.py:656
  375.8 28.1 %collective-permute-start.32 = (bf16[384,768]{1,0:T(8,128)(2,1)S(1)}, bf16[384,768]{1,0:T(8,128)(2,1)}, u32[]{:S(2)}, u32[]{:S(2)}) collective-permute-start(bf16[384,768]{1,0:T(8,128)(2,1)S(1)} %add_convert_fusion.24), channel_id=1, source_target_pairs={{2,4},{3,5},{4,2},{5,3},{10,12},{11,13},{12,10},{13,11},{18,20},{1... | collective-permute-start | bytes 1769480 | tf_op jit(solution)/shard_map/ppermute | solution.py:656
  399.0 25.6 %collective-permute-start.36 = (bf16[384,768]{1,0:T(8,128)(2,1)S(1)}, bf16[384,768]{1,0:T(8,128)(2,1)S(1)}, u32[]{:S(2)}, u32[]{:S(2)}) collective-permute-start(bf16[384,768]{1,0:T(8,128)(2,1)S(1)} %get-tuple-element.476), channel_id=1, source_target_pairs={{0,2},{1,3},{6,4},{7,5},{8,10},{9,11},{14,12},{15,13},{16,18},{17,... | collective-permute-start | bytes 1769480 | tf_op jit(solution)/shard_map/ppermute | solution.py:656
  403.7 43.6 %collective-permute-start.27 = (bf16[384,2304]{1,0:T(8,128)(2,1)S(1)}, bf16[384,2304]{1,0:T(8,128)(2,1)S(1)}, u32[]{:S(2)}, u32[]{:S(2)}) collective-permute-start(bf16[384,2304]{1,0:T(8,128)(2,1)S(1)} %copy-done.24), channel_id=1, source_target_pairs={{0,1},{1,0},{2,3},{3,2},{4,5},{5,4},{6,7},{7,6},{8,9},{9,8},{10,11... | collective-permute-start | bytes 5308424 | tf_op jit(solution)/shard_map/ppermute | solution.py:725
  455.6 23.1 %collective-permute-start.48 = (bf16[400,768]{1,0:T(8,128)(2,1)S(1)}, bf16[400,768]{1,0:T(8,128)(2,1)S(1)}, u32[]{:S(2)}, u32[]{:S(2)}) collective-permute-start(bf16[400,768]{1,0:T(8,128)(2,1)S(1)} %pad_maximum_fusion.6), channel_id=1, source_target_pairs={{0,1},{1,0},{2,3},{3,2},{4,5},{5,4},{6,7},{7,6},{8,9},{9,8},{10,11... | collective-permute-start | bytes 1843208 | tf_op jit(solution)/shard_map/ppermute | solution.py:725
  455.8 25.1 %collective-permute-start.46 = (bf16[384,768]{1,0:T(8,128)(2,1)S(1)}, bf16[384,768]{1,0:T(8,128)(2,1)S(1)}, u32[]{:S(2)}, u32[]{:S(2)}) collective-permute-start(bf16[384,768]{1,0:T(8,128)(2,1)S(1)} %add_convert_fusion.12), channel_id=1, source_target_pairs={{2,4},{3,5},{4,2},{5,3},{10,12},{11,13},{12,10},{13,11},{18,20},{1... | collective-permute-start | bytes 1769480 | tf_op jit(solution)/shard_map/ppermute | solution.py:656
  456.8 27.4 %collective-permute-start.45 = (bf16[384,768]{1,0:T(8,128)(2,1)S(1)}, bf16[384,768]{1,0:T(8,128)(2,1)S(1)}, u32[]{:S(2)}, u32[]{:S(2)}) collective-permute-start(bf16[384,768]{1,0:T(8,128)(2,1)S(1)} %get-tuple-element.531), channel_id=1, source_target_pairs={{0,2},{1,3},{6,4},{7,5},{2,0},{3,1},{4,6},{5,7},{8,10},{9,11},{14,... | collective-permute-start | bytes 1769480 | tf_op jit(solution)/shard_map/ppermute | solution.py:656
  478.9 26.9 %collective-permute-start.49 = (bf16[400,768]{1,0:T(8,128)(2,1)S(1)}, bf16[400,768]{1,0:T(8,128)(2,1)S(1)}, u32[]{:S(2)}, u32[]{:S(2)}) collective-permute-start(bf16[400,768]{1,0:T(8,128)(2,1)S(1)} %add_convert_fusion.6), channel_id=1, source_target_pairs={{0,2},{1,3},{6,4},{7,5},{8,10},{9,11},{14,12},{15,13},{16,18},{17,... | collective-permute-start | bytes 1843208 | tf_op jit(solution)/shard_map/ppermute | solution.py:656
  506.4 53.5 %collective-permute-start.52 = (bf16[384,3072]{1,0:T(8,128)(2,1)S(1)}, bf16[384,3072]{1,0:T(8,128)(2,1)S(1)}, u32[]{:S(2)}, u32[]{:S(2)}) collective-permute-start(bf16[384,3072]{1,0:T(8,128)(2,1)S(1)} %pad_maximum_fusion.1), channel_id=1, source_target_pairs={{0,1},{1,0},{2,3},{3,2},{4,5},{5,4},{6,7},{7,6},{8,9},{9,8},{10,11... | collective-permute-start | bytes 7077896 | tf_op jit(solution)/shard_map/ppermute | solution.py:656
  506.6 28.2 %collective-permute-start.44 = (bf16[384,768]{1,0:T(8,128)(2,1)S(1)}, bf16[384,768]{1,0:T(8,128)(2,1)S(1)}, u32[]{:S(2)}, u32[]{:S(2)}) collective-permute-start(bf16[384,768]{1,0:T(8,128)(2,1)S(1)} %add_convert_fusion.14), channel_id=1, source_target_pairs={{2,0},{3,1},{4,6},{5,7},{10,8},{11,9},{12,14},{13,15},{18,16},{19,... | collective-permute-start | bytes 1769480 | tf_op jit(solution)/shard_map/ppermute | solution.py:656
  508.1 51.8 %collective-permute-start.55 = (bf16[400,768]{1,0:T(8,128)(2,1)S(1)}, bf16[400,768]{1,0:T(8,128)(2,1)S(1)}, u32[]{:S(2)}, u32[]{:S(2)}) collective-permute-start(bf16[400,768]{1,0:T(8,128)(2,1)S(1)} %add_convert_fusion.5), channel_id=1, source_target_pairs={{2,4},{3,5},{4,2},{5,3},{10,12},{11,13},{12,10},{13,11},{18,20},{1... | collective-permute-start | bytes 1843208 | tf_op jit(solution)/shard_map/ppermute | solution.py:656
  508.9 38.5 %collective-permute-start.54 = (bf16[384,768]{1,0:T(8,128)(2,1)S(1)}, bf16[384,768]{1,0:T(8,128)(2,1)S(1)}, u32[]{:S(2)}, u32[]{:S(2)}) collective-permute-start(bf16[384,768]{1,0:T(8,128)(2,1)S(1)} %add_convert_fusion.7), channel_id=1, source_target_pairs={{2,0},{3,1},{4,6},{5,7},{10,8},{11,9},{12,14},{13,15},{18,16},{19,... | collective-permute-start | bytes 1769480 | tf_op jit(solution)/shard_map/ppermute | solution.py:656
  510.4 49.5 %collective-permute-start.53 = (bf16[384,768]{1,0:T(8,128)(2,1)S(1)}, bf16[384,768]{1,0:T(8,128)(2,1)S(1)}, u32[]{:S(2)}, u32[]{:S(2)}) collective-permute-start(bf16[384,768]{1,0:T(8,128)(2,1)S(1)} %add_convert_fusion.8), channel_id=1, source_target_pairs={{2,0},{3,1},{4,6},{5,7},{10,8},{11,9},{12,14},{13,15},{18,16},{19,... | collective-permute-start | bytes 1769480 | tf_op jit(solution)/shard_map/ppermute | solution.py:656
  (60 other events, 722.8 us)

commit v5 on v4

--- a/solution.py
+++ b/solution.py
@@ -711,6 +711,7 @@
             self.step(outer=4, inner=4)
         while self.sums or self.totals or self.flying:
             self.step(outer=4, inner=4, ahead=9)
+            self.step(outer=4, inner=4, ahead=2)
 
     def pulse(self, *gate):
         return self.step(*gate, inner=self.clock % 2, outer=1 - self.clock % 2)

time: 594 us -> 591 us (level)
  transfers between devices with their start and end apart: 59 -> 59, of which waited for: 18 -> 19; matrix products, arithmetic and copies ran while one was open for 8% -> 8% of each run, Pallas kernels for 24% -> 24%
where the time goes in v5:
time: 591 us; the launch traced here: 586 us
  waiting for transfers between devices  224 us (38%)
  Pallas kernels  157 us (27%)
  starting transfers between devices  136 us (23%)
  other arithmetic  52.3 us (9%)
  local copies, waits for them, and re-layouts  14.3 us (2%)
    pallas_call x16, Pallas kernels, call_states(): pl.pallas_call(partial(kernel, first), out_shape=list(plain_out) + state_...  116 us
    ppermute x18, waiting for transfers between devices, send(): return lax.ppermute(value, 'section', [(source, target)])  115 us
    ppermute x33, waiting for transfers between devices, start(): lax.ppermute(value, 'dp', pairs)  108 us
    ppermute x33, starting transfers between devices, start(): lax.ppermute(value, 'dp', pairs)  71.9 us
    ppermute x18, starting transfers between devices, send(): return lax.ppermute(value, 'section', [(source, target)])  56.3 us
    pallas_call x5, Pallas kernels, product_call(): pl.pallas_call(partial(product_kernel, offset, block), out_shape=[jax.Sha...  33 us
    convert_element_type x4, other arithmetic, join(): self.result = jnp.concatenate([low, high], axis=0).astype(f32)  13.1 us
    convert_element_type x22, other arithmetic, added(): return (one.astype(f32) + other.astype(f32)).astype(bf16)  13.1 us
  transfers between devices with their start and end apart: 59, of which 19 were waited for; matrix products, arithmetic and copies ran while one was open for 8% of the time, Pallas kernels for 24%

profile of v5, /device:TPU:0, one launch (start us, length us, event | category | flops | bytes accessed | tf_op | source)
XLA Modules:
  0.0 585.7 jit_solution(5642136965436682693)
XLA Ops:
  14.7 17.4 %layer_front.8 = (bf16[400,768]{1,0:T(8,128)(2,1)}, bf16[2,400,768]{2,1,0:T(8,128)(2,1)}, bf16[2,400,768]{2,1,0:T(8,128)(2,1)}, bf16[2,400,2304]{2,1,0:T(8,128)(...) custom-call(s32[1]{0:T(128)} %bitcast.1.scal, ...), custom_call_target="tpu_custom_call" | custom-call | tf_op jit(solution)/shard_map/layer_front/pallas_call | solution.py:241
  34.9 17.6 %layer_front.9 = (bf16[400,768]{1,0:T(8,128)(2,1)}, bf16[2,400,768]{2,1,0:T(8,128)(2,1)}, bf16[2,400,768]{2,1,0:T(8,128)(2,1)}, bf16[2,400,2304]{2,1,0:T(8,128)(...) custom-call(s32[1]{0:T(128)} %bitcast.1.scal, ...), custom_call_target="tpu_custom_call", output_to_operand_aliasing={{1}: (19, {}), {2}: (20, {}), {3}: (21, {}), {4}: (22, {}),... | custom-call | tf_op jit(solution)/shard_map/layer_front/pallas_call | solution.py:241
  60.2 8.2 %collective-permute-done.3.refs_0_ = bf16[400,768]{1,0:T(8,128)(2,1)S(1)} collective-permute-done((bf16[400,768]{1,0:T(8,128)(2,1)}, bf16[400,768]{1,0:T(8,128)(2,1)S(1)}, u32[]{:S(2)}, u32[]{:S(2)}) %collective-permute-start.3) | collective-permute-done | bytes 614432 | tf_op jit(solution)/shard_map/ppermute | solution.py:613
  91.7 8.5 %layer_back.8 = (bf16[400,768]{1,0:T(8,128)(2,1)}, bf16[2,400,3072]{2,1,0:T(8,128)(2,1)}, bf16[2,400,768]{2,1,0:T(8,128)(2,1)}, bf16[2,400,2304]{2,1,0:T(8,128)(2,1)}, f32[2,8,768]{2,1,0:T(8,128)}) custom-call(s32[1]{0:T(128)} %bitcast.1.scal, s32[2]{0:T(128)} %constant.106.clone.layer, bf16[400,768]{1,0:T(8,128)(2,1)} %get-tuple-element.576.refs_0_, ...), custom_call_target="tpu_custom_call" | custom-call | tf_op jit(solution)/shard_map/layer_back/pallas_call | solution.py:241
  100.3 7.0 %collective-permute-start.12 = (bf16[400,768]{1,0:T(8,128)(2,1)}, bf16[400,768]{1,0:T(8,128)(2,1)S(1)}, u32[]{:S(2)}, u32[]{:S(2)}) collective-permute-start(bf16[400,768]{1,0:T(8,128)(2,1)} %get-tuple-element.358.refs_16_), channel_id=1, source_target_pairs={{24,16},{25,17},{26,18},{27,19},{28,20},{29,21},{30,22},{31,23}} | collective-permute-start | bytes 1843208 | tf_op jit(solution)/shard_map/ppermute | solution.py:613
  116.1 8.5 %collective-permute-start.14 = (bf16[400,768]{1,0:T(8,128)(2,1)}, bf16[400,768]{1,0:T(8,128)(2,1)S(1)}, u32[]{:S(2)}, u32[]{:S(2)}) collective-permute-start(bf16[400,768]{1,0:T(8,128)(2,1)} %get-tuple-element.380), channel_id=1, source_target_pairs={{24,16},{25,17},{26,18},{27,19},{28,20},{29,21},{30,22},{31,23}} | collective-permute-start | bytes 1843208 | tf_op jit(solution)/shard_map/ppermute | solution.py:613
  143.9 7.3 %collective-permute-start.15 = (bf16[400,768]{1,0:T(8,128)(2,1)}, bf16[400,768]{1,0:T(8,128)(2,1)}, u32[]{:S(2)}, u32[]{:S(2)}) collective-permute-start(bf16[400,768]{1,0:T(8,128)(2,1)} %get-tuple-element.389), channel_id=1, source_target_pairs={{8,0},{9,1},{10,2},{11,3},{12,4},{13,5},{14,6},{15,7}} | collective-permute-start | bytes 1843208 | tf_op jit(solution)/shard_map/ppermute | solution.py:613
  153.1 7.0 %collective-permute-start.17 = (bf16[400,768]{1,0:T(8,128)(2,1)}, bf16[400,768]{1,0:T(8,128)(2,1)S(1)}, u32[]{:S(2)}, u32[]{:S(2)}) collective-permute-start(bf16[400,768]{1,0:T(8,128)(2,1)} %get-tuple-element.400), channel_id=1, source_target_pairs={{8,0},{9,1},{10,2},{11,3},{12,4},{13,5},{14,6},{15,7}} | collective-permute-start | bytes 1843208 | tf_op jit(solution)/shard_map/ppermute | solution.py:613
  160.3 83.7 %collective-permute-done.15.refs_0_ = bf16[400,768]{1,0:T(8,128)(2,1)} collective-permute-done((bf16[400,768]{1,0:T(8,128)(2,1)}, bf16[400,768]{1,0:T(8,128)(2,1)}, u32[]{:S(2)}, u32[]{:S(2)}) %collective-permute-start.15) | collective-permute-done | bytes 614432 | tf_op jit(solution)/shard_map/ppermute | solution.py:613
  244.0 22.7 %layer_back.14 = (bf16[400,768]{1,0:T(8,128)(2,1)}, bf16[2,400,3072]{2,1,0:T(8,128)(2,1)}, bf16[2,400,768]{2,1,0:T(8,128)(2,1)}, bf16[2,400,2304]{2,1,0:T(8,128)(2,1)}, f32[2,8,768]{2,1,0:T(8,128)}) custom-call(s32[1]{0:T(128)} %bitcast.1.scal, s32[2]{0:T(128)} %call_exported.0.layer, ...), custom_call_target="tpu_custom_call", output_to_operand_aliasing={{1}: (20, {}), {2}: (21, {}), {3}: (22, {}), {4}: (23, {})} | custom-call | tf_op jit(solution)/shard_map/layer_back/pallas_call | solution.py:241
  266.7 20.1 %collective-permute-done.17.refs_0_ = bf16[400,768]{1,0:T(8,128)(2,1)S(1)} collective-permute-done((bf16[400,768]{1,0:T(8,128)(2,1)}, bf16[400,768]{1,0:T(8,128)(2,1)S(1)}, u32[]{:S(2)}, u32[]{:S(2)}) %collective-permute-start.17) | collective-permute-done | bytes 614432 | tf_op jit(solution)/shard_map/ppermute | solution.py:613
  306.8 23.0 %layer_back.15 = (bf16[400,768]{1,0:T(8,128)(2,1)}, bf16[2,400,3072]{2,1,0:T(8,128)(2,1)}, bf16[2,400,768]{2,1,0:T(8,128)(2,1)}, bf16[2,400,2304]{2,1,0:T(8,128)(2,1)}, f32[2,8,768]{2,1,0:T(8,128)}) custom-call(s32[1]{0:T(128)} %bitcast.1.scal, s32[2]{0:T(128)} %call_exported.1.layer, ...), custom_call_target="tpu_custom_call", output_to_operand_aliasing={{1}: (20, {}), {2}: (21, {}), {3}: (22, {}), {4}: (23, {})} | custom-call | tf_op jit(solution)/shard_map/layer_back/pallas_call | solution.py:241
  331.5 9.6 %weight_grad.7 = (bf16[384,3072]{1,0:T(8,128)(2,1)}, bf16[384,3072]{1,0:T(8,128)(2,1)}, f32[8,3072]{1,0:T(8,128)}) custom-call(s32[1]{0:T(128)} %bitcast.core_ref, bf16[800,768]{1,0:T(8,128)(2,1)} %bitcast.97, bf16[800,3072]{1,0:T(8,128)(2,1)} %bitcast.76), custom_call_target="tpu_custom_call" | custom-call | tf_op jit(solution)/shard_map/weight_grad/pallas_call | solution.py:555
  349.4 7.2 %collective-permute-start.22 = (bf16[384,768]{1,0:T(8,128)(2,1)S(1)}, bf16[384,768]{1,0:T(8,128)(2,1)}, u32[]{:S(2)}, u32[]{:S(2)}) collective-permute-start(bf16[384,768]{1,0:T(8,128)(2,1)S(1)} %get-tuple-element.460), channel_id=1, source_target_pairs={{0,2},{1,3},{6,4},{7,5},{8,10},{9,11},{14,12},{15,13},{16,18},{17,... | collective-permute-start | bytes 1769480 | tf_op jit(solution)/shard_map/ppermute | solution.py:656
  377.4 7.9 %weight_grad.8 = (bf16[384,2304]{1,0:T(8,128)(2,1)}, bf16[384,2304]{1,0:T(8,128)(2,1)}, f32[8,2304]{1,0:T(8,128)}) custom-call(s32[1]{0:T(128)} %bitcast.core_ref, bf16[800,768]{1,0:T(8,128)(2,1)} %bitcast.96, bf16[800,2304]{1,0:T(8,128)(2,1)} %bitcast.94), custom_call_target="tpu_custom_call" | custom-call | tf_op jit(solution)/shard_map/weight_grad/pallas_call | solution.py:555
  403.8 8.1 %collective-permute-done.31 = bf16[384,768]{1,0:T(8,128)(2,1)S(1)} collective-permute-done((bf16[384,768]{1,0:T(8,128)(2,1)S(1)}, bf16[384,768]{1,0:T(8,128)(2,1)S(1)}, u32[]{:S(2)}, u32[]{:S(2)}) %collective-permute-start.31) | collective-permute-done | bytes 589856 | tf_op jit(solution)/shard_map/ppermute | solution.py:656
  437.2 9.7 %collective-permute-done.38 = bf16[384,768]{1,0:T(8,128)(2,1)S(1)} collective-permute-done((bf16[384,768]{1,0:T(8,128)(2,1)S(1)}, bf16[384,768]{1,0:T(8,128)(2,1)S(1)}, u32[]{:S(2)}, u32[]{:S(2)}) %collective-permute-start.38) | collective-permute-done | bytes 589856 | tf_op jit(solution)/shard_map/ppermute | solution.py:656
  456.8 13.2 %collective-permute-start.45 = (bf16[384,768]{1,0:T(8,128)(2,1)S(1)}, bf16[384,768]{1,0:T(8,128)(2,1)S(1)}, u32[]{:S(2)}, u32[]{:S(2)}) collective-permute-start(bf16[384,768]{1,0:T(8,128)(2,1)S(1)} %get-tuple-element.531), channel_id=1, source_target_pairs={{0,2},{1,3},{6,4},{7,5},{2,0},{3,1},{4,6},{5,7},{8,10},{9,11},{14,... | collective-permute-start | bytes 1769480 | tf_op jit(solution)/shard_map/ppermute | solution.py:656
  486.5 10.3 %collective-permute-done.42 = bf16[384,768]{1,0:T(8,128)(2,1)S(1)} collective-permute-done((bf16[384,768]{1,0:T(8,128)(2,1)S(1)}, bf16[384,768]{1,0:T(8,128)(2,1)S(1)}, u32[]{:S(2)}, u32[]{:S(2)}) %collective-permute-start.42) | collective-permute-done | bytes 589856 | tf_op jit(solution)/shard_map/ppermute | solution.py:656
  498.1 7.7 %collective-permute-done.49 = bf16[400,768]{1,0:T(8,128)(2,1)S(1)} collective-permute-done((bf16[400,768]{1,0:T(8,128)(2,1)S(1)}, bf16[400,768]{1,0:T(8,128)(2,1)S(1)}, u32[]{:S(2)}, u32[]{:S(2)}) %collective-permute-start.49) | collective-permute-done | bytes 614432 | tf_op jit(solution)/shard_map/ppermute | solution.py:656
  511.7 23.1 %collective-permute-done.44 = bf16[384,768]{1,0:T(8,128)(2,1)S(1)} collective-permute-done((bf16[384,768]{1,0:T(8,128)(2,1)S(1)}, bf16[384,768]{1,0:T(8,128)(2,1)S(1)}, u32[]{:S(2)}, u32[]{:S(2)}) %collective-permute-start.44) | collective-permute-done | bytes 589856 | tf_op jit(solution)/shard_map/ppermute | solution.py:656
  534.8 12.6 %collective-permute-done.54 = bf16[384,768]{1,0:T(8,128)(2,1)S(1)} collective-permute-done((bf16[384,768]{1,0:T(8,128)(2,1)S(1)}, bf16[384,768]{1,0:T(8,128)(2,1)S(1)}, u32[]{:S(2)}, u32[]{:S(2)}) %collective-permute-start.54) | collective-permute-done | bytes 589856 | tf_op jit(solution)/shard_map/ppermute | solution.py:656
  547.4 12.4 %collective-permute-done.53 = bf16[384,768]{1,0:T(8,128)(2,1)S(1)} collective-permute-done((bf16[384,768]{1,0:T(8,128)(2,1)S(1)}, bf16[384,768]{1,0:T(8,128)(2,1)S(1)}, u32[]{:S(2)}, u32[]{:S(2)}) %collective-permute-start.53) | collective-permute-done | bytes 589856 | tf_op jit(solution)/shard_map/ppermute | solution.py:656
  570.8 7.8 %collective-permute-done.56 = bf16[400,768]{1,0:T(8,128)(2,1)S(1)} collective-permute-done((bf16[400,768]{1,0:T(8,128)(2,1)S(1)}, bf16[400,768]{1,0:T(8,128)(2,1)S(1)}, u32[]{:S(2)}, u32[]{:S(2)}) %collective-permute-start.56) | collective-permute-done | bytes 614432 | tf_op jit(solution)/shard_map/ppermute | solution.py:656
  (256 shorter events, 222.7 us)
Async XLA Ops:
  1.9 31.5 %collective-permute-start = (bf16[200,768]{1,0:T(8,128)(2,1)}, bf16[200,768]{1,0:T(8,128)(2,1)S(1)}, u32[]{:S(2)}, u32[]{:S(2)}) collective-permute-start(bf16[200,768]{1,0:T(8,128)(2,1)} %refs_16_.13), channel_id=1, source_target_pairs={{16,0},{17,1},{18,2},{19,3},{20,4},{21,5},{22,6},{23,7}} | collective-permute-start | bytes 921608 | tf_op jit(solution)/shard_map/ppermute | solution.py:613
  3.2 30.2 %collective-permute-start.1 = (bf16[200,768]{1,0:T(8,128)(2,1)}, bf16[200,768]{1,0:T(8,128)(2,1)S(1)}, u32[]{:S(2)}, u32[]{:S(2)}) collective-permute-start(bf16[200,768]{1,0:T(8,128)(2,1)} %refs_16_.13), channel_id=1, source_target_pairs={{24,0},{25,1},{26,2},{27,3},{28,4},{29,5},{30,6},{31,7}} | collective-permute-start | bytes 921608 | tf_op jit(solution)/shard_map/ppermute | solution.py:613
  32.1 25.1 %collective-permute-start.4 = (bf16[400,768]{1,0:T(8,128)(2,1)}, bf16[400,768]{1,0:T(8,128)(2,1)S(1)}, u32[]{:S(2)}, u32[]{:S(2)}) collective-permute-start(bf16[400,768]{1,0:T(8,128)(2,1)} %get-tuple-element.288), channel_id=1, source_target_pairs={{0,8},{1,9},{2,10},{3,11},{4,12},{5,13},{6,14},{7,15}} | collective-permute-start | bytes 1843208 | tf_op jit(solution)/shard_map/ppermute | solution.py:613
  100.3 24.4 %collective-permute-start.12 = (bf16[400,768]{1,0:T(8,128)(2,1)}, bf16[400,768]{1,0:T(8,128)(2,1)S(1)}, u32[]{:S(2)}, u32[]{:S(2)}) collective-permute-start(bf16[400,768]{1,0:T(8,128)(2,1)} %get-tuple-element.358.refs_16_), channel_id=1, source_target_pairs={{24,16},{25,17},{26,18},{27,19},{28,20},{29,21},{30,22},{31,23}} | collective-permute-start | bytes 1843208 | tf_op jit(solution)/shard_map/ppermute | solution.py:613
  143.9 100.1 %collective-permute-start.15 = (bf16[400,768]{1,0:T(8,128)(2,1)}, bf16[400,768]{1,0:T(8,128)(2,1)}, u32[]{:S(2)}, u32[]{:S(2)}) collective-permute-start(bf16[400,768]{1,0:T(8,128)(2,1)} %get-tuple-element.389), channel_id=1, source_target_pairs={{8,0},{9,1},{10,2},{11,3},{12,4},{13,5},{14,6},{15,7}} | collective-permute-start | bytes 1843208 | tf_op jit(solution)/shard_map/ppermute | solution.py:613
  153.1 133.7 %collective-permute-start.17 = (bf16[400,768]{1,0:T(8,128)(2,1)}, bf16[400,768]{1,0:T(8,128)(2,1)S(1)}, u32[]{:S(2)}, u32[]{:S(2)}) collective-permute-start(bf16[400,768]{1,0:T(8,128)(2,1)} %get-tuple-element.400), channel_id=1, source_target_pairs={{8,0},{9,1},{10,2},{11,3},{12,4},{13,5},{14,6},{15,7}} | collective-permute-start | bytes 1843208 | tf_op jit(solution)/shard_map/ppermute | solution.py:613
  300.7 29.2 %collective-permute-start.21 = (bf16[768,768]{1,0:T(8,128)(2,1)}, bf16[768,768]{1,0:T(8,128)(2,1)}, u32[]{:S(2)}, u32[]{:S(2)}) collective-permute-start(bf16[768,768]{1,0:T(8,128)(2,1)} %get-tuple-element.409), channel_id=1, source_target_pairs={{0,1},{1,0},{2,3},{3,2},{4,5},{5,4},{6,7},{7,6},{8,9},{9,8},{10,11... | collective-permute-start | bytes 3538952 | tf_op jit(solution)/shard_map/ppermute | solution.py:726
  301.5 30.0 %collective-permute-start.19 = (bf16[384,768]{1,0:T(8,128)(2,1)S(1)}, bf16[384,768]{1,0:T(8,128)(2,1)}, u32[]{:S(2)}, u32[]{:S(2)}) collective-permute-start(bf16[384,768]{1,0:T(8,128)(2,1)S(1)} %get-tuple-element.423), channel_id=1, source_target_pairs={{0,2},{1,3},{6,4},{7,5},{8,10},{9,11},{14,12},{15,13},{16,18},{17,... | collective-permute-start | bytes 1769480 | tf_op jit(solution)/shard_map/ppermute | solution.py:656
  305.4 26.1 %collective-permute-start.20 = (bf16[384,768]{1,0:T(8,128)(2,1)S(1)}, bf16[384,768]{1,0:T(8,128)(2,1)S(1)}, u32[]{:S(2)}, u32[]{:S(2)}) collective-permute-start(bf16[384,768]{1,0:T(8,128)(2,1)S(1)} %get-tuple-element.442), channel_id=1, source_target_pairs={{0,2},{1,3},{6,4},{7,5},{8,10},{9,11},{14,12},{15,13},{16,18},{17,... | collective-permute-start | bytes 1769480 | tf_op jit(solution)/shard_map/ppermute | solution.py:656
  341.1 48.9 %collective-permute-start.30 = (bf16[384,3072]{1,0:T(8,128)(2,1)}, bf16[384,3072]{1,0:T(8,128)(2,1)}, u32[]{:S(2)}, u32[]{:S(2)}) collective-permute-start(bf16[384,3072]{1,0:T(8,128)(2,1)} %get-tuple-element.445), channel_id=1, source_target_pairs={{0,1},{1,0},{2,3},{3,2},{4,5},{5,4},{6,7},{7,6},{8,9},{9,8},{10,11... | collective-permute-start | bytes 7077896 | tf_op jit(solution)/shard_map/ppermute | solution.py:726
  347.9 24.3 %collective-permute-start.23 = (bf16[384,768]{1,0:T(8,128)(2,1)}, bf16[384,768]{1,0:T(8,128)(2,1)}, u32[]{:S(2)}, u32[]{:S(2)}) collective-permute-start(bf16[384,768]{1,0:T(8,128)(2,1)} %add_convert_fusion.28), channel_id=1, source_target_pairs={{2,4},{3,5},{4,2},{5,3},{10,12},{11,13},{12,10},{13,11},{18,20},{1... | collective-permute-start | bytes 1769480 | tf_op jit(solution)/shard_map/ppermute | solution.py:656
  367.8 25.7 %collective-permute-start.29 = (bf16[384,768]{1,0:T(8,128)(2,1)}, bf16[384,768]{1,0:T(8,128)(2,1)}, u32[]{:S(2)}, u32[]{:S(2)}) collective-permute-start(bf16[384,768]{1,0:T(8,128)(2,1)} %add_convert_fusion.26), channel_id=1, source_target_pairs={{2,4},{3,5},{4,2},{5,3},{10,12},{11,13},{12,10},{13,11},{18,20},{1... | collective-permute-start | bytes 1769480 | tf_op jit(solution)/shard_map/ppermute | solution.py:656
  375.8 28.1 %collective-permute-start.32 = (bf16[384,768]{1,0:T(8,128)(2,1)S(1)}, bf16[384,768]{1,0:T(8,128)(2,1)}, u32[]{:S(2)}, u32[]{:S(2)}) collective-permute-start(bf16[384,768]{1,0:T(8,128)(2,1)S(1)} %add_convert_fusion.24), channel_id=1, source_target_pairs={{2,4},{3,5},{4,2},{5,3},{10,12},{11,13},{12,10},{13,11},{18,20},{1... | collective-permute-start | bytes 1769480 | tf_op jit(solution)/shard_map/ppermute | solution.py:656
  399.0 25.6 %collective-permute-start.36 = (bf16[384,768]{1,0:T(8,128)(2,1)S(1)}, bf16[384,768]{1,0:T(8,128)(2,1)S(1)}, u32[]{:S(2)}, u32[]{:S(2)}) collective-permute-start(bf16[384,768]{1,0:T(8,128)(2,1)S(1)} %get-tuple-element.476), channel_id=1, source_target_pairs={{0,2},{1,3},{6,4},{7,5},{8,10},{9,11},{14,12},{15,13},{16,18},{17,... | collective-permute-start | bytes 1769480 | tf_op jit(solution)/shard_map/ppermute | solution.py:656
  403.7 43.6 %collective-permute-start.27 = (bf16[384,2304]{1,0:T(8,128)(2,1)S(1)}, bf16[384,2304]{1,0:T(8,128)(2,1)S(1)}, u32[]{:S(2)}, u32[]{:S(2)}) collective-permute-start(bf16[384,2304]{1,0:T(8,128)(2,1)S(1)} %copy-done.24), channel_id=1, source_target_pairs={{0,1},{1,0},{2,3},{3,2},{4,5},{5,4},{6,7},{7,6},{8,9},{9,8},{10,11... | collective-permute-start | bytes 5308424 | tf_op jit(solution)/shard_map/ppermute | solution.py:726
  455.6 23.1 %collective-permute-start.48 = (bf16[400,768]{1,0:T(8,128)(2,1)S(1)}, bf16[400,768]{1,0:T(8,128)(2,1)S(1)}, u32[]{:S(2)}, u32[]{:S(2)}) collective-permute-start(bf16[400,768]{1,0:T(8,128)(2,1)S(1)} %pad_maximum_fusion.6), channel_id=1, source_target_pairs={{0,1},{1,0},{2,3},{3,2},{4,5},{5,4},{6,7},{7,6},{8,9},{9,8},{10,11... | collective-permute-start | bytes 1843208 | tf_op jit(solution)/shard_map/ppermute | solution.py:726
  455.8 25.1 %collective-permute-start.46 = (bf16[384,768]{1,0:T(8,128)(2,1)S(1)}, bf16[384,768]{1,0:T(8,128)(2,1)S(1)}, u32[]{:S(2)}, u32[]{:S(2)}) collective-permute-start(bf16[384,768]{1,0:T(8,128)(2,1)S(1)} %add_convert_fusion.12), channel_id=1, source_target_pairs={{2,4},{3,5},{4,2},{5,3},{10,12},{11,13},{12,10},{13,11},{18,20},{1... | collective-permute-start | bytes 1769480 | tf_op jit(solution)/shard_map/ppermute | solution.py:656
  456.8 27.4 %collective-permute-start.45 = (bf16[384,768]{1,0:T(8,128)(2,1)S(1)}, bf16[384,768]{1,0:T(8,128)(2,1)S(1)}, u32[]{:S(2)}, u32[]{:S(2)}) collective-permute-start(bf16[384,768]{1,0:T(8,128)(2,1)S(1)} %get-tuple-element.531), channel_id=1, source_target_pairs={{0,2},{1,3},{6,4},{7,5},{2,0},{3,1},{4,6},{5,7},{8,10},{9,11},{14,... | collective-permute-start | bytes 1769480 | tf_op jit(solution)/shard_map/ppermute | solution.py:656
  478.9 26.9 %collective-permute-start.49 = (bf16[400,768]{1,0:T(8,128)(2,1)S(1)}, bf16[400,768]{1,0:T(8,128)(2,1)S(1)}, u32[]{:S(2)}, u32[]{:S(2)}) collective-permute-start(bf16[400,768]{1,0:T(8,128)(2,1)S(1)} %add_convert_fusion.6), channel_id=1, source_target_pairs={{0,2},{1,3},{6,4},{7,5},{8,10},{9,11},{14,12},{15,13},{16,18},{17,... | collective-permute-start | bytes 1843208 | tf_op jit(solution)/shard_map/ppermute | solution.py:656
  506.4 53.5 %collective-permute-start.52 = (bf16[384,3072]{1,0:T(8,128)(2,1)S(1)}, bf16[384,3072]{1,0:T(8,128)(2,1)S(1)}, u32[]{:S(2)}, u32[]{:S(2)}) collective-permute-start(bf16[384,3072]{1,0:T(8,128)(2,1)S(1)} %pad_maximum_fusion.1), channel_id=1, source_target_pairs={{0,1},{1,0},{2,3},{3,2},{4,5},{5,4},{6,7},{7,6},{8,9},{9,8},{10,11... | collective-permute-start | bytes 7077896 | tf_op jit(solution)/shard_map/ppermute | solution.py:656
  506.6 28.2 %collective-permute-start.44 = (bf16[384,768]{1,0:T(8,128)(2,1)S(1)}, bf16[384,768]{1,0:T(8,128)(2,1)S(1)}, u32[]{:S(2)}, u32[]{:S(2)}) collective-permute-start(bf16[384,768]{1,0:T(8,128)(2,1)S(1)} %add_convert_fusion.14), channel_id=1, source_target_pairs={{2,0},{3,1},{4,6},{5,7},{10,8},{11,9},{12,14},{13,15},{18,16},{19,... | collective-permute-start | bytes 1769480 | tf_op jit(solution)/shard_map/ppermute | solution.py:656
  508.1 51.8 %collective-permute-start.55 = (bf16[400,768]{1,0:T(8,128)(2,1)S(1)}, bf16[400,768]{1,0:T(8,128)(2,1)S(1)}, u32[]{:S(2)}, u32[]{:S(2)}) collective-permute-start(bf16[400,768]{1,0:T(8,128)(2,1)S(1)} %add_convert_fusion.5), channel_id=1, source_target_pairs={{2,4},{3,5},{4,2},{5,3},{10,12},{11,13},{12,10},{13,11},{18,20},{1... | collective-permute-start | bytes 1843208 | tf_op jit(solution)/shard_map/ppermute | solution.py:656
  508.9 38.5 %collective-permute-start.54 = (bf16[384,768]{1,0:T(8,128)(2,1)S(1)}, bf16[384,768]{1,0:T(8,128)(2,1)S(1)}, u32[]{:S(2)}, u32[]{:S(2)}) collective-permute-start(bf16[384,768]{1,0:T(8,128)(2,1)S(1)} %add_convert_fusion.7), channel_id=1, source_target_pairs={{2,0},{3,1},{4,6},{5,7},{10,8},{11,9},{12,14},{13,15},{18,16},{19,... | collective-permute-start | bytes 1769480 | tf_op jit(solution)/shard_map/ppermute | solution.py:656
  510.4 49.5 %collective-permute-start.53 = (bf16[384,768]{1,0:T(8,128)(2,1)S(1)}, bf16[384,768]{1,0:T(8,128)(2,1)S(1)}, u32[]{:S(2)}, u32[]{:S(2)}) collective-permute-start(bf16[384,768]{1,0:T(8,128)(2,1)S(1)} %add_convert_fusion.8), channel_id=1, source_target_pairs={{2,0},{3,1},{4,6},{5,7},{10,8},{11,9},{12,14},{13,15},{18,16},{19,... | collective-permute-start | bytes 1769480 | tf_op jit(solution)/shard_map/ppermute | solution.py:656
  (60 other events, 708.8 us)

commit v6 on v5

--- a/solution.py
+++ b/solution.py
@@ -299,17 +299,14 @@
         steps = HIDDEN // chunk
         get_dy = copies.start(dy_in, dy_v)
         get_wd, get_gp = [], []
-        for step in range(steps):
+
+        def get_chunk(step):
             part = pl.ds(step * chunk, chunk)
             get_wd.append(copies.start(wd_in.at[part], wd_v.at[part]))
             get_gp.append(copies.start(saved["gp"].at[slot, :, part], gp_v.at[:, part]))
-        get_wu = copies.start(wu_in, wu_v)
-        get_norm = [
-            copies.start(saved["n2"].at[slot], n2_v),
-            copies.start(saved["r2"].at[slot], r2_v),
-            copies.start(gain_one_in, gains_v.at[pl.ds(0, 1)]),
-            copies.start(gain_two_in, gains_v.at[pl.ds(8, 1)]),
-        ]
+
+        get_chunk(0)
+        get_chunk(1)
 
         def put(source, name):
             copies.start(source, state[name].at[slot])
@@ -319,6 +316,16 @@
         for step in range(steps):
             part = slice(step * chunk, (step + 1) * chunk)
             wait(get_wd[step], get_gp[step])
+            if step == 0:
+                for later in range(2, steps):
+                    get_chunk(later)
+                get_wu = copies.start(wu_in, wu_v)
+                get_norm = [
+                    copies.start(saved["n2"].at[slot], n2_v),
+                    copies.start(saved["r2"].at[slot], r2_v),
+                    copies.start(gain_one_in, gains_v.at[pl.ds(0, 1)]),
+                    copies.start(gain_two_in, gains_v.at[pl.ds(8, 1)]),
+                ]
             act = lax.dot_general(dy_v[...], wd_v[part, :], NT, preferred_element_type=f32)
             du_v[:, part] = act.astype(bf16) * gp_v[:, part]
         get_wp = copies.start(wp_in, wp_v)

time: 591 us -> 593 us (level)
  no operation moved by 1% of the time
where the time goes in v6:
time: 593 us; the launch traced here: 587 us
  waiting for transfers between devices  225 us (38%)
  Pallas kernels  158 us (27%)
  starting transfers between devices  135 us (23%)
  other arithmetic  52.3 us (9%)
  local copies, waits for them, and re-layouts  14.3 us (2%)
    ppermute x18, waiting for transfers between devices, send(): return lax.ppermute(value, 'section', [(source, target)])  117 us
    pallas_call x16, Pallas kernels, call_states(): pl.pallas_call(partial(kernel, first), out_shape=list(plain_out) + state_...  117 us
    ppermute x33, waiting for transfers between devices, start(): lax.ppermute(value, 'dp', pairs)  108 us
    ppermute x33, starting transfers between devices, start(): lax.ppermute(value, 'dp', pairs)  71.6 us
    ppermute x18, starting transfers between devices, send(): return lax.ppermute(value, 'section', [(source, target)])  56.4 us
    pallas_call x5, Pallas kernels, product_call(): pl.pallas_call(partial(product_kernel, offset, block), out_shape=[jax.Sha...  33 us
    convert_element_type x4, other arithmetic, join(): self.result = jnp.concatenate([low, high], axis=0).astype(f32)  13.1 us
    convert_element_type x22, other arithmetic, added(): return (one.astype(f32) + other.astype(f32)).astype(bf16)  13.1 us
  transfers between devices with their start and end apart: 59, of which 19 were waited for; matrix products, arithmetic and copies ran while one was open for 8% of the time, Pallas kernels for 24%

profile of v6, /device:TPU:0, one launch (start us, length us, event | category | flops | bytes accessed | tf_op | source)
XLA Modules:
  0.0 587.3 jit_solution(15020234700037778714)
XLA Ops:
  14.7 17.4 %layer_front.8 = (bf16[400,768]{1,0:T(8,128)(2,1)}, bf16[2,400,768]{2,1,0:T(8,128)(2,1)}, bf16[2,400,768]{2,1,0:T(8,128)(2,1)}, bf16[2,400,2304]{2,1,0:T(8,128)(...) custom-call(s32[1]{0:T(128)} %bitcast.1.scal, ...), custom_call_target="tpu_custom_call" | custom-call | tf_op jit(solution)/shard_map/layer_front/pallas_call | solution.py:241
  34.9 17.6 %layer_front.9 = (bf16[400,768]{1,0:T(8,128)(2,1)}, bf16[2,400,768]{2,1,0:T(8,128)(2,1)}, bf16[2,400,768]{2,1,0:T(8,128)(2,1)}, bf16[2,400,2304]{2,1,0:T(8,128)(...) custom-call(s32[1]{0:T(128)} %bitcast.1.scal, ...), custom_call_target="tpu_custom_call", output_to_operand_aliasing={{1}: (19, {}), {2}: (20, {}), {3}: (21, {}), {4}: (22, {}),... | custom-call | tf_op jit(solution)/shard_map/layer_front/pallas_call | solution.py:241
  60.2 8.2 %collective-permute-done.3.refs_0_ = bf16[400,768]{1,0:T(8,128)(2,1)S(1)} collective-permute-done((bf16[400,768]{1,0:T(8,128)(2,1)}, bf16[400,768]{1,0:T(8,128)(2,1)S(1)}, u32[]{:S(2)}, u32[]{:S(2)}) %collective-permute-start.3) | collective-permute-done | bytes 614432 | tf_op jit(solution)/shard_map/ppermute | solution.py:620
  91.7 8.5 %layer_back.8 = (bf16[400,768]{1,0:T(8,128)(2,1)}, bf16[2,400,3072]{2,1,0:T(8,128)(2,1)}, bf16[2,400,768]{2,1,0:T(8,128)(2,1)}, bf16[2,400,2304]{2,1,0:T(8,128)(2,1)}, f32[2,8,768]{2,1,0:T(8,128)}) custom-call(s32[1]{0:T(128)} %bitcast.1.scal, s32[2]{0:T(128)} %constant.106.clone.layer, bf16[400,768]{1,0:T(8,128)(2,1)} %get-tuple-element.576.refs_0_, ...), custom_call_target="tpu_custom_call" | custom-call | tf_op jit(solution)/shard_map/layer_back/pallas_call | solution.py:241
  100.3 7.0 %collective-permute-start.12 = (bf16[400,768]{1,0:T(8,128)(2,1)}, bf16[400,768]{1,0:T(8,128)(2,1)S(1)}, u32[]{:S(2)}, u32[]{:S(2)}) collective-permute-start(bf16[400,768]{1,0:T(8,128)(2,1)} %get-tuple-element.358.refs_16_), channel_id=1, source_target_pairs={{24,16},{25,17},{26,18},{27,19},{28,20},{29,21},{30,22},{31,23}} | collective-permute-start | bytes 1843208 | tf_op jit(solution)/shard_map/ppermute | solution.py:620
  116.1 8.6 %collective-permute-start.14 = (bf16[400,768]{1,0:T(8,128)(2,1)}, bf16[400,768]{1,0:T(8,128)(2,1)S(1)}, u32[]{:S(2)}, u32[]{:S(2)}) collective-permute-start(bf16[400,768]{1,0:T(8,128)(2,1)} %get-tuple-element.380), channel_id=1, source_target_pairs={{24,16},{25,17},{26,18},{27,19},{28,20},{29,21},{30,22},{31,23}} | collective-permute-start | bytes 1843208 | tf_op jit(solution)/shard_map/ppermute | solution.py:620
  135.1 7.0 %collective-permute-start.16 = (bf16[400,768]{1,0:T(8,128)(2,1)}, bf16[400,768]{1,0:T(8,128)(2,1)S(1)}, u32[]{:S(2)}, u32[]{:S(2)}) collective-permute-start(bf16[400,768]{1,0:T(8,128)(2,1)} %get-tuple-element.390), channel_id=1, source_target_pairs={{16,8},{17,9},{18,10},{19,11},{20,12},{21,13},{22,14},{23,15}} | collective-permute-start | bytes 1843208 | tf_op jit(solution)/shard_map/ppermute | solution.py:620
  143.9 7.3 %collective-permute-start.15 = (bf16[400,768]{1,0:T(8,128)(2,1)}, bf16[400,768]{1,0:T(8,128)(2,1)}, u32[]{:S(2)}, u32[]{:S(2)}) collective-permute-start(bf16[400,768]{1,0:T(8,128)(2,1)} %get-tuple-element.389), channel_id=1, source_target_pairs={{8,0},{9,1},{10,2},{11,3},{12,4},{13,5},{14,6},{15,7}} | collective-permute-start | bytes 1843208 | tf_op jit(solution)/shard_map/ppermute | solution.py:620
  153.1 7.0 %collective-permute-start.17 = (bf16[400,768]{1,0:T(8,128)(2,1)}, bf16[400,768]{1,0:T(8,128)(2,1)S(1)}, u32[]{:S(2)}, u32[]{:S(2)}) collective-permute-start(bf16[400,768]{1,0:T(8,128)(2,1)} %get-tuple-element.400), channel_id=1, source_target_pairs={{8,0},{9,1},{10,2},{11,3},{12,4},{13,5},{14,6},{15,7}} | collective-permute-start | bytes 1843208 | tf_op jit(solution)/shard_map/ppermute | solution.py:620
  160.3 84.8 %collective-permute-done.15.refs_0_ = bf16[400,768]{1,0:T(8,128)(2,1)} collective-permute-done((bf16[400,768]{1,0:T(8,128)(2,1)}, bf16[400,768]{1,0:T(8,128)(2,1)}, u32[]{:S(2)}, u32[]{:S(2)}) %collective-permute-start.15) | collective-permute-done | bytes 614432 | tf_op jit(solution)/shard_map/ppermute | solution.py:620
  245.1 23.1 %layer_back.14 = (bf16[400,768]{1,0:T(8,128)(2,1)}, bf16[2,400,3072]{2,1,0:T(8,128)(2,1)}, bf16[2,400,768]{2,1,0:T(8,128)(2,1)}, bf16[2,400,2304]{2,1,0:T(8,128)(2,1)}, f32[2,8,768]{2,1,0:T(8,128)}) custom-call(s32[1]{0:T(128)} %bitcast.1.scal, s32[2]{0:T(128)} %call_exported.0.layer, ...), custom_call_target="tpu_custom_call", output_to_operand_aliasing={{1}: (20, {}), {2}: (21, {}), {3}: (22, {}), {4}: (23, {})} | custom-call | tf_op jit(solution)/shard_map/layer_back/pallas_call | solution.py:241
  268.2 20.2 %collective-permute-done.17.refs_0_ = bf16[400,768]{1,0:T(8,128)(2,1)S(1)} collective-permute-done((bf16[400,768]{1,0:T(8,128)(2,1)}, bf16[400,768]{1,0:T(8,128)(2,1)S(1)}, u32[]{:S(2)}, u32[]{:S(2)}) %collective-permute-start.17) | collective-permute-done | bytes 614432 | tf_op jit(solution)/shard_map/ppermute | solution.py:620
  308.4 23.5 %layer_back.15 = (bf16[400,768]{1,0:T(8,128)(2,1)}, bf16[2,400,3072]{2,1,0:T(8,128)(2,1)}, bf16[2,400,768]{2,1,0:T(8,128)(2,1)}, bf16[2,400,2304]{2,1,0:T(8,128)(2,1)}, f32[2,8,768]{2,1,0:T(8,128)}) custom-call(s32[1]{0:T(128)} %bitcast.1.scal, s32[2]{0:T(128)} %call_exported.1.layer, ...), custom_call_target="tpu_custom_call", output_to_operand_aliasing={{1}: (20, {}), {2}: (21, {}), {3}: (22, {}), {4}: (23, {})} | custom-call | tf_op jit(solution)/shard_map/layer_back/pallas_call | solution.py:241
  333.6 9.6 %weight_grad.7 = (bf16[384,3072]{1,0:T(8,128)(2,1)}, bf16[384,3072]{1,0:T(8,128)(2,1)}, f32[8,3072]{1,0:T(8,128)}) custom-call(s32[1]{0:T(128)} %bitcast.core_ref, bf16[800,768]{1,0:T(8,128)(2,1)} %bitcast.97, bf16[800,3072]{1,0:T(8,128)(2,1)} %bitcast.76), custom_call_target="tpu_custom_call" | custom-call | tf_op jit(solution)/shard_map/weight_grad/pallas_call | solution.py:562
  379.0 7.9 %weight_grad.8 = (bf16[384,2304]{1,0:T(8,128)(2,1)}, bf16[384,2304]{1,0:T(8,128)(2,1)}, f32[8,2304]{1,0:T(8,128)}) custom-call(s32[1]{0:T(128)} %bitcast.core_ref, bf16[800,768]{1,0:T(8,128)(2,1)} %bitcast.96, bf16[800,2304]{1,0:T(8,128)(2,1)} %bitcast.94), custom_call_target="tpu_custom_call" | custom-call | tf_op jit(solution)/shard_map/weight_grad/pallas_call | solution.py:562
  405.4 8.1 %collective-permute-done.31 = bf16[384,768]{1,0:T(8,128)(2,1)S(1)} collective-permute-done((bf16[384,768]{1,0:T(8,128)(2,1)S(1)}, bf16[384,768]{1,0:T(8,128)(2,1)S(1)}, u32[]{:S(2)}, u32[]{:S(2)}) %collective-permute-start.31) | collective-permute-done | bytes 589856 | tf_op jit(solution)/shard_map/ppermute | solution.py:663
  438.8 9.7 %collective-permute-done.38 = bf16[384,768]{1,0:T(8,128)(2,1)S(1)} collective-permute-done((bf16[384,768]{1,0:T(8,128)(2,1)S(1)}, bf16[384,768]{1,0:T(8,128)(2,1)S(1)}, u32[]{:S(2)}, u32[]{:S(2)}) %collective-permute-start.38) | collective-permute-done | bytes 589856 | tf_op jit(solution)/shard_map/ppermute | solution.py:663
  458.4 13.2 %collective-permute-start.45 = (bf16[384,768]{1,0:T(8,128)(2,1)S(1)}, bf16[384,768]{1,0:T(8,128)(2,1)S(1)}, u32[]{:S(2)}, u32[]{:S(2)}) collective-permute-start(bf16[384,768]{1,0:T(8,128)(2,1)S(1)} %get-tuple-element.531), channel_id=1, source_target_pairs={{0,2},{1,3},{6,4},{7,5},{2,0},{3,1},{4,6},{5,7},{8,10},{9,11},{14,... | collective-permute-start | bytes 1769480 | tf_op jit(solution)/shard_map/ppermute | solution.py:663
  488.1 10.3 %collective-permute-done.42 = bf16[384,768]{1,0:T(8,128)(2,1)S(1)} collective-permute-done((bf16[384,768]{1,0:T(8,128)(2,1)S(1)}, bf16[384,768]{1,0:T(8,128)(2,1)S(1)}, u32[]{:S(2)}, u32[]{:S(2)}) %collective-permute-start.42) | collective-permute-done | bytes 589856 | tf_op jit(solution)/shard_map/ppermute | solution.py:663
  499.7 7.7 %collective-permute-done.49 = bf16[400,768]{1,0:T(8,128)(2,1)S(1)} collective-permute-done((bf16[400,768]{1,0:T(8,128)(2,1)S(1)}, bf16[400,768]{1,0:T(8,128)(2,1)S(1)}, u32[]{:S(2)}, u32[]{:S(2)}) %collective-permute-start.49) | collective-permute-done | bytes 614432 | tf_op jit(solution)/shard_map/ppermute | solution.py:663
  513.3 23.1 %collective-permute-done.44 = bf16[384,768]{1,0:T(8,128)(2,1)S(1)} collective-permute-done((bf16[384,768]{1,0:T(8,128)(2,1)S(1)}, bf16[384,768]{1,0:T(8,128)(2,1)S(1)}, u32[]{:S(2)}, u32[]{:S(2)}) %collective-permute-start.44) | collective-permute-done | bytes 589856 | tf_op jit(solution)/shard_map/ppermute | solution.py:663
  536.4 12.6 %collective-permute-done.54 = bf16[384,768]{1,0:T(8,128)(2,1)S(1)} collective-permute-done((bf16[384,768]{1,0:T(8,128)(2,1)S(1)}, bf16[384,768]{1,0:T(8,128)(2,1)S(1)}, u32[]{:S(2)}, u32[]{:S(2)}) %collective-permute-start.54) | collective-permute-done | bytes 589856 | tf_op jit(solution)/shard_map/ppermute | solution.py:663
  549.0 12.4 %collective-permute-done.53 = bf16[384,768]{1,0:T(8,128)(2,1)S(1)} collective-permute-done((bf16[384,768]{1,0:T(8,128)(2,1)S(1)}, bf16[384,768]{1,0:T(8,128)(2,1)S(1)}, u32[]{:S(2)}, u32[]{:S(2)}) %collective-permute-start.53) | collective-permute-done | bytes 589856 | tf_op jit(solution)/shard_map/ppermute | solution.py:663
  572.5 7.8 %collective-permute-done.56 = bf16[400,768]{1,0:T(8,128)(2,1)S(1)} collective-permute-done((bf16[400,768]{1,0:T(8,128)(2,1)S(1)}, bf16[400,768]{1,0:T(8,128)(2,1)S(1)}, u32[]{:S(2)}, u32[]{:S(2)}) %collective-permute-start.56) | collective-permute-done | bytes 614432 | tf_op jit(solution)/shard_map/ppermute | solution.py:663
  (256 shorter events, 222.5 us)
Async XLA Ops:
  1.9 31.5 %collective-permute-start = (bf16[200,768]{1,0:T(8,128)(2,1)}, bf16[200,768]{1,0:T(8,128)(2,1)S(1)}, u32[]{:S(2)}, u32[]{:S(2)}) collective-permute-start(bf16[200,768]{1,0:T(8,128)(2,1)} %refs_16_.13), channel_id=1, source_target_pairs={{16,0},{17,1},{18,2},{19,3},{20,4},{21,5},{22,6},{23,7}} | collective-permute-start | bytes 921608 | tf_op jit(solution)/shard_map/ppermute | solution.py:620
  3.2 30.2 %collective-permute-start.1 = (bf16[200,768]{1,0:T(8,128)(2,1)}, bf16[200,768]{1,0:T(8,128)(2,1)S(1)}, u32[]{:S(2)}, u32[]{:S(2)}) collective-permute-start(bf16[200,768]{1,0:T(8,128)(2,1)} %refs_16_.13), channel_id=1, source_target_pairs={{24,0},{25,1},{26,2},{27,3},{28,4},{29,5},{30,6},{31,7}} | collective-permute-start | bytes 921608 | tf_op jit(solution)/shard_map/ppermute | solution.py:620
  32.1 25.1 %collective-permute-start.4 = (bf16[400,768]{1,0:T(8,128)(2,1)}, bf16[400,768]{1,0:T(8,128)(2,1)S(1)}, u32[]{:S(2)}, u32[]{:S(2)}) collective-permute-start(bf16[400,768]{1,0:T(8,128)(2,1)} %get-tuple-element.288), channel_id=1, source_target_pairs={{0,8},{1,9},{2,10},{3,11},{4,12},{5,13},{6,14},{7,15}} | collective-permute-start | bytes 1843208 | tf_op jit(solution)/shard_map/ppermute | solution.py:620
  100.3 24.4 %collective-permute-start.12 = (bf16[400,768]{1,0:T(8,128)(2,1)}, bf16[400,768]{1,0:T(8,128)(2,1)S(1)}, u32[]{:S(2)}, u32[]{:S(2)}) collective-permute-start(bf16[400,768]{1,0:T(8,128)(2,1)} %get-tuple-element.358.refs_16_), channel_id=1, source_target_pairs={{24,16},{25,17},{26,18},{27,19},{28,20},{29,21},{30,22},{31,23}} | collective-permute-start | bytes 1843208 | tf_op jit(solution)/shard_map/ppermute | solution.py:620
  143.9 101.2 %collective-permute-start.15 = (bf16[400,768]{1,0:T(8,128)(2,1)}, bf16[400,768]{1,0:T(8,128)(2,1)}, u32[]{:S(2)}, u32[]{:S(2)}) collective-permute-start(bf16[400,768]{1,0:T(8,128)(2,1)} %get-tuple-element.389), channel_id=1, source_target_pairs={{8,0},{9,1},{10,2},{11,3},{12,4},{13,5},{14,6},{15,7}} | collective-permute-start | bytes 1843208 | tf_op jit(solution)/shard_map/ppermute | solution.py:620
  153.1 135.3 %collective-permute-start.17 = (bf16[400,768]{1,0:T(8,128)(2,1)}, bf16[400,768]{1,0:T(8,128)(2,1)S(1)}, u32[]{:S(2)}, u32[]{:S(2)}) collective-permute-start(bf16[400,768]{1,0:T(8,128)(2,1)} %get-tuple-element.400), channel_id=1, source_target_pairs={{8,0},{9,1},{10,2},{11,3},{12,4},{13,5},{14,6},{15,7}} | collective-permute-start | bytes 1843208 | tf_op jit(solution)/shard_map/ppermute | solution.py:620
  302.3 29.6 %collective-permute-start.21 = (bf16[768,768]{1,0:T(8,128)(2,1)}, bf16[768,768]{1,0:T(8,128)(2,1)}, u32[]{:S(2)}, u32[]{:S(2)}) collective-permute-start(bf16[768,768]{1,0:T(8,128)(2,1)} %get-tuple-element.409), channel_id=1, source_target_pairs={{0,1},{1,0},{2,3},{3,2},{4,5},{5,4},{6,7},{7,6},{8,9},{9,8},{10,11... | collective-permute-start | bytes 3538952 | tf_op jit(solution)/shard_map/ppermute | solution.py:733
  303.2 30.4 %collective-permute-start.19 = (bf16[384,768]{1,0:T(8,128)(2,1)S(1)}, bf16[384,768]{1,0:T(8,128)(2,1)}, u32[]{:S(2)}, u32[]{:S(2)}) collective-permute-start(bf16[384,768]{1,0:T(8,128)(2,1)S(1)} %get-tuple-element.423), channel_id=1, source_target_pairs={{0,2},{1,3},{6,4},{7,5},{8,10},{9,11},{14,12},{15,13},{16,18},{17,... | collective-permute-start | bytes 1769480 | tf_op jit(solution)/shard_map/ppermute | solution.py:663
  307.0 26.5 %collective-permute-start.20 = (bf16[384,768]{1,0:T(8,128)(2,1)S(1)}, bf16[384,768]{1,0:T(8,128)(2,1)S(1)}, u32[]{:S(2)}, u32[]{:S(2)}) collective-permute-start(bf16[384,768]{1,0:T(8,128)(2,1)S(1)} %get-tuple-element.442), channel_id=1, source_target_pairs={{0,2},{1,3},{6,4},{7,5},{8,10},{9,11},{14,12},{15,13},{16,18},{17,... | collective-permute-start | bytes 1769480 | tf_op jit(solution)/shard_map/ppermute | solution.py:663
  343.2 48.5 %collective-permute-start.30 = (bf16[384,3072]{1,0:T(8,128)(2,1)}, bf16[384,3072]{1,0:T(8,128)(2,1)}, u32[]{:S(2)}, u32[]{:S(2)}) collective-permute-start(bf16[384,3072]{1,0:T(8,128)(2,1)} %get-tuple-element.445), channel_id=1, source_target_pairs={{0,1},{1,0},{2,3},{3,2},{4,5},{5,4},{6,7},{7,6},{8,9},{9,8},{10,11... | collective-permute-start | bytes 7077896 | tf_op jit(solution)/shard_map/ppermute | solution.py:733
  349.8 24.0 %collective-permute-start.23 = (bf16[384,768]{1,0:T(8,128)(2,1)}, bf16[384,768]{1,0:T(8,128)(2,1)}, u32[]{:S(2)}, u32[]{:S(2)}) collective-permute-start(bf16[384,768]{1,0:T(8,128)(2,1)} %add_convert_fusion.28), channel_id=1, source_target_pairs={{2,4},{3,5},{4,2},{5,3},{10,12},{11,13},{12,10},{13,11},{18,20},{1... | collective-permute-start | bytes 1769480 | tf_op jit(solution)/shard_map/ppermute | solution.py:663
  369.4 25.7 %collective-permute-start.29 = (bf16[384,768]{1,0:T(8,128)(2,1)}, bf16[384,768]{1,0:T(8,128)(2,1)}, u32[]{:S(2)}, u32[]{:S(2)}) collective-permute-start(bf16[384,768]{1,0:T(8,128)(2,1)} %add_convert_fusion.26), channel_id=1, source_target_pairs={{2,4},{3,5},{4,2},{5,3},{10,12},{11,13},{12,10},{13,11},{18,20},{1... | collective-permute-start | bytes 1769480 | tf_op jit(solution)/shard_map/ppermute | solution.py:663
  377.4 28.1 %collective-permute-start.32 = (bf16[384,768]{1,0:T(8,128)(2,1)S(1)}, bf16[384,768]{1,0:T(8,128)(2,1)}, u32[]{:S(2)}, u32[]{:S(2)}) collective-permute-start(bf16[384,768]{1,0:T(8,128)(2,1)S(1)} %add_convert_fusion.24), channel_id=1, source_target_pairs={{2,4},{3,5},{4,2},{5,3},{10,12},{11,13},{12,10},{13,11},{18,20},{1... | collective-permute-start | bytes 1769480 | tf_op jit(solution)/shard_map/ppermute | solution.py:663
  400.6 25.6 %collective-permute-start.36 = (bf16[384,768]{1,0:T(8,128)(2,1)S(1)}, bf16[384,768]{1,0:T(8,128)(2,1)S(1)}, u32[]{:S(2)}, u32[]{:S(2)}) collective-permute-start(bf16[384,768]{1,0:T(8,128)(2,1)S(1)} %get-tuple-element.476), channel_id=1, source_target_pairs={{0,2},{1,3},{6,4},{7,5},{8,10},{9,11},{14,12},{15,13},{16,18},{17,... | collective-permute-start | bytes 1769480 | tf_op jit(solution)/shard_map/ppermute | solution.py:663
  405.3 43.6 %collective-permute-start.27 = (bf16[384,2304]{1,0:T(8,128)(2,1)S(1)}, bf16[384,2304]{1,0:T(8,128)(2,1)S(1)}, u32[]{:S(2)}, u32[]{:S(2)}) collective-permute-start(bf16[384,2304]{1,0:T(8,128)(2,1)S(1)} %copy-done.24), channel_id=1, source_target_pairs={{0,1},{1,0},{2,3},{3,2},{4,5},{5,4},{6,7},{7,6},{8,9},{9,8},{10,11... | collective-permute-start | bytes 5308424 | tf_op jit(solution)/shard_map/ppermute | solution.py:733
  457.2 23.1 %collective-permute-start.48 = (bf16[400,768]{1,0:T(8,128)(2,1)S(1)}, bf16[400,768]{1,0:T(8,128)(2,1)S(1)}, u32[]{:S(2)}, u32[]{:S(2)}) collective-permute-start(bf16[400,768]{1,0:T(8,128)(2,1)S(1)} %pad_maximum_fusion.6), channel_id=1, source_target_pairs={{0,1},{1,0},{2,3},{3,2},{4,5},{5,4},{6,7},{7,6},{8,9},{9,8},{10,11... | collective-permute-start | bytes 1843208 | tf_op jit(solution)/shard_map/ppermute | solution.py:733
  457.4 25.1 %collective-permute-start.46 = (bf16[384,768]{1,0:T(8,128)(2,1)S(1)}, bf16[384,768]{1,0:T(8,128)(2,1)S(1)}, u32[]{:S(2)}, u32[]{:S(2)}) collective-permute-start(bf16[384,768]{1,0:T(8,128)(2,1)S(1)} %add_convert_fusion.12), channel_id=1, source_target_pairs={{2,4},{3,5},{4,2},{5,3},{10,12},{11,13},{12,10},{13,11},{18,20},{1... | collective-permute-start | bytes 1769480 | tf_op jit(solution)/shard_map/ppermute | solution.py:663
  458.4 27.4 %collective-permute-start.45 = (bf16[384,768]{1,0:T(8,128)(2,1)S(1)}, bf16[384,768]{1,0:T(8,128)(2,1)S(1)}, u32[]{:S(2)}, u32[]{:S(2)}) collective-permute-start(bf16[384,768]{1,0:T(8,128)(2,1)S(1)} %get-tuple-element.531), channel_id=1, source_target_pairs={{0,2},{1,3},{6,4},{7,5},{2,0},{3,1},{4,6},{5,7},{8,10},{9,11},{14,... | collective-permute-start | bytes 1769480 | tf_op jit(solution)/shard_map/ppermute | solution.py:663
  480.5 26.9 %collective-permute-start.49 = (bf16[400,768]{1,0:T(8,128)(2,1)S(1)}, bf16[400,768]{1,0:T(8,128)(2,1)S(1)}, u32[]{:S(2)}, u32[]{:S(2)}) collective-permute-start(bf16[400,768]{1,0:T(8,128)(2,1)S(1)} %add_convert_fusion.6), channel_id=1, source_target_pairs={{0,2},{1,3},{6,4},{7,5},{8,10},{9,11},{14,12},{15,13},{16,18},{17,... | collective-permute-start | bytes 1843208 | tf_op jit(solution)/shard_map/ppermute | solution.py:663
  508.0 53.5 %collective-permute-start.52 = (bf16[384,3072]{1,0:T(8,128)(2,1)S(1)}, bf16[384,3072]{1,0:T(8,128)(2,1)S(1)}, u32[]{:S(2)}, u32[]{:S(2)}) collective-permute-start(bf16[384,3072]{1,0:T(8,128)(2,1)S(1)} %pad_maximum_fusion.1), channel_id=1, source_target_pairs={{0,1},{1,0},{2,3},{3,2},{4,5},{5,4},{6,7},{7,6},{8,9},{9,8},{10,11... | collective-permute-start | bytes 7077896 | tf_op jit(solution)/shard_map/ppermute | solution.py:663
  508.2 28.2 %collective-permute-start.44 = (bf16[384,768]{1,0:T(8,128)(2,1)S(1)}, bf16[384,768]{1,0:T(8,128)(2,1)S(1)}, u32[]{:S(2)}, u32[]{:S(2)}) collective-permute-start(bf16[384,768]{1,0:T(8,128)(2,1)S(1)} %add_convert_fusion.14), channel_id=1, source_target_pairs={{2,0},{3,1},{4,6},{5,7},{10,8},{11,9},{12,14},{13,15},{18,16},{19,... | collective-permute-start | bytes 1769480 | tf_op jit(solution)/shard_map/ppermute | solution.py:663
  509.7 51.8 %collective-permute-start.55 = (bf16[400,768]{1,0:T(8,128)(2,1)S(1)}, bf16[400,768]{1,0:T(8,128)(2,1)S(1)}, u32[]{:S(2)}, u32[]{:S(2)}) collective-permute-start(bf16[400,768]{1,0:T(8,128)(2,1)S(1)} %add_convert_fusion.5), channel_id=1, source_target_pairs={{2,4},{3,5},{4,2},{5,3},{10,12},{11,13},{12,10},{13,11},{18,20},{1... | collective-permute-start | bytes 1843208 | tf_op jit(solution)/shard_map/ppermute | solution.py:663
  510.6 38.5 %collective-permute-start.54 = (bf16[384,768]{1,0:T(8,128)(2,1)S(1)}, bf16[384,768]{1,0:T(8,128)(2,1)S(1)}, u32[]{:S(2)}, u32[]{:S(2)}) collective-permute-start(bf16[384,768]{1,0:T(8,128)(2,1)S(1)} %add_convert_fusion.7), channel_id=1, source_target_pairs={{2,0},{3,1},{4,6},{5,7},{10,8},{11,9},{12,14},{13,15},{18,16},{19,... | collective-permute-start | bytes 1769480 | tf_op jit(solution)/shard_map/ppermute | solution.py:663
  512.0 49.5 %collective-permute-start.53 = (bf16[384,768]{1,0:T(8,128)(2,1)S(1)}, bf16[384,768]{1,0:T(8,128)(2,1)S(1)}, u32[]{:S(2)}, u32[]{:S(2)}) collective-permute-start(bf16[384,768]{1,0:T(8,128)(2,1)S(1)} %add_convert_fusion.8), channel_id=1, source_target_pairs={{2,0},{3,1},{4,6},{5,7},{10,8},{11,9},{12,14},{13,15},{18,16},{19,... | collective-permute-start | bytes 1769480 | tf_op jit(solution)/shard_map/ppermute | solution.py:663
  (60 other events, 708.8 us)
